TPU v7x, 32 devices: a whole 2x2x4 slice. The times are simulated.
32 devices in a mesh: blk: 8 (over y, x, core), grp: 4 (over z).
Axes of the slice: x: 2, y: 2, z: 4, core: 2. Of those that a mesh axis runs over, the one named last changes fastest.
Arguments:
- tensor_blocks: bfloat16 [1152, 64, 4096], P(('blk', 'grp')), may hold values from 0 to 1
- block_coords: int32 [3, 1152], P(None, ('blk', 'grp')), may hold values from 0 to 63, as said below
- block_count: int32 [32], P(('blk', 'grp')), may hold values from 1 to 36, as said below
- row_owner: int32 [3, 64], replicated, may hold values from 0 to 63, as said below
- factors: float32 [3, 4096, 256], P(None, ('blk', 'grp')), may hold values from -2.4 to 2.4
- moment1: float32 [4096, 256], P(('blk', 'grp')), may hold values from -1.8 to 1.8
- moment2: float32 [4096, 256], P(('blk', 'grp')), may hold values from 0.01 to 1
Outputs:
- new_factor: float32 [4096, 256], P(('blk', 'grp'))
- new_moment1: float32 [4096, 256], P(('blk', 'grp'))
- new_moment2: float32 [4096, 256], P(('blk', 'grp'))
Inputs may be any that keep to these rules, and one draw needn't show every extreme that they name: `row_owner`: for each mode a permutation; storage position p lies on device p // 2 of blk+grp. `block_coords`: of the 108 row blocks named by one device's slots, at most 5 have positions on any one device, and exactly 5 on some device; of the 36 first-mode row blocks named by one device's slots, at most 2 have positions on any one device, and exactly 2 on some device. `block_count`: some device has all slots live.
All inputs are finite; a program needn't handle non-finite values.
Results may differ from a plain program's by a relative error of at most 0.0012.
Values may be sent and summed in bfloat16 or wider, within the bound.
No kernel may reach another device: no remote copies, remote signals or barrier semaphores. Data moves between devices by JAX's collectives and lax.ppermute only.
A program may use at most 128 MiB of HBM per device.

v0:
```python
import jax
import jax.numpy as jnp
from jax import lax
from jax.sharding import PartitionSpec as P


def route_requests(values):
    return lax.all_to_all(values, ("blk", "grp"), split_axis=0, concat_axis=0, tiled=True)


def route_rows(values):
    return lax.all_to_all(values, ("blk", "grp"), split_axis=0, concat_axis=0, tiled=True)


def route_partials(values):
    return lax.all_to_all(values, ("blk", "grp"), split_axis=0, concat_axis=0, tiled=True)


def group_width(slot_count):
    best = 1
    for width in range(1, 9):
        if slot_count % width == 0:
            best = width
    return best


def per_device(tensor_blocks, block_coords, block_count, row_owner, factors, moment1, moment2):
    slot_count = tensor_blocks.shape[0]
    edge = tensor_blocks.shape[1]
    rank = factors.shape[2]
    devices = lax.axis_size(("blk", "grp"))
    local_blocks = moment1.shape[0] // edge
    capacity = (3 * slot_count + devices - 1) // devices + 1
    first_cap = (slot_count + devices - 1) // devices
    buffer_len = devices * capacity
    first_len = devices * first_cap
    wanted = 3 * slot_count
    positions = jnp.concatenate([jnp.take(row_owner[m], block_coords[m]) for m in range(3)])
    owners = positions // local_blocks
    local_index = positions % local_blocks + jnp.repeat(
        jnp.arange(3, dtype=jnp.int32) * local_blocks, slot_count
    )
    order = jnp.arange(wanted, dtype=jnp.int32)
    earlier = order[None, :] < order[:, None]
    standing = jnp.sum(((owners[None, :] == owners[:, None]) & earlier).astype(jnp.int32), axis=1)
    buffer_index = owners * capacity + standing
    requests = jnp.full((buffer_len,), -1, jnp.int32).at[buffer_index].set(local_index)
    incoming = route_requests(requests)
    table = factors.reshape(3 * local_blocks, edge, rank).astype(jnp.bfloat16)
    present = incoming >= 0
    reply = jnp.where(
        present[:, None, None],
        jnp.take(table, jnp.maximum(incoming, 0), axis=0),
        jnp.zeros((), jnp.bfloat16),
    )
    fetched = route_rows(reply)
    gathered = jnp.take(fetched, buffer_index, axis=0).reshape(3, slot_count, edge, rank)
    alive = (jnp.arange(slot_count, dtype=jnp.int32) < block_count[0]).astype(jnp.float32)
    width = group_width(slot_count)
    groups = slot_count // width
    grouped_blocks = tensor_blocks.reshape(groups, width, edge, edge * edge)
    grouped_rows = gathered.reshape(3, groups, width, edge, rank)
    grouped_alive = alive.reshape(groups, width)

    def group_step(carry, item):
        block, rows_a, rows_b, rows_c, weight = item
        pair = (
            (rows_b.astype(jnp.float32)[:, :, None, :] * rows_c.astype(jnp.float32)[:, None, :, :])
            .reshape(width, edge * edge, rank)
            .astype(jnp.bfloat16)
        )
        model = lax.dot_general(
            rows_a, pair, (((2,), (2,)), ((0,), (0,))), preferred_element_type=jnp.float32
        )
        resid = (
            (jax.nn.sigmoid(model) - block.astype(jnp.float32)) * weight[:, None, None]
        ).astype(jnp.bfloat16)
        return (
            carry,
            lax.dot_general(
                resid, pair, (((2,), (1,)), ((0,), (0,))), preferred_element_type=jnp.float32
            ),
        )

    _, parts = lax.scan(
        group_step,
        0.0,
        (grouped_blocks, grouped_rows[0], grouped_rows[1], grouped_rows[2], grouped_alive),
    )
    parts = parts.reshape(slot_count, edge, rank)
    first_index = owners[:slot_count] * first_cap + standing[:slot_count]
    outgoing = jnp.zeros((first_len, edge, rank), jnp.float32).at[first_index].set(parts)
    arrived = route_partials(outgoing)
    first_requests = incoming.reshape(devices, capacity)[:, :first_cap].reshape(first_len)
    targets = jnp.arange(local_blocks, dtype=jnp.int32)
    select = (first_requests[None, :] == targets[:, None]).astype(jnp.float32)
    grad = jnp.dot(select, arrived.reshape(first_len, edge * rank), precision=lax.Precision.HIGHEST)
    grad = grad.reshape(local_blocks * edge, rank)
    new_moment1 = 0.9 * moment1 + 0.1 * grad
    new_moment2 = 0.999 * moment2 + 0.001 * grad * grad
    new_factor = factors[0] - 0.02 * (new_moment1 / (1.0 - 0.9**8)) / (
        jnp.sqrt(new_moment2 / (1.0 - 0.999**8)) + 1e-08
    )
    return (new_factor, new_moment1, new_moment2)


def solution(mesh):
    return jax.shard_map(
        per_device,
        mesh=mesh,
        in_specs=(
            P(("blk", "grp"), None, None),
            P(None, ("blk", "grp")),
            P(("blk", "grp")),
            P(),
            P(None, ("blk", "grp"), None),
            P(("blk", "grp"), None),
            P(("blk", "grp"), None),
        ),
        out_specs=(P(("blk", "grp"), None), P(("blk", "grp"), None), P(("blk", "grp"), None)),
        check_vma=False,
    )
```

profile of v0, /device:TPU:0, one launch (start us, length us, event | category | flops | bytes accessed | tf_op | source)
XLA Modules:
  0.0 421.2 jit_solution(3021406071319475185)
XLA Ops:
  7.5 7.3 %all-to-all-start = ((s32[32,5,1]{1,2,0:T(1,128)}), s32[32,5,1]{1,2,0:T(1,128)S(1)}, u32[]{:S(2)}, u32[]{:S(2)}) async-start(s32[32,5,1]{1,2,0:T(1,128)} %bitcast.19), calls=%async_computation | async-start | bytes 32768 | tf_op jit(solution)/shard_map/all_to_all | solution.py:8
  15.9 6.1 %all-to-all-done = s32[32,5,1]{1,2,0:T(1,128)S(1)} async-done(((s32[32,5,1]{1,2,0:T(1,128)}), s32[32,5,1]{1,2,0:T(1,128)S(1)}, u32[]{:S(2)}, u32[]{:S(2)}) %all-to-all-start) | async-done | bytes 672 | tf_op jit(solution)/shard_map/all_to_all | solution.py:8
  22.5 7.7 %gather_fusion = bf16[160,64,256]{2,1,0:T(8,128)(2,1)} fusion(bf16[6,64,256]{2,1,0:T(8,128)(2,1)S(1)} %bitcast.85, s32[1024]{0:T(1024)S(1)} %pad_clamp_fusion.1), kind=kCustom, calls=%fused_computation.3 | custom fusion | bytes 10486400 | tf_op jit(solution)/shard_map/jit(_take)/gather | solution.py:53
  30.1 6.3 %select_select_fusion = bf16[160,64,256]{2,1,0:T(8,128)(2,1)} fusion(bf16[160,64,256]{2,1,0:T(8,128)(2,1)} %gather_fusion, pred[160]{0:T(512)(128)(4,1)S(1)} %le.36, pred[160]{0:T(512)(128)(4,1)S(1)} %ge.33), kind=kLoop, calls=%fused_computation.21 | loop fusion | flops 5242880 | bytes 10486080 | tf_op jit(solution)/shard_map/jit(_where)/select_n | solution.py:51
  36.4 3.8 all-to-all-start.1
  43.1 111.4 %all-to-all-done.1 = bf16[160,64,256]{2,1,0:T(8,128)(2,1)} async-done(((bf16[160,64,256]{2,1,0:T(8,128)(2,1)}), bf16[160,64,256]{2,1,0:T(8,128)(2,1)}, u32[]{:S(2)}, u32[]{:S(2)}) %all-to-all-start.1) | async-done | bytes 5242912 | tf_op jit(solution)/shard_map/all_to_all | solution.py:12
  154.5 3.4 gather_fusion.1
  160.4 144.3 %while.10 = (s32[]{:T(128)}, f32[6,6,64,256]{3,2,1,0:T(8,128)}, bf16[6,6,64,256]{3,2,1,0:T(8,128)(2,1)}, bf16[6,6,64,256]{3,2,1,0:T(8,128)(2,1)S(1)}, bf16[6,6,6...) while((s32[]{:T(128)}, f32[6,6,64,256]{3,2,1,0:T(8,128)}, ...), condition=%wide.region_3.5_spmd, body=%wide.region_2.4_spmd.sunk | while | flops 1634402304 | bytes 43452068 | solution.py:85
  160.5 10.3 %multiply_convert_fusion.2 = bf16[6,64,64,256]{3,2,1,0:T(8,128)(2,1)} fusion(f32[6,64,256]{2,1,0:T(8,128)S(1)} %get-tuple-element.124, f32[6,64,256]{2,1,0:T(8,128)S(1)} %get-tuple-element.125), kind=kLoop, calls=%fused_computation.7.clone.1 | loop fusion | flops 12582912 | bytes 13369344 | tf_op jit(solution)/shard_map/while/body/eval_jaxpr/convert_element_type | solution.py:70
  171.4 13.0 %fusion.35 = f32[6,6,64,256]{3,2,1,0:T(8,128)} fusion(f32[6,6,64,256]{3,2,1,0:T(8,128)} %get-tuple-element.135, s32[]{:T(128)} %get-tuple-element.134, bf16[6,4096,256]{2,1,0:T(8,128)(2,1)} %bitcast.84, f32[6]{0:T(128)S(1)} %fusion.34, bf16[6,6,64,4096]{3,2,1,0:T(8,128)(2,1)} %get-tuple-element.147, bf16[6,6,64,256]{3,2,1,0:T(8,128)(2,1)} %get-tuple-element.144), kind=kOutput, calls=%fused_computation.12.clone.1 | convolution fusion | flops 1621622784 | bytes 28902936 | tf_op jit(solution)/shard_map/while/body/eval_jaxpr/dot_general | solution.py:80
  184.5 10.3 %multiply_convert_fusion.2 = bf16[6,64,64,256]{3,2,1,0:T(8,128)(2,1)} fusion(f32[6,64,256]{2,1,0:T(8,128)S(1)} %get-tuple-element.124, f32[6,64,256]{2,1,0:T(8,128)S(1)} %get-tuple-element.125), kind=kLoop, calls=%fused_computation.7.clone.1 | loop fusion | flops 12582912 | bytes 13369344 | tf_op jit(solution)/shard_map/while/body/eval_jaxpr/convert_element_type | solution.py:70
  195.5 13.0 %fusion.35 = f32[6,6,64,256]{3,2,1,0:T(8,128)} fusion(f32[6,6,64,256]{3,2,1,0:T(8,128)} %get-tuple-element.135, s32[]{:T(128)} %get-tuple-element.134, bf16[6,4096,256]{2,1,0:T(8,128)(2,1)} %bitcast.84, f32[6]{0:T(128)S(1)} %fusion.34, bf16[6,6,64,4096]{3,2,1,0:T(8,128)(2,1)} %get-tuple-element.147, bf16[6,6,64,256]{3,2,1,0:T(8,128)(2,1)} %get-tuple-element.144), kind=kOutput, calls=%fused_computation.12.clone.1 | convolution fusion | flops 1621622784 | bytes 28902936 | tf_op jit(solution)/shard_map/while/body/eval_jaxpr/dot_general | solution.py:80
  208.6 10.3 %multiply_convert_fusion.2 = bf16[6,64,64,256]{3,2,1,0:T(8,128)(2,1)} fusion(f32[6,64,256]{2,1,0:T(8,128)S(1)} %get-tuple-element.124, f32[6,64,256]{2,1,0:T(8,128)S(1)} %get-tuple-element.125), kind=kLoop, calls=%fused_computation.7.clone.1 | loop fusion | flops 12582912 | bytes 13369344 | tf_op jit(solution)/shard_map/while/body/eval_jaxpr/convert_element_type | solution.py:70
  219.5 13.1 %fusion.35 = f32[6,6,64,256]{3,2,1,0:T(8,128)} fusion(f32[6,6,64,256]{3,2,1,0:T(8,128)} %get-tuple-element.135, s32[]{:T(128)} %get-tuple-element.134, bf16[6,4096,256]{2,1,0:T(8,128)(2,1)} %bitcast.84, f32[6]{0:T(128)S(1)} %fusion.34, bf16[6,6,64,4096]{3,2,1,0:T(8,128)(2,1)} %get-tuple-element.147, bf16[6,6,64,256]{3,2,1,0:T(8,128)(2,1)} %get-tuple-element.144), kind=kOutput, calls=%fused_computation.12.clone.1 | convolution fusion | flops 1621622784 | bytes 28902936 | tf_op jit(solution)/shard_map/while/body/eval_jaxpr/dot_general | solution.py:80
  232.7 10.3 %multiply_convert_fusion.2 = bf16[6,64,64,256]{3,2,1,0:T(8,128)(2,1)} fusion(f32[6,64,256]{2,1,0:T(8,128)S(1)} %get-tuple-element.124, f32[6,64,256]{2,1,0:T(8,128)S(1)} %get-tuple-element.125), kind=kLoop, calls=%fused_computation.7.clone.1 | loop fusion | flops 12582912 | bytes 13369344 | tf_op jit(solution)/shard_map/while/body/eval_jaxpr/convert_element_type | solution.py:70
  243.7 13.0 %fusion.35 = f32[6,6,64,256]{3,2,1,0:T(8,128)} fusion(f32[6,6,64,256]{3,2,1,0:T(8,128)} %get-tuple-element.135, s32[]{:T(128)} %get-tuple-element.134, bf16[6,4096,256]{2,1,0:T(8,128)(2,1)} %bitcast.84, f32[6]{0:T(128)S(1)} %fusion.34, bf16[6,6,64,4096]{3,2,1,0:T(8,128)(2,1)} %get-tuple-element.147, bf16[6,6,64,256]{3,2,1,0:T(8,128)(2,1)} %get-tuple-element.144), kind=kOutput, calls=%fused_computation.12.clone.1 | convolution fusion | flops 1621622784 | bytes 28902936 | tf_op jit(solution)/shard_map/while/body/eval_jaxpr/dot_general | solution.py:80
  256.7 10.3 %multiply_convert_fusion.2 = bf16[6,64,64,256]{3,2,1,0:T(8,128)(2,1)} fusion(f32[6,64,256]{2,1,0:T(8,128)S(1)} %get-tuple-element.124, f32[6,64,256]{2,1,0:T(8,128)S(1)} %get-tuple-element.125), kind=kLoop, calls=%fused_computation.7.clone.1 | loop fusion | flops 12582912 | bytes 13369344 | tf_op jit(solution)/shard_map/while/body/eval_jaxpr/convert_element_type | solution.py:70
  267.7 13.0 %fusion.35 = f32[6,6,64,256]{3,2,1,0:T(8,128)} fusion(f32[6,6,64,256]{3,2,1,0:T(8,128)} %get-tuple-element.135, s32[]{:T(128)} %get-tuple-element.134, bf16[6,4096,256]{2,1,0:T(8,128)(2,1)} %bitcast.84, f32[6]{0:T(128)S(1)} %fusion.34, bf16[6,6,64,4096]{3,2,1,0:T(8,128)(2,1)} %get-tuple-element.147, bf16[6,6,64,256]{3,2,1,0:T(8,128)(2,1)} %get-tuple-element.144), kind=kOutput, calls=%fused_computation.12.clone.1 | convolution fusion | flops 1621622784 | bytes 28902936 | tf_op jit(solution)/shard_map/while/body/eval_jaxpr/dot_general | solution.py:80
  280.7 10.3 %multiply_convert_fusion.2 = bf16[6,64,64,256]{3,2,1,0:T(8,128)(2,1)} fusion(f32[6,64,256]{2,1,0:T(8,128)S(1)} %get-tuple-element.124, f32[6,64,256]{2,1,0:T(8,128)S(1)} %get-tuple-element.125), kind=kLoop, calls=%fused_computation.7.clone.1 | loop fusion | flops 12582912 | bytes 13369344 | tf_op jit(solution)/shard_map/while/body/eval_jaxpr/convert_element_type | solution.py:70
  291.7 13.0 %fusion.35 = f32[6,6,64,256]{3,2,1,0:T(8,128)} fusion(f32[6,6,64,256]{3,2,1,0:T(8,128)} %get-tuple-element.135, s32[]{:T(128)} %get-tuple-element.134, bf16[6,4096,256]{2,1,0:T(8,128)(2,1)} %bitcast.84, f32[6]{0:T(128)S(1)} %fusion.34, bf16[6,6,64,4096]{3,2,1,0:T(8,128)(2,1)} %get-tuple-element.147, bf16[6,6,64,256]{3,2,1,0:T(8,128)(2,1)} %get-tuple-element.144), kind=kOutput, calls=%fused_computation.12.clone.1 | convolution fusion | flops 1621622784 | bytes 28902936 | tf_op jit(solution)/shard_map/while/body/eval_jaxpr/dot_general | solution.py:80
  307.1 7.6 %scatter_fusion = f32[64,64,256]{2,1,0:T(8,128)} fusion(f32[64,64,256]{2,1,0:T(8,128)} %broadcast_in_dim.69, s32[36]{0:T(128)S(1)} %copy-done.3, f32[36,64,256]{2,1,0:T(8,128)S(1)} %bitcast.89), kind=kCustom, calls=%fused_computation.6 | custom fusion | bytes 7078032 | tf_op jit(solution)/shard_map/scatter | solution.py:92
  314.7 6.6 %all-to-all-start.2 = ((f32[64,64,256]{2,1,0:T(8,128)}), f32[64,64,256]{2,1,0:T(8,128)}, u32[]{:S(2)}, u32[]{:S(2)}) async-start(f32[64,64,256]{2,1,0:T(8,128)} %scatter_fusion), calls=%async_computation.2 | async-start | bytes 8388608 | tf_op jit(solution)/shard_map/all_to_all | solution.py:16
  321.4 91.9 %all-to-all-done.2 = f32[64,64,256]{2,1,0:T(8,128)} async-done(((f32[64,64,256]{2,1,0:T(8,128)}), f32[64,64,256]{2,1,0:T(8,128)}, u32[]{:S(2)}, u32[]{:S(2)}) %all-to-all-start.2) | async-done | bytes 4194336 | tf_op jit(solution)/shard_map/all_to_all | solution.py:16
  413.3 4.6 %copy.12 = f32[8,8,64,256]{3,1,2,0:T(8,128)S(1)} copy(f32[8,8,64,256]{3,2,1,0:T(8,128)} %bitcast.31) | data formatting | bytes 8388608
  (56 shorter events, 23.5 us)
Async XLA Ops:
  7.5 14.4 %all-to-all-start = ((s32[32,5,1]{1,2,0:T(1,128)}), s32[32,5,1]{1,2,0:T(1,128)S(1)}, u32[]{:S(2)}, u32[]{:S(2)}) async-start(s32[32,5,1]{1,2,0:T(1,128)} %bitcast.19), calls=%async_computation | async-start | bytes 32768 | tf_op jit(solution)/shard_map/all_to_all | solution.py:8
  36.4 118.1 %all-to-all-start.1 = ((bf16[160,64,256]{2,1,0:T(8,128)(2,1)}), bf16[160,64,256]{2,1,0:T(8,128)(2,1)}, u32[]{:S(2)}, u32[]{:S(2)}) async-start(bf16[160,64,256]{2,1,0:T(8,128)(2,1)} %select_select_fusion), calls=%async_computation.1 | async-start | bytes 10485760 | tf_op jit(solution)/shard_map/all_to_all | solution.py:12
  304.7 2.5 copy-start
  304.7 2.5 copy-start.3
  314.7 98.6 %all-to-all-start.2 = ((f32[64,64,256]{2,1,0:T(8,128)}), f32[64,64,256]{2,1,0:T(8,128)}, u32[]{:S(2)}, u32[]{:S(2)}) async-start(f32[64,64,256]{2,1,0:T(8,128)} %scatter_fusion), calls=%async_computation.2 | async-start | bytes 8388608 | tf_op jit(solution)/shard_map/all_to_all | solution.py:16
  417.9 1.6 copy-start.1
  417.9 1.6 copy-start.2
where the time goes:
time: 423 us; the launch traced here: 421 us
  waiting for transfers between devices  209 us (49%)
  matrix products  79.5 us (19%)
  other arithmetic  76.5 us (18%)
  local copies, waits for them, and re-layouts  36.7 us (9%)
  starting transfers between devices  17.6 us (4%)
    all_to_all x1, waiting for transfers between devices, route_rows(): lax.all_to_all(values, ('blk', 'grp'), split_axis=0, concat_axis=0, tiled...  111 us
    all_to_all x1, waiting for transfers between devices, route_partials(): lax.all_to_all(values, ('blk', 'grp'), split_axis=0, concat_axis=0, tiled...  91.9 us
    dot_general x6, matrix products, group_step(): lax.dot_general(resid, pair, (((2,), (1,)), ((0,), (0,))), preferred_elem...  78.1 us
    convert_element_type x6, other arithmetic, group_step(): pair = (rows_b.astype(jnp.float32)[:, :, None, :] * rows_c.astype(jnp.flo...  61.6 us
  transfers between devices with their start and end apart: 3, of which 3 were waited for; matrix products, arithmetic and copies ran while one was open for 1% of the time, Pallas kernels for 0%

commit v1 on v0

v1 whole, which is shorter than its diff:
```python
import functools

import jax
import jax.numpy as jnp
from jax import lax
from jax.experimental import pallas as pl
from jax.experimental.pallas import tpu as pltpu
from jax.sharding import PartitionSpec as P

AXES = ("blk", "grp")
BUFFERS = 3
TILE_J = 4


def slots_kernel(
    local_blocks,
    coords_ref,
    count_ref,
    owner_ref,
    blocks_ref,
    table_ref,
    grad_ref,
    blocks_buf,
    rows_buf,
    block_sems,
    row_sems,
):
    edge, rank = rows_buf.shape[2], rows_buf.shape[3]
    count = count_ref[0]
    grad_ref[...] = jnp.zeros_like(grad_ref)

    def copies(slot):
        at = lax.rem(slot, BUFFERS)
        out = [pltpu.make_async_copy(blocks_ref.at[slot], blocks_buf.at[at], block_sems.at[at])]
        for mode in range(3):
            pos = owner_ref[mode, coords_ref[mode, slot]]
            device = lax.div(pos, local_blocks)
            place = (device * 3 + mode) * local_blocks + lax.rem(pos, local_blocks)
            out.append(
                pltpu.make_async_copy(
                    table_ref.at[place], rows_buf.at[at, mode], row_sems.at[at, mode]
                )
            )
        return out

    def start(slot):
        @pl.when(slot < count)
        def _():
            for copy in copies(slot):
                copy.start()

    for slot in range(BUFFERS - 1):
        start(slot)

    def step(slot, carry):
        start(slot + BUFFERS - 1)
        for copy in copies(slot):
            copy.wait()
        at = lax.rem(slot, BUFFERS)
        rows_a = rows_buf[at, 0] * jnp.asarray(0.5, jnp.bfloat16)
        rows_c = rows_buf[at, 2]
        width = TILE_J * edge
        tiles = edge // TILE_J

        def pair_of(tile):
            return jnp.concatenate(
                [
                    rows_buf[at, 1, pl.ds(tile * TILE_J + j, 1), :] * rows_c
                    for j in range(TILE_J)
                ],
                axis=0,
            )

        def half_model(pair):
            return lax.dot_general(
                rows_a, pair, (((1,), (1,)), ((), ())), preferred_element_type=jnp.float32
            )

        total = jnp.zeros((edge, rank), jnp.float32)
        pair = pair_of(0)
        model = half_model(pair)
        for tile in range(tiles):
            if tile + 1 < tiles:
                next_pair = pair_of(tile + 1)
                next_model = half_model(next_pair)
            twice = blocks_buf[at, :, tile * width : (tile + 1) * width].astype(jnp.float32) * 2.0
            resid = ((jnp.tanh(model) + 1.0) - twice).astype(jnp.bfloat16)
            total = total + jnp.dot(resid, pair, preferred_element_type=jnp.float32)
            if tile + 1 < tiles:
                pair, model = next_pair, next_model
        target = owner_ref[0, coords_ref[0, slot]]
        grad_ref[target] += 0.5 * total
        return carry

    lax.fori_loop(0, count, step, 0)


def per_device(tensor_blocks, block_coords, block_count, row_owner, factors, moment1, moment2):
    slot_count, edge, width = tensor_blocks.shape
    rank = factors.shape[2]
    local_blocks = moment1.shape[0] // edge
    row_blocks = row_owner.shape[1]
    shard = factors.astype(jnp.bfloat16).reshape(3 * local_blocks, edge, rank)
    table = lax.all_gather(shard, AXES, axis=0, tiled=True)
    smem = pl.BlockSpec(memory_space=pltpu.SMEM)
    hbm = pl.BlockSpec(memory_space=pl.ANY)
    flops = 4 * slot_count * edge * width * rank
    grads = pl.pallas_call(
        functools.partial(slots_kernel, local_blocks),
        out_shape=jax.ShapeDtypeStruct((row_blocks, edge, rank), jnp.float32),
        in_specs=[smem, smem, smem, hbm, hbm],
        out_specs=pl.BlockSpec(memory_space=pltpu.VMEM),
        scratch_shapes=[
            pltpu.VMEM((BUFFERS, edge, width), jnp.bfloat16),
            pltpu.VMEM((BUFFERS, 3, edge, rank), jnp.bfloat16),
            pltpu.SemaphoreType.DMA((BUFFERS,)),
            pltpu.SemaphoreType.DMA((BUFFERS, 3)),
        ],
        compiler_params=pltpu.CompilerParams(vmem_limit_bytes=48 * 1024 * 1024),
        cost_estimate=pl.CostEstimate(
            flops=flops,
            bytes_accessed=2 * slot_count * edge * width,
            transcendentals=slot_count * edge * width,
        ),
    )(block_coords, block_count, row_owner, tensor_blocks, table)
    grad = lax.psum_scatter(
        grads.reshape(row_blocks * edge, rank), AXES, scatter_dimension=0, tiled=True
    )
    new_moment1 = 0.9 * moment1 + 0.1 * grad
    new_moment2 = 0.999 * moment2 + 0.001 * grad * grad
    new_factor = factors[0] - 0.02 * (new_moment1 / (1.0 - 0.9**8)) / (
        jnp.sqrt(new_moment2 / (1.0 - 0.999**8)) + 1e-08
    )
    return (new_factor, new_moment1, new_moment2)


def solution(mesh):
    return jax.shard_map(
        per_device,
        mesh=mesh,
        in_specs=(
            P(AXES, None, None),
            P(None, AXES),
            P(AXES),
            P(),
            P(None, AXES, None),
            P(AXES, None),
            P(AXES, None),
        ),
        out_specs=(P(AXES, None), P(AXES, None), P(AXES, None)),
        check_vma=False,
    )
```

time: 423 us -> 292 us (0.69)
  matrix products: 79.5 us -> 0 us
  other arithmetic: 76.5 us -> 3.44 us
  Pallas kernels: 0 us -> 50.6 us
  local copies, waits for them, and re-layouts: 36.7 us -> 3.3 us
  starting transfers between devices: 17.6 us -> 0.08 us
  between operations: 1.43 us -> 14.7 us
  waiting for transfers between devices: 209 us -> 220 us
    all_to_all x3 -> x0, waiting for transfers between devices: 209 us -> none  [the longest x1 111 us: route_rows(): lax.all_to_all(values, ('blk', 'grp'), split_axis=0, concat_axis=0, tiled...]
    reduce_scatter x0 -> x1, waiting for transfers between devices: none -> 146 us  [per_device(): lax.psum_scatter(grads.reshape(row_blocks * edge, rank), AXES, scatter_di...]
    dot_general x7 -> x0, matrix products: 79.5 us -> none  [the longest x6 78.1 us: group_step(): lax.dot_general(resid, pair, (((2,), (1,)), ((0,), (0,))), preferred_elem...]
    all_gather x0 -> x1, waiting for transfers between devices: none -> 73.6 us  [per_device(): table = lax.all_gather(shard, AXES, axis=0, tiled=True)]
    convert_element_type x14 -> x1, other arithmetic: 63.6 us -> 1.69 us  [per_device(): shard = factors.astype(jnp.bfloat16).reshape(3 * local_blocks, edge, rank)]
    pallas_call x0 -> x1, Pallas kernels: none -> 50.6 us  [per_device(): pl.pallas_call(functools.partial(slots_kernel, local_blocks), out_shape=j...]
    all_to_all x3 -> x0, starting transfers between devices: 17.6 us -> none  [the longest x1 7.3 us: route_requests(): lax.all_to_all(values, ('blk', 'grp'), split_axis=0, concat_axis=0, tiled...]
    gather x5 -> x0, local copies, waits for them, and re-layouts: 13.4 us -> none  [the longest x1 7.65 us: per_device(): jnp.take(table, jnp.maximum(incoming, 0), axis=0)]
  transfers between devices with their start and end apart: 3 -> 2, of which waited for: 3 -> 2; matrix products, arithmetic and copies ran while one was open for 1% -> 0% of each run, Pallas kernels for 0% -> 0%
where the time goes in v1:
time: 292 us
  waiting for transfers between devices  220 us (75%)
  Pallas kernels  50.6 us (17%)
  between operations  14.7 us (5%)
  other arithmetic  3.44 us (1%)
  local copies, waits for them, and re-layouts  3.3 us (1%)
    reduce_scatter x1, waiting for transfers between devices, per_device(): lax.psum_scatter(grads.reshape(row_blocks * edge, rank), AXES, scatter_di...  146 us
    all_gather x1, waiting for transfers between devices, per_device(): table = lax.all_gather(shard, AXES, axis=0, tiled=True)  73.6 us
    pallas_call x1, Pallas kernels, per_device(): pl.pallas_call(functools.partial(slots_kernel, local_blocks), out_shape=j...  50.6 us
  transfers between devices with their start and end apart: 2, of which 2 were waited for; matrix products, arithmetic and copies ran while one was open for 0% of the time, Pallas kernels for 0%

profile of v1, /device:TPU:0, one launch (start us, length us, event | category | flops | bytes accessed | tf_op | source)
XLA Modules:
  0.0 292.0 jit_solution(6401748707094724111)
XLA Ops:
  7.2 0.0 all-gather.2.cloned.1.call-start
  7.2 1.7 convert_element_type.3
  8.9 0.0 all-gather.2.cloned.1.call-update
  8.9 0.0 reduce-scatter.2.cloned.1.call-start
  9.6 73.6 %all-gather.2.cloned.1.call-done.table_ref = bf16[192,64,256]{2,1,0:T(8,128)(2,1)} async-done(((bf16[6,64,256]{2,1,0:T(8,128)(2,1)}), bf16[192,64,256]{2,1,0:T(8,128)(2,1)}) %all-gather.2.cloned.1.call-update) | async-done | bytes 6291472 | tf_op jit(solution)/shard_map/all_gather | solution.py:104
  83.2 0.0 copy-start.1
  83.2 0.7 copy-done.1
  83.9 0.0 copy-start.2
  83.9 0.7 copy-done.2
  84.5 0.0 copy-start.3
  84.5 0.0 copy-start.4
  84.5 50.6 %shard_map.94 = f32[64,64,256]{2,1,0:T(8,128)S(1)} custom-call(s32[3,36]{1,0:T(4,128)S(1)} %copy-done.1, s32[1]{0:T(128)S(6)} %copy.10.count_ref, s32[3,64]{1,0:T(4,128)S(1)} %copy-done.2, bf16[36,64,4096]{2,1,0:T(8,128)(2,1)} %blocks_ref.1, bf16[192,64,256]{2,1,0:T(8,128)(2,1)} %all-gather.2.cloned.1.call-done.table_ref), custom_call_target="tpu_custom_call" | custom-call | flops 9663676416 | bytes 18874368 | tf_op jit(solution)/shard_map/pallas_call | solution.py:108
  135.1 0.0 copy-start
  135.1 1.9 copy-done
  137.0 0.0 reduce-scatter.2.cloned.1.call-update
  137.1 146.4 %reduce-scatter.2.cloned.1.call-done = f32[128,256]{1,0:T(8,128)} async-done(((f32[4096,256]{1,0:T(8,128)}), f32[128,256]{1,0:T(8,128)}) %reduce-scatter.2.cloned.1.call-update) | async-done | bytes 131088 | tf_op jit(solution)/shard_map/reduce_scatter | solution.py:126
  283.4 0.0 copy-done.3
  283.4 0.0 copy-done.4
  283.4 1.8 bitcast_subtract_fusion
Async XLA Ops:
  7.2 76.0 %all-gather.2.cloned.1.call-start = ((), (), s32[]{:S(2)}) async-start(), calls=%async_computation.1 | async-start | bytes 6488064 | tf_op jit(solution)/shard_map/all_gather | solution.py:104
  8.9 274.5 %reduce-scatter.2.cloned.1.call-start = ((), (), s32[]{:S(2)}) async-start(), calls=%async_computation.2 | async-start | bytes 4325376 | tf_op jit(solution)/shard_map/reduce_scatter | solution.py:126
  83.2 0.7 copy-start.1
  83.9 0.7 copy-start.2
  84.5 198.9 %copy-start.3 = (f32[128,256]{1,0:T(8,128)S(1)}, f32[128,256]{1,0:T(8,128)}, u32[]{:S(2)}) copy-start(f32[128,256]{1,0:T(8,128)} %param.12) | copy-start | bytes 393220
  84.5 198.9 %copy-start.4 = (f32[128,256]{1,0:T(8,128)S(1)}, f32[128,256]{1,0:T(8,128)}, u32[]{:S(2)}) copy-start(f32[128,256]{1,0:T(8,128)} %param.13) | copy-start | bytes 393220
  135.1 1.9 copy-start
Sparse Core Ops, SparseCore 0:
  10.9 72.2 all-gather.1
  137.2 146.1 reduce-scatter.1

commit v2 on v1

v2 whole, which is shorter than its diff:
```python
import functools

import jax
import jax.numpy as jnp
from jax import lax
from jax.experimental import pallas as pl
from jax.experimental.pallas import tpu as pltpu
from jax.sharding import PartitionSpec as P

AXES = ("blk", "grp")
CORES = 2
BUFFERS = 4
AHEAD = 2
TILE_J = 4
LAG = 2


def mesh_dims(blk, grp):
    chips = blk // CORES
    inner = 1
    for width in range(1, chips + 1):
        if chips % width == 0 and width * width <= chips:
            inner = width
    return {"outer": chips // inner, "inner": inner, "core": CORES, "line": grp}


def split_index(index, dims):
    line = lax.rem(index, dims["line"])
    rest = lax.div(index, dims["line"])
    core = lax.rem(rest, dims["core"])
    rest = lax.div(rest, dims["core"])
    return {
        "outer": lax.div(rest, dims["inner"]),
        "inner": lax.rem(rest, dims["inner"]),
        "core": core,
        "line": line,
    }


def shift(values, dims, name, step):
    strides = {
        "line": 1,
        "core": dims["line"],
        "inner": dims["line"] * dims["core"],
        "outer": dims["line"] * dims["core"] * dims["inner"],
    }
    total = strides["outer"] * dims["outer"]
    stride, size = strides[name], dims[name]
    perm = []
    for source in range(total):
        at = source // stride % size
        perm.append((source, source + ((at + step) % size - at) * stride))
    return lax.ppermute(values, AXES, perm)


ORDERS = (("outer", "inner"), ("inner", "outer"))


def gather_rows(shard, dims):
    count = shard.shape[0]
    cut = count // 2
    line = [shard] + [shift(shard, dims, "line", k) for k in range(1, dims["line"])]
    halves = []
    for part, (first, second) in zip((slice(0, cut), slice(cut, count)), ORDERS):
        own = jnp.concatenate([piece[part] for piece in line])
        own = jnp.concatenate([own] + [shift(own, dims, first, k) for k in range(1, dims[first])])
        pieces = [own] + [shift(own, dims, second, k) for k in range(1, dims[second])]
        pieces = pieces + [shift(piece, dims, "core", 1) for piece in pieces]
        halves.append(pieces)
    return halves


def slots_kernel(dims, local_blocks, piece_count, *refs):
    coords_ref, count_ref, owner_ref, blocks_ref = refs[:4]
    pieces = refs[4 : 4 + piece_count]
    (
        mine_ref,
        other_ref,
        table_ref,
        grad_ref,
        blocks_buf,
        pair_ref,
        model_ref,
        total_ref,
        block_sems,
        piece_sems,
        out_sems,
    ) = refs[4 + piece_count :]
    edge, rank = grad_ref.shape[1], grad_ref.shape[2]
    width = TILE_J * edge
    tiles = edge // TILE_J
    count = count_ref[0]
    cut = 3 * local_blocks // 2
    here = split_index(lax.axis_index("blk") * dims["line"] + lax.axis_index("grp"), dims)
    columns = dims["core"] * dims["outer"] * dims["inner"] * dims["line"]

    def row_place(mode, slot):
        pos = owner_ref[mode, coords_ref[mode, slot]]
        there = split_index(lax.div(pos, local_blocks), dims)
        away = {
            name: lax.rem(here[name] - there[name] + dims[name], dims[name]) for name in dims
        }
        block = mode * local_blocks + lax.rem(pos, local_blocks)
        late = block >= cut
        second = jnp.where(late, away["outer"], away["inner"])
        first = jnp.where(late, away["inner"], away["outer"])
        size_first = jnp.where(late, dims["inner"], dims["outer"])
        size_second = jnp.where(late, dims["outer"], dims["inner"])
        spot = ((away["core"] * size_second + second) * size_first + first) * dims["line"]
        spot = spot + away["line"]
        blocks_of = jnp.where(late, 3 * local_blocks - cut, cut)
        base = jnp.where(late, columns * cut, 0)
        return base + spot * blocks_of + jnp.where(late, block - cut, block)

    def grad_place(slot):
        pos = owner_ref[0, coords_ref[0, slot]]
        there = split_index(lax.div(pos, local_blocks), dims)
        away = {
            name: lax.rem(there[name] - here[name] + dims[name], dims[name]) for name in dims
        }
        local = lax.rem(pos, local_blocks)
        half_blocks = local_blocks // 2
        late = local >= half_blocks
        second = jnp.where(late, away["outer"], away["inner"])
        first = jnp.where(late, away["inner"], away["outer"])
        size_first = jnp.where(late, dims["inner"], dims["outer"])
        size_second = jnp.where(late, dims["outer"], dims["inner"])
        half = jnp.where(late, 1, 0)
        spot = ((away["core"] * 2 + half) * size_second + second) * size_first + first
        spot = spot * dims["line"] + away["line"]
        return spot * half_blocks + jnp.where(late, local - half_blocks, local)

    def block_copy(slot):
        at = lax.rem(slot, BUFFERS)
        return pltpu.make_async_copy(blocks_ref.at[slot], blocks_buf.at[at], block_sems.at[at])

    def start(slot):
        @pl.when(slot < count)
        def _():
            block_copy(slot).start()

    fills = []
    offset = 0
    for index, piece in enumerate(pieces):
        size = piece.shape[0]
        fills.append(
            pltpu.make_async_copy(
                piece, table_ref.at[pl.ds(offset, size)], piece_sems.at[index]
            )
        )
        offset += size
    for fill in fills:
        fill.start()
    for slot in range(AHEAD):
        start(slot)
    grad_ref[...] = jnp.zeros_like(grad_ref)
    for tile in range(tiles - LAG, tiles):
        pair_ref[tile] = jnp.zeros((width, rank), jnp.bfloat16)
        model_ref[tile] = jnp.zeros((edge, width), jnp.float32)
    total_ref[...] = jnp.zeros_like(total_ref)
    for fill in fills:
        fill.wait()

    def finish(tile, at, total):
        twice = blocks_buf[at, :, tile * width : (tile + 1) * width].astype(jnp.float32) * 2.0
        resid = ((jnp.tanh(model_ref[tile]) + 1.0) - twice).astype(jnp.bfloat16)
        return total + jnp.dot(resid, pair_ref[tile], preferred_element_type=jnp.float32)

    def step(slot, carry):
        start(slot + AHEAD)
        block_copy(slot).wait()
        at = lax.rem(slot, BUFFERS)
        before = jnp.maximum(slot - 1, 0)
        at_before = lax.rem(before, BUFFERS)
        place_b = row_place(1, slot)
        rows_a = table_ref[row_place(0, slot)] * jnp.asarray(0.5, jnp.bfloat16)
        rows_c = table_ref[row_place(2, slot)]
        total_before = total_ref[...]
        total = jnp.zeros((edge, rank), jnp.float32)
        for tile in range(tiles):
            if tile >= LAG:
                total = finish(tile - LAG, at, total)
            else:
                total_before = finish(tiles - LAG + tile, at_before, total_before)
            pair = jnp.concatenate(
                [
                    table_ref[place_b, pl.ds(tile * TILE_J + j, 1), :] * rows_c
                    for j in range(TILE_J)
                ],
                axis=0,
            )
            pair_ref[tile] = pair
            model_ref[tile] = lax.dot_general(
                rows_a, pair, (((1,), (1,)), ((), ())), preferred_element_type=jnp.float32
            )
        grad_ref[grad_place(before)] += 0.5 * total_before
        total_ref[...] = total
        return carry

    lax.fori_loop(0, count, step, 0)
    last = count - 1
    total = total_ref[...]
    for tile in range(tiles - LAG, tiles):
        total = finish(tile, lax.rem(last, BUFFERS), total)
    grad_ref[grad_place(last)] += 0.5 * total
    half = grad_ref.shape[0] // 2
    for index, out in enumerate((mine_ref, other_ref)):
        pltpu.make_async_copy(
            grad_ref.at[pl.ds(index * half, half)], out, out_sems.at[index]
        ).start()
    for index, out in enumerate((mine_ref, other_ref)):
        pltpu.make_async_copy(
            grad_ref.at[pl.ds(index * half, half)], out, out_sems.at[index]
        ).wait()


def per_device(tensor_blocks, block_coords, block_count, row_owner, factors, moment1, moment2):
    slot_count, edge, width = tensor_blocks.shape
    rank = factors.shape[2]
    local_blocks = moment1.shape[0] // edge
    row_blocks = row_owner.shape[1]
    dims = mesh_dims(lax.axis_size("blk"), lax.axis_size("grp"))
    shard = factors.astype(jnp.bfloat16).reshape(3 * local_blocks, edge, rank)
    halves = gather_rows(shard, dims)
    pieces = halves[0] + halves[1]
    smem = pl.BlockSpec(memory_space=pltpu.SMEM)
    hbm = pl.BlockSpec(memory_space=pl.ANY)
    tiles = edge // TILE_J
    outgoing = jax.ShapeDtypeStruct((row_blocks // 2, edge, rank), jnp.float32)
    mine, other = pl.pallas_call(
        functools.partial(slots_kernel, dims, local_blocks, len(pieces)),
        out_shape=(outgoing, outgoing),
        in_specs=[smem, smem, smem, hbm] + [hbm] * len(pieces),
        out_specs=(hbm, hbm),
        scratch_shapes=[
            pltpu.VMEM((3 * row_blocks, edge, rank), jnp.bfloat16),
            pltpu.VMEM((row_blocks, edge, rank), jnp.float32),
            pltpu.VMEM((BUFFERS, edge, width), jnp.bfloat16),
            pltpu.VMEM((tiles, TILE_J * edge, rank), jnp.bfloat16),
            pltpu.VMEM((tiles, edge, TILE_J * edge), jnp.float32),
            pltpu.VMEM((edge, rank), jnp.float32),
            pltpu.SemaphoreType.DMA((BUFFERS,)),
            pltpu.SemaphoreType.DMA((len(pieces),)),
            pltpu.SemaphoreType.DMA((2,)),
        ],
        compiler_params=pltpu.CompilerParams(vmem_limit_bytes=56 * 1024 * 1024),
        cost_estimate=pl.CostEstimate(
            flops=4 * slot_count * edge * width * rank,
            bytes_accessed=2 * slot_count * edge * width,
            transcendentals=slot_count * edge * width,
        ),
    )(block_coords, block_count, row_owner, tensor_blocks, *pieces)

    def by_half(values):
        values = values.reshape(2, row_blocks // 4, edge, rank)
        out = []
        for half, (first, second) in enumerate(ORDERS):
            out.append(
                values[half].reshape(
                    dims[second], dims[first], dims["line"], local_blocks // 2 * edge, rank
                )
            )
        return out

    arrived = by_half(shift(other, dims, "core", 1))
    kept_halves = by_half(mine)
    grads = []
    for half, (first, second) in enumerate(ORDERS):
        kept, got = kept_halves[half], [arrived[half]]
        for name in (second, first, "line"):
            sums = [
                functools.reduce(jnp.add, [g[k] for g in got], kept[k]) for k in range(dims[name])
            ]
            kept = sums[0]
            got = [shift(sums[k], dims, name, k) for k in range(1, dims[name])]
        grads.append(functools.reduce(jnp.add, got, kept))
    grad = jnp.concatenate(grads)
    new_moment1 = 0.9 * moment1 + 0.1 * grad
    new_moment2 = 0.999 * moment2 + 0.001 * grad * grad
    new_factor = factors[0] - 0.02 * (new_moment1 / (1.0 - 0.9**8)) / (
        jnp.sqrt(new_moment2 / (1.0 - 0.999**8)) + 1e-08
    )
    return (new_factor, new_moment1, new_moment2)


def solution(mesh):
    return jax.shard_map(
        per_device,
        mesh=mesh,
        in_specs=(
            P(AXES, None, None),
            P(None, AXES),
            P(AXES),
            P(),
            P(None, AXES, None),
            P(AXES, None),
            P(AXES, None),
        ),
        out_specs=(P(AXES, None), P(AXES, None), P(AXES, None)),
        check_vma=False,
    )
```

time: 292 us -> 154 us (0.53)
  waiting for transfers between devices: 220 us -> 53.9 us
  starting transfers between devices: 0.08 us -> 73.4 us
  Pallas kernels: 50.6 us -> 17.9 us
  between operations: 14.7 us -> 1.54 us
    reduce_scatter x1 -> x0, waiting for transfers between devices: 146 us -> none  [per_device(): lax.psum_scatter(grads.reshape(row_blocks * edge, rank), AXES, scatter_di...]
    all_gather x1 -> x0, waiting for transfers between devices: 73.6 us -> none  [per_device(): table = lax.all_gather(shard, AXES, axis=0, tiled=True)]
    ppermute x0 -> x22, starting transfers between devices: none -> 73.4 us  [shift(): return lax.ppermute(values, AXES, perm)]
    ppermute x0 -> x22, waiting for transfers between devices: none -> 53.9 us  [shift(): return lax.ppermute(values, AXES, perm)]
    pallas_call x1, Pallas kernels: 50.6 us -> 17.9 us  [per_device(): pl.pallas_call(functools.partial(slots_kernel, dims, local_blocks, len(pi...]
  transfers between devices with their start and end apart: 2 -> 22, of which waited for: 2 -> 11; matrix products, arithmetic and copies ran while one was open for 0% -> 0% of each run, Pallas kernels for 0% -> 0%
where the time goes in v2:
time: 154 us; the launch traced here: 153 us
  starting transfers between devices  73.4 us (48%)
  waiting for transfers between devices  53.9 us (35%)
  Pallas kernels  17.9 us (12%)
  other arithmetic  4.93 us (3%)
  between operations  1.54 us (1%)
    ppermute x22, starting transfers between devices, shift(): return lax.ppermute(values, AXES, perm)  73.4 us
    ppermute x22, waiting for transfers between devices, shift(): return lax.ppermute(values, AXES, perm)  53.9 us
    pallas_call x1, Pallas kernels, per_device(): pl.pallas_call(functools.partial(slots_kernel, dims, local_blocks, len(pi...  17.9 us
  transfers between devices with their start and end apart: 22, of which 11 were waited for; matrix products, arithmetic and copies ran while one was open for 0% of the time, Pallas kernels for 0%

profile of v2, /device:TPU:0, one launch (start us, length us, event | category | flops | bytes accessed | tf_op | source)
XLA Modules:
  0.0 152.7 jit_solution(5400881020031021747)
XLA Ops:
  1.7 5.1 %collective-permute-start.2 = (bf16[6,64,256]{2,1,0:T(8,128)(2,1)S(1)}, bf16[6,64,256]{2,1,0:T(8,128)(2,1)S(1)}, u32[]{:S(2)}, u32[]{:S(2)}) collective-permute-start(bf16[6,64,256]{2,1,0:T(8,128)(2,1)S(1)} %bitcast.85), channel_id=1, source_target_pairs={{0,3},{1,0},{2,1},{3,2},{4,7},{5,4},{6,5},{7,6},{8,11},{9,8},{10,9... | collective-permute-start | bytes 589832 | tf_op jit(solution)/shard_map/ppermute | solution.py:53
  7.8 12.5 %collective-permute-done = bf16[6,64,256]{2,1,0:T(8,128)(2,1)S(1)} collective-permute-done((bf16[6,64,256]{2,1,0:T(8,128)(2,1)S(1)}, bf16[6,64,256]{2,1,0:T(8,128)(2,1)S(1)}, u32[]{:S(2)}, u32[]{:S(2)}) %collective-permute-start) | collective-permute-done | bytes 196640 | tf_op jit(solution)/shard_map/ppermute | solution.py:53
  20.4 3.1 %collective-permute-done.1 = bf16[6,64,256]{2,1,0:T(8,128)(2,1)S(1)} collective-permute-done((bf16[6,64,256]{2,1,0:T(8,128)(2,1)S(1)}, bf16[6,64,256]{2,1,0:T(8,128)(2,1)S(1)}, u32[]{:S(2)}, u32[]{:S(2)}) %collective-permute-start.1) | collective-permute-done | bytes 196640 | tf_op jit(solution)/shard_map/ppermute | solution.py:53
  23.6 1.6 %collective-permute-start.7 = (bf16[12,64,256]{2,1,0:T(8,128)(2,1)S(1)}, bf16[12,64,256]{2,1,0:T(8,128)(2,1)S(1)}, u32[]{:S(2)}, u32[]{:S(2)}) collective-permute-start(bf16[12,64,256]{2,1,0:T(8,128)(2,1)S(1)} %pad_maximum_fusion.1), channel_id=1, source_target_pairs={{0,8},{1,9},{2,10},{3,11},{4,12},{5,13},{6,14},{7,15},{8,0},{9,1},... | collective-permute-start | bytes 1179656 | tf_op jit(solution)/shard_map/ppermute | solution.py:53
  25.2 1.6 %collective-permute-start.3 = (bf16[12,64,256]{2,1,0:T(8,128)(2,1)S(1)}, bf16[12,64,256]{2,1,0:T(8,128)(2,1)S(1)}, u32[]{:S(2)}, u32[]{:S(2)}) collective-permute-start(bf16[12,64,256]{2,1,0:T(8,128)(2,1)S(1)} %pad_maximum_fusion), channel_id=1, source_target_pairs={{0,16},{1,17},{2,18},{3,19},{4,20},{5,21},{6,22},{7,23},{8,24},{9,... | collective-permute-start | bytes 1179656 | tf_op jit(solution)/shard_map/ppermute | solution.py:53
  26.8 7.1 %collective-permute-done.7 = bf16[12,64,256]{2,1,0:T(8,128)(2,1)S(1)} collective-permute-done((bf16[12,64,256]{2,1,0:T(8,128)(2,1)S(1)}, bf16[12,64,256]{2,1,0:T(8,128)(2,1)S(1)}, u32[]{:S(2)}, u32[]{:S(2)}) %collective-permute-start.7) | collective-permute-done | bytes 393248 | tf_op jit(solution)/shard_map/ppermute | solution.py:53
  33.9 1.6 %collective-permute-start.8 = (bf16[24,64,256]{2,1,0:T(8,128)(2,1)S(1)}, bf16[24,64,256]{2,1,0:T(8,128)(2,1)S(1)}, u32[]{:S(2)}, u32[]{:S(2)}) collective-permute-start(bf16[24,64,256]{2,1,0:T(8,128)(2,1)S(1)} %constant_dynamic-update-slice_fusion.5.refs_8_), channel_id=1, source_target_pairs={{0,16},{1,17},{2,18},{3,19},{4,20},{5,21},{6,22},{7,23},{8,24},{9,... | collective-permute-start | bytes 2359304 | tf_op jit(solution)/shard_map/ppermute | solution.py:53
  35.5 1.5 %collective-permute-start.4 = (bf16[24,64,256]{2,1,0:T(8,128)(2,1)S(1)}, bf16[24,64,256]{2,1,0:T(8,128)(2,1)S(1)}, u32[]{:S(2)}, u32[]{:S(2)}) collective-permute-start(bf16[24,64,256]{2,1,0:T(8,128)(2,1)S(1)} %constant_dynamic-update-slice_fusion.refs_4_), channel_id=1, source_target_pairs={{0,8},{1,9},{2,10},{3,11},{4,12},{5,13},{6,14},{7,15},{8,0},{9,1},... | collective-permute-start | bytes 2359304 | tf_op jit(solution)/shard_map/ppermute | solution.py:53
  37.6 14.4 %collective-permute-done.8.refs_9_ = bf16[24,64,256]{2,1,0:T(8,128)(2,1)S(1)} collective-permute-done((bf16[24,64,256]{2,1,0:T(8,128)(2,1)S(1)}, bf16[24,64,256]{2,1,0:T(8,128)(2,1)S(1)}, u32[]{:S(2)}, u32[]{:S(2)}) %collective-permute-start.8) | collective-permute-done | bytes 786464 | tf_op jit(solution)/shard_map/ppermute | solution.py:53
  56.4 17.9 %shard_map.94 = (f32[32,64,256]{2,1,0:T(8,128)}, f32[32,64,256]{2,1,0:T(8,128)}) custom-call(s32[3,36]{1,0:T(4,128)} %refs_0_.1, s32[1]{0:T(128)S(6)} %copy.18.refs_1_, s32[3,64]{1,0:T(4,128)} %refs_2_.1, bf16[36,64,4096]{2,1,0:T(8,128)(2,1)} %refs_3_.1, bf16[24,64,256]{2,1,0:T(8,128)(2,1)} %copy-done.2, bf16[24,64,256]{2,1,0:T(8,128)(2,1)} %copy-done.5, ...), custom_call_target="tpu_custom_call" | custom-call | flops 9663676416 | bytes 18874368 | tf_op jit(solution)/shard_map/pallas_call | solution.py:230
  74.3 14.8 %collective-permute-start.11 = (f32[32,64,256]{2,1,0:T(8,128)}, f32[32,64,256]{2,1,0:T(8,128)S(1)}, u32[]{:S(2)}, u32[]{:S(2)}) collective-permute-start(f32[32,64,256]{2,1,0:T(8,128)} %get-tuple-element.6), channel_id=1, source_target_pairs={{0,4},{1,5},{2,6},{3,7},{4,0},{5,1},{6,2},{7,3},{8,12},{9,13},{10,... | collective-permute-start | bytes 6291464 | tf_op jit(solution)/shard_map/ppermute | solution.py:53
  89.1 4.0 %collective-permute-done.11 = f32[32,64,256]{2,1,0:T(8,128)S(1)} collective-permute-done((f32[32,64,256]{2,1,0:T(8,128)}, f32[32,64,256]{2,1,0:T(8,128)S(1)}, u32[]{:S(2)}, u32[]{:S(2)}) %collective-permute-start.11) | collective-permute-done | bytes 2097184 | tf_op jit(solution)/shard_map/ppermute | solution.py:53
  93.1 1.9 %slice_add_fusion.3 = (f32[8,64,256]{2,1,0:T(8,128)S(1)}, f32[8,64,256]{2,1,0:T(8,128)S(1)}, f32[8,64,256]{2,1,0:T(8,128)S(1)}, f32[8,64,256]{2,1,0:T(8,128)S(1)}) fusion(f32[32,64,256]{2,1,0:T(8,128)S(1)} %collective-permute-done.11, f32[32,64,256]{2,1,0:T(8,128)} %get-tuple-element.5), kind=kLoop, calls=%fused_computation.3 | loop fusion | flops 524288 | bytes 6291456 | tf_op jit(solution)/shard_map/add | solution.py:272
  94.9 1.6 %collective-permute-start.17 = (f32[2,4,64,256]{3,2,1,0:T(8,128)S(1)}, f32[2,4,64,256]{3,2,1,0:T(8,128)S(1)}, u32[]{:S(2)}, u32[]{:S(2)}) collective-permute-start(f32[2,4,64,256]{3,2,1,0:T(8,128)S(1)} %bitcast.90), channel_id=1, source_target_pairs={{0,16},{1,17},{2,18},{3,19},{4,20},{5,21},{6,22},{7,23},{8,24},{9,... | collective-permute-start | bytes 1572872 | tf_op jit(solution)/shard_map/ppermute | solution.py:53
  96.5 18.4 %collective-permute-start.12 = (f32[2,4,64,256]{3,2,1,0:T(8,128)S(1)}, f32[2,4,64,256]{3,2,1,0:T(8,128)S(1)}, u32[]{:S(2)}, u32[]{:S(2)}) collective-permute-start(f32[2,4,64,256]{3,2,1,0:T(8,128)S(1)} %bitcast.89), channel_id=1, source_target_pairs={{0,8},{1,9},{2,10},{3,11},{4,12},{5,13},{6,14},{7,15},{8,0},{9,1},... | collective-permute-start | bytes 1572872 | tf_op jit(solution)/shard_map/ppermute | solution.py:53
  115.0 12.5 %collective-permute-start.18 = (f32[4,64,256]{2,1,0:T(8,128)S(1)}, f32[4,64,256]{2,1,0:T(8,128)S(1)}, u32[]{:S(2)}, u32[]{:S(2)}) collective-permute-start(f32[4,64,256]{2,1,0:T(8,128)S(1)} %get-tuple-element.17), channel_id=1, source_target_pairs={{0,8},{1,9},{2,10},{3,11},{4,12},{5,13},{6,14},{7,15},{8,0},{9,1},... | collective-permute-start | bytes 786440 | tf_op jit(solution)/shard_map/ppermute | solution.py:53
  127.6 1.8 %collective-permute-start.13 = (f32[4,64,256]{2,1,0:T(8,128)S(1)}, f32[4,64,256]{2,1,0:T(8,128)S(1)}, u32[]{:S(2)}, u32[]{:S(2)}) collective-permute-start(f32[4,64,256]{2,1,0:T(8,128)S(1)} %get-tuple-element.15), channel_id=1, source_target_pairs={{0,16},{1,17},{2,18},{3,19},{4,20},{5,21},{6,22},{7,23},{8,24},{9,... | collective-permute-start | bytes 786440 | tf_op jit(solution)/shard_map/ppermute | solution.py:53
  129.4 4.4 %collective-permute-done.18 = f32[4,64,256]{2,1,0:T(8,128)S(1)} collective-permute-done((f32[4,64,256]{2,1,0:T(8,128)S(1)}, f32[4,64,256]{2,1,0:T(8,128)S(1)}, u32[]{:S(2)}, u32[]{:S(2)}) %collective-permute-start.18) | collective-permute-done | bytes 262176 | tf_op jit(solution)/shard_map/ppermute | solution.py:53
  133.8 5.7 %collective-permute-start.19 = (f32[64,256]{1,0:T(8,128)S(1)}, f32[64,256]{1,0:T(8,128)S(1)}, u32[]{:S(2)}, u32[]{:S(2)}) collective-permute-start(f32[64,256]{1,0:T(8,128)S(1)} %get-tuple-element.21), channel_id=1, source_target_pairs={{0,1},{1,2},{2,3},{3,0},{4,5},{5,6},{6,7},{7,4},{8,9},{9,10},{10,1... | collective-permute-start | bytes 196616 | tf_op jit(solution)/shard_map/ppermute | solution.py:53
  139.5 1.5 collective-permute-start.20
  141.6 3.3 %collective-permute-start.16 = (f32[64,256]{1,0:T(8,128)S(1)}, f32[64,256]{1,0:T(8,128)S(1)}, u32[]{:S(2)}, u32[]{:S(2)}) collective-permute-start(f32[64,256]{1,0:T(8,128)S(1)} %get-tuple-element.19), channel_id=1, source_target_pairs={{0,3},{1,0},{2,1},{3,2},{4,7},{5,4},{6,5},{7,6},{8,11},{9,8},{10,9... | collective-permute-start | bytes 196616 | tf_op jit(solution)/shard_map/ppermute | solution.py:53
  145.3 4.0 %collective-permute-done.20 = f32[64,256]{1,0:T(8,128)S(1)} collective-permute-done((f32[64,256]{1,0:T(8,128)S(1)}, f32[64,256]{1,0:T(8,128)S(1)}, u32[]{:S(2)}, u32[]{:S(2)}) %collective-permute-start.20) | collective-permute-done | bytes 65568 | tf_op jit(solution)/shard_map/ppermute | solution.py:53
  149.3 1.7 %collective-permute-done.15 = f32[64,256]{1,0:T(8,128)S(1)} collective-permute-done((f32[64,256]{1,0:T(8,128)S(1)}, f32[64,256]{1,0:T(8,128)S(1)}, u32[]{:S(2)}, u32[]{:S(2)}) %collective-permute-start.15) | collective-permute-done | bytes 65568 | tf_op jit(solution)/shard_map/ppermute | solution.py:53
  151.0 1.7 %bitcast_subtract_fusion = (f32[128,256]{1,0:T(8,128)}, f32[128,256]{1,0:T(8,128)}, f32[128,256]{1,0:T(8,128)}) fusion(f32[3,128,256]{2,1,0:T(8,128)} %param.11, f32[64,256]{1,0:T(8,128)S(1)} %fusion.9, f32[64,256]{1,0:T(8,128)S(1)} %fusion.16, f32[128,256]{1,0:T(8,128)S(1)} %copy-done, f32[128,256]{1,0:T(8,128)S(1)} %copy-done.1), kind=kLoop, calls=%fused_computation.19 | loop fusion | flops 425984 | bytes 917504 | tf_op jit(solution)/shard_map/sub | solution.py:280
  (58 shorter events, 7.7 us)
Async XLA Ops:
  1.7 21.8 %collective-permute-start.2 = (bf16[6,64,256]{2,1,0:T(8,128)(2,1)S(1)}, bf16[6,64,256]{2,1,0:T(8,128)(2,1)S(1)}, u32[]{:S(2)}, u32[]{:S(2)}) collective-permute-start(bf16[6,64,256]{2,1,0:T(8,128)(2,1)S(1)} %bitcast.85), channel_id=1, source_target_pairs={{0,3},{1,0},{2,1},{3,2},{4,7},{5,4},{6,5},{7,6},{8,11},{9,8},{10,9... | collective-permute-start | bytes 589832 | tf_op jit(solution)/shard_map/ppermute | solution.py:53
  6.8 16.7 %collective-permute-start.1 = (bf16[6,64,256]{2,1,0:T(8,128)(2,1)S(1)}, bf16[6,64,256]{2,1,0:T(8,128)(2,1)S(1)}, u32[]{:S(2)}, u32[]{:S(2)}) collective-permute-start(bf16[6,64,256]{2,1,0:T(8,128)(2,1)S(1)} %bitcast.86), channel_id=1, source_target_pairs={{0,2},{1,3},{2,0},{3,1},{4,6},{5,7},{6,4},{7,5},{8,10},{9,11},{10,... | collective-permute-start | bytes 589832 | tf_op jit(solution)/shard_map/ppermute | solution.py:53
  6.8 13.6 %collective-permute-start = (bf16[6,64,256]{2,1,0:T(8,128)(2,1)S(1)}, bf16[6,64,256]{2,1,0:T(8,128)(2,1)S(1)}, u32[]{:S(2)}, u32[]{:S(2)}) collective-permute-start(bf16[6,64,256]{2,1,0:T(8,128)(2,1)S(1)} %bitcast.87), channel_id=1, source_target_pairs={{0,1},{1,2},{2,3},{3,0},{4,5},{5,6},{6,7},{7,4},{8,9},{9,10},{10,1... | collective-permute-start | bytes 589832 | tf_op jit(solution)/shard_map/ppermute | solution.py:53
  23.6 10.3 %collective-permute-start.7 = (bf16[12,64,256]{2,1,0:T(8,128)(2,1)S(1)}, bf16[12,64,256]{2,1,0:T(8,128)(2,1)S(1)}, u32[]{:S(2)}, u32[]{:S(2)}) collective-permute-start(bf16[12,64,256]{2,1,0:T(8,128)(2,1)S(1)} %pad_maximum_fusion.1), channel_id=1, source_target_pairs={{0,8},{1,9},{2,10},{3,11},{4,12},{5,13},{6,14},{7,15},{8,0},{9,1},... | collective-permute-start | bytes 1179656 | tf_op jit(solution)/shard_map/ppermute | solution.py:53
  25.2 10.3 %collective-permute-start.3 = (bf16[12,64,256]{2,1,0:T(8,128)(2,1)S(1)}, bf16[12,64,256]{2,1,0:T(8,128)(2,1)S(1)}, u32[]{:S(2)}, u32[]{:S(2)}) collective-permute-start(bf16[12,64,256]{2,1,0:T(8,128)(2,1)S(1)} %pad_maximum_fusion), channel_id=1, source_target_pairs={{0,16},{1,17},{2,18},{3,19},{4,20},{5,21},{6,22},{7,23},{8,24},{9,... | collective-permute-start | bytes 1179656 | tf_op jit(solution)/shard_map/ppermute | solution.py:53
  33.9 18.1 %collective-permute-start.8 = (bf16[24,64,256]{2,1,0:T(8,128)(2,1)S(1)}, bf16[24,64,256]{2,1,0:T(8,128)(2,1)S(1)}, u32[]{:S(2)}, u32[]{:S(2)}) collective-permute-start(bf16[24,64,256]{2,1,0:T(8,128)(2,1)S(1)} %constant_dynamic-update-slice_fusion.5.refs_8_), channel_id=1, source_target_pairs={{0,16},{1,17},{2,18},{3,19},{4,20},{5,21},{6,22},{7,23},{8,24},{9,... | collective-permute-start | bytes 2359304 | tf_op jit(solution)/shard_map/ppermute | solution.py:53
  35.5 17.5 %collective-permute-start.4 = (bf16[24,64,256]{2,1,0:T(8,128)(2,1)S(1)}, bf16[24,64,256]{2,1,0:T(8,128)(2,1)S(1)}, u32[]{:S(2)}, u32[]{:S(2)}) collective-permute-start(bf16[24,64,256]{2,1,0:T(8,128)(2,1)S(1)} %constant_dynamic-update-slice_fusion.refs_4_), channel_id=1, source_target_pairs={{0,8},{1,9},{2,10},{3,11},{4,12},{5,13},{6,14},{7,15},{8,0},{9,1},... | collective-permute-start | bytes 2359304 | tf_op jit(solution)/shard_map/ppermute | solution.py:53
  37.1 16.6 %collective-permute-start.9 = (bf16[24,64,256]{2,1,0:T(8,128)(2,1)S(1)}, bf16[24,64,256]{2,1,0:T(8,128)(2,1)S(1)}, u32[]{:S(2)}, u32[]{:S(2)}) collective-permute-start(bf16[24,64,256]{2,1,0:T(8,128)(2,1)S(1)} %constant_dynamic-update-slice_fusion.5.refs_8_), channel_id=1, source_target_pairs={{0,4},{1,5},{2,6},{3,7},{4,0},{5,1},{6,2},{7,3},{8,12},{9,13},{10,... | collective-permute-start | bytes 2359304 | tf_op jit(solution)/shard_map/ppermute | solution.py:53
  37.1 16.6 %collective-permute-start.5 = (bf16[24,64,256]{2,1,0:T(8,128)(2,1)S(1)}, bf16[24,64,256]{2,1,0:T(8,128)(2,1)S(1)}, u32[]{:S(2)}, u32[]{:S(2)}) collective-permute-start(bf16[24,64,256]{2,1,0:T(8,128)(2,1)S(1)} %constant_dynamic-update-slice_fusion.refs_4_), channel_id=1, source_target_pairs={{0,4},{1,5},{2,6},{3,7},{4,0},{5,1},{6,2},{7,3},{8,12},{9,13},{10,... | collective-permute-start | bytes 2359304 | tf_op jit(solution)/shard_map/ppermute | solution.py:53
  52.0 2.3 %collective-permute-start.10 = (bf16[24,64,256]{2,1,0:T(8,128)(2,1)S(1)}, bf16[24,64,256]{2,1,0:T(8,128)(2,1)S(1)}, u32[]{:S(2)}, u32[]{:S(2)}) collective-permute-start(bf16[24,64,256]{2,1,0:T(8,128)(2,1)S(1)} %collective-permute-done.8.refs_9_), channel_id=1, source_target_pairs={{0,4},{1,5},{2,6},{3,7},{4,0},{5,1},{6,2},{7,3},{8,12},{9,13},{10,... | collective-permute-start | bytes 2359304 | tf_op jit(solution)/shard_map/ppermute | solution.py:53
  53.0 2.4 %collective-permute-start.6 = (bf16[24,64,256]{2,1,0:T(8,128)(2,1)S(1)}, bf16[24,64,256]{2,1,0:T(8,128)(2,1)S(1)}, u32[]{:S(2)}, u32[]{:S(2)}) collective-permute-start(bf16[24,64,256]{2,1,0:T(8,128)(2,1)S(1)} %collective-permute-done.4.refs_5_), channel_id=1, source_target_pairs={{0,4},{1,5},{2,6},{3,7},{4,0},{5,1},{6,2},{7,3},{8,12},{9,13},{10,... | collective-permute-start | bytes 2359304 | tf_op jit(solution)/shard_map/ppermute | solution.py:53
  74.3 18.8 %collective-permute-start.11 = (f32[32,64,256]{2,1,0:T(8,128)}, f32[32,64,256]{2,1,0:T(8,128)S(1)}, u32[]{:S(2)}, u32[]{:S(2)}) collective-permute-start(f32[32,64,256]{2,1,0:T(8,128)} %get-tuple-element.6), channel_id=1, source_target_pairs={{0,4},{1,5},{2,6},{3,7},{4,0},{5,1},{6,2},{7,3},{8,12},{9,13},{10,... | collective-permute-start | bytes 6291464 | tf_op jit(solution)/shard_map/ppermute | solution.py:53
  94.9 20.0 %collective-permute-start.17 = (f32[2,4,64,256]{3,2,1,0:T(8,128)S(1)}, f32[2,4,64,256]{3,2,1,0:T(8,128)S(1)}, u32[]{:S(2)}, u32[]{:S(2)}) collective-permute-start(f32[2,4,64,256]{3,2,1,0:T(8,128)S(1)} %bitcast.90), channel_id=1, source_target_pairs={{0,16},{1,17},{2,18},{3,19},{4,20},{5,21},{6,22},{7,23},{8,24},{9,... | collective-permute-start | bytes 1572872 | tf_op jit(solution)/shard_map/ppermute | solution.py:53
  96.5 31.0 %collective-permute-start.12 = (f32[2,4,64,256]{3,2,1,0:T(8,128)S(1)}, f32[2,4,64,256]{3,2,1,0:T(8,128)S(1)}, u32[]{:S(2)}, u32[]{:S(2)}) collective-permute-start(f32[2,4,64,256]{3,2,1,0:T(8,128)S(1)} %bitcast.89), channel_id=1, source_target_pairs={{0,8},{1,9},{2,10},{3,11},{4,12},{5,13},{6,14},{7,15},{8,0},{9,1},... | collective-permute-start | bytes 1572872 | tf_op jit(solution)/shard_map/ppermute | solution.py:53
  115.0 36.0 %copy-start = (f32[128,256]{1,0:T(8,128)S(1)}, f32[128,256]{1,0:T(8,128)}, u32[]{:S(2)}) copy-start(f32[128,256]{1,0:T(8,128)} %param.12) | copy-start | bytes 393220
  115.0 36.0 %copy-start.1 = (f32[128,256]{1,0:T(8,128)S(1)}, f32[128,256]{1,0:T(8,128)}, u32[]{:S(2)}) copy-start(f32[128,256]{1,0:T(8,128)} %param.13) | copy-start | bytes 393220
  115.0 18.8 %collective-permute-start.18 = (f32[4,64,256]{2,1,0:T(8,128)S(1)}, f32[4,64,256]{2,1,0:T(8,128)S(1)}, u32[]{:S(2)}, u32[]{:S(2)}) collective-permute-start(f32[4,64,256]{2,1,0:T(8,128)S(1)} %get-tuple-element.17), channel_id=1, source_target_pairs={{0,8},{1,9},{2,10},{3,11},{4,12},{5,13},{6,14},{7,15},{8,0},{9,1},... | collective-permute-start | bytes 786440 | tf_op jit(solution)/shard_map/ppermute | solution.py:53
  127.6 13.4 %collective-permute-start.13 = (f32[4,64,256]{2,1,0:T(8,128)S(1)}, f32[4,64,256]{2,1,0:T(8,128)S(1)}, u32[]{:S(2)}, u32[]{:S(2)}) collective-permute-start(f32[4,64,256]{2,1,0:T(8,128)S(1)} %get-tuple-element.15), channel_id=1, source_target_pairs={{0,16},{1,17},{2,18},{3,19},{4,20},{5,21},{6,22},{7,23},{8,24},{9,... | collective-permute-start | bytes 786440 | tf_op jit(solution)/shard_map/ppermute | solution.py:53
  133.8 11.1 %collective-permute-start.19 = (f32[64,256]{1,0:T(8,128)S(1)}, f32[64,256]{1,0:T(8,128)S(1)}, u32[]{:S(2)}, u32[]{:S(2)}) collective-permute-start(f32[64,256]{1,0:T(8,128)S(1)} %get-tuple-element.21), channel_id=1, source_target_pairs={{0,1},{1,2},{2,3},{3,0},{4,5},{5,6},{6,7},{7,4},{8,9},{9,10},{10,1... | collective-permute-start | bytes 196616 | tf_op jit(solution)/shard_map/ppermute | solution.py:53
  139.5 5.8 %collective-permute-start.21 = (f32[64,256]{1,0:T(8,128)S(1)}, f32[64,256]{1,0:T(8,128)S(1)}, u32[]{:S(2)}, u32[]{:S(2)}) collective-permute-start(f32[64,256]{1,0:T(8,128)S(1)} %get-tuple-element.22), channel_id=1, source_target_pairs={{0,3},{1,0},{2,1},{3,2},{4,7},{5,4},{6,5},{7,6},{8,11},{9,8},{10,9... | collective-permute-start | bytes 196616 | tf_op jit(solution)/shard_map/ppermute | solution.py:53
  139.5 9.8 %collective-permute-start.20 = (f32[64,256]{1,0:T(8,128)S(1)}, f32[64,256]{1,0:T(8,128)S(1)}, u32[]{:S(2)}, u32[]{:S(2)}) collective-permute-start(f32[64,256]{1,0:T(8,128)S(1)} %get-tuple-element.23), channel_id=1, source_target_pairs={{0,2},{1,3},{2,0},{3,1},{4,6},{5,7},{6,4},{7,5},{8,10},{9,11},{10,... | collective-permute-start | bytes 196616 | tf_op jit(solution)/shard_map/ppermute | solution.py:53
  141.0 8.3 %collective-permute-start.14 = (f32[64,256]{1,0:T(8,128)S(1)}, f32[64,256]{1,0:T(8,128)S(1)}, u32[]{:S(2)}, u32[]{:S(2)}) collective-permute-start(f32[64,256]{1,0:T(8,128)S(1)} %get-tuple-element.18), channel_id=1, source_target_pairs={{0,1},{1,2},{2,3},{3,0},{4,5},{5,6},{6,7},{7,4},{8,9},{9,10},{10,1... | collective-permute-start | bytes 196616 | tf_op jit(solution)/shard_map/ppermute | solution.py:53
  141.6 7.7 %collective-permute-start.16 = (f32[64,256]{1,0:T(8,128)S(1)}, f32[64,256]{1,0:T(8,128)S(1)}, u32[]{:S(2)}, u32[]{:S(2)}) collective-permute-start(f32[64,256]{1,0:T(8,128)S(1)} %get-tuple-element.19), channel_id=1, source_target_pairs={{0,3},{1,0},{2,1},{3,2},{4,7},{5,4},{6,5},{7,6},{8,11},{9,8},{10,9... | collective-permute-start | bytes 196616 | tf_op jit(solution)/shard_map/ppermute | solution.py:53
  144.9 6.1 %collective-permute-start.15 = (f32[64,256]{1,0:T(8,128)S(1)}, f32[64,256]{1,0:T(8,128)S(1)}, u32[]{:S(2)}, u32[]{:S(2)}) collective-permute-start(f32[64,256]{1,0:T(8,128)S(1)} %get-tuple-element.20), channel_id=1, source_target_pairs={{0,2},{1,3},{2,0},{3,1},{4,6},{5,7},{6,4},{7,5},{8,10},{9,11},{10,... | collective-permute-start | bytes 196616 | tf_op jit(solution)/shard_map/ppermute | solution.py:53
  (8 other events, 53.0 us)

commit v3 on v2

v3 whole, which is shorter than its diff:
```python
import functools

import jax
import jax.numpy as jnp
from jax import lax
from jax.experimental import pallas as pl
from jax.experimental.pallas import tpu as pltpu
from jax.sharding import PartitionSpec as P

AXES = ("blk", "grp")
CORES = 2
BUFFERS = 4
AHEAD = 2
TILE_J = 4
QUARTERS = 4


def mesh_dims(blk, grp):
    chips = blk // CORES
    inner = 1
    for width in range(1, chips + 1):
        if chips % width == 0 and width * width <= chips:
            inner = width
    return {"outer": chips // inner, "inner": inner, "core": CORES, "line": grp}


def split_index(index, dims):
    line = lax.rem(index, dims["line"])
    rest = lax.div(index, dims["line"])
    core = lax.rem(rest, dims["core"])
    rest = lax.div(rest, dims["core"])
    return {
        "outer": lax.div(rest, dims["inner"]),
        "inner": lax.rem(rest, dims["inner"]),
        "core": core,
        "line": line,
    }


def shift(values, dims, name, step):
    strides = {
        "line": 1,
        "core": dims["line"],
        "inner": dims["line"] * dims["core"],
        "outer": dims["line"] * dims["core"] * dims["inner"],
    }
    total = strides["outer"] * dims["outer"]
    stride, size = strides[name], dims[name]
    perm = []
    for source in range(total):
        at = source // stride % size
        perm.append((source, source + ((at + step) % size - at) * stride))
    return lax.ppermute(values, AXES, perm)


ORDERS = (("outer", "inner"), ("inner", "outer"))
SIDE_ORDER = ("outer", "inner", "line")
SIDE_ROWS = 16


def gather_rows(shard, dims):
    cut = shard.shape[0] // 2
    side = shard[:, :SIDE_ROWS]
    main = shard[:, SIDE_ROWS:]
    line = [main] + [shift(main, dims, "line", k) for k in range(1, dims["line"])]
    for name in SIDE_ORDER[:2]:
        side = jnp.concatenate([side] + [shift(side, dims, name, k) for k in range(1, dims[name])])
    sides = [side] + [shift(side, dims, SIDE_ORDER[2], k) for k in range(1, dims[SIDE_ORDER[2]])]
    mains = []
    for part, (first, second) in zip((slice(0, cut), slice(cut, None)), ORDERS):
        own = jnp.concatenate([piece[part] for piece in line])
        own = jnp.concatenate([own] + [shift(own, dims, first, k) for k in range(1, dims[first])])
        mains.append([own] + [shift(own, dims, second, k) for k in range(1, dims[second])])
    mains = [pieces + [shift(piece, dims, "core", 1) for piece in pieces] for pieces in mains]
    sides = sides + [shift(piece, dims, "core", 1) for piece in sides]
    return mains[0] + mains[1], sides


def reduce_along(kept, got, dims, names):
    for name in names:
        sums = [functools.reduce(jnp.add, [g[k] for g in got], kept[k]) for k in range(dims[name])]
        kept = sums[0]
        got = [shift(sums[k], dims, name, k) for k in range(1, dims[name])]
    return functools.reduce(jnp.add, got, kept)


def away_from(there, here, dims):
    return {name: lax.rem(there[name] - here[name] + dims[name], dims[name]) for name in dims}


def main_spot(away, late, dims):
    second = jnp.where(late, away["outer"], away["inner"])
    first = jnp.where(late, away["inner"], away["outer"])
    size_first = jnp.where(late, dims["inner"], dims["outer"])
    size_second = jnp.where(late, dims["outer"], dims["inner"])
    return (second * size_first + first) * dims["line"] + away["line"], size_first * size_second


def side_spot(away, dims):
    spot = away["core"]
    for name in SIDE_ORDER[::-1]:
        spot = spot * dims[name] + away[name]
    return spot


def slots_kernel(dims, local_blocks, main_count, piece_count, *refs):
    coords_ref, count_ref, owner_ref, blocks_ref = refs[:4]
    pieces = refs[4 : 4 + piece_count]
    (
        mine_main_ref,
        other_main_ref,
        mine_side_ref,
        other_side_ref,
        main_ref,
        side_ref,
        grad_main_ref,
        grad_side_ref,
        blocks_buf,
        weight_ref,
        pair_ref,
        model_ref,
        total_ref,
        block_sems,
        piece_sems,
        out_sems,
    ) = refs[4 + piece_count :]
    edge, rank = total_ref.shape
    tiles = pair_ref.shape[0]
    width = TILE_J * edge
    quarter = edge * edge // QUARTERS
    count = count_ref[0]
    here = split_index(lax.axis_index("blk") * dims["line"] + lax.axis_index("grp"), dims)
    columns = dims["core"] * dims["outer"] * dims["inner"] * dims["line"]
    cut = 3 * local_blocks // 2
    half_blocks = local_blocks // 2

    def row_places(mode, slot):
        pos = owner_ref[mode, coords_ref[mode, slot]]
        there = split_index(lax.div(pos, local_blocks), dims)
        away = away_from(here, there, dims)
        block = mode * local_blocks + lax.rem(pos, local_blocks)
        late = block >= cut
        spot, size = main_spot(away, late, dims)
        spot = away["core"] * size * dims["line"] + spot
        blocks_of = jnp.where(late, 3 * local_blocks - cut, cut)
        main = jnp.where(late, columns * cut + block - cut, block) + spot * blocks_of
        side = side_spot(away, dims) * (3 * local_blocks) + block
        return main, side

    def grad_places(slot):
        pos = owner_ref[0, coords_ref[0, slot]]
        there = split_index(lax.div(pos, local_blocks), dims)
        away = away_from(there, here, dims)
        local = lax.rem(pos, local_blocks)
        late = local >= half_blocks
        spot, size = main_spot(away, late, dims)
        half = jnp.where(late, 1, 0)
        spot = (away["core"] * 2 + half) * size * dims["line"] + spot
        main = spot * half_blocks + jnp.where(late, local - half_blocks, local)
        side = side_spot(away, dims) * local_blocks + local
        return main, side

    def rows_of(places):
        main, side = places
        return jnp.concatenate([side_ref[side], main_ref[main]], axis=0)

    def row_of(places, j):
        main, side = places
        if j < SIDE_ROWS:
            return side_ref[side, pl.ds(j, 1), :]
        return main_ref[main, pl.ds(j - SIDE_ROWS, 1), :]

    def block_copy(slot):
        at = lax.rem(slot, BUFFERS)
        return pltpu.make_async_copy(blocks_ref.at[slot], blocks_buf.at[at], block_sems.at[at])

    def start(slot):
        @pl.when(slot < count)
        def _():
            block_copy(slot).start()

    fills = []
    for table, group in ((main_ref, range(main_count)), (side_ref, range(main_count, piece_count))):
        offset = 0
        for index in group:
            size = pieces[index].shape[0]
            fills.append(
                pltpu.make_async_copy(
                    pieces[index], table.at[pl.ds(offset, size)], piece_sems.at[index]
                )
            )
            offset += size
    for fill in fills:
        fill.start()
    for slot in range(AHEAD):
        start(slot)
    grad_main_ref[...] = jnp.zeros_like(grad_main_ref)
    grad_side_ref[...] = jnp.zeros_like(grad_side_ref)
    weight_ref[...] = jnp.zeros_like(weight_ref)
    pair_ref[tiles - 1] = jnp.zeros(pair_ref.shape[1:], pair_ref.dtype)
    model_ref[tiles - 1] = jnp.zeros(model_ref.shape[1:], model_ref.dtype)
    total_ref[...] = jnp.zeros_like(total_ref)
    for fill in fills:
        fill.wait()

    def finish(tile, at, total):
        model = model_ref[tile].T
        for q in range(QUARTERS):
            begin = q * quarter + tile * width
            twice = blocks_buf[at, :, begin : begin + width].astype(jnp.float32) * 2.0
            resid = ((jnp.tanh(model[q * edge : (q + 1) * edge]) + 1.0) - twice).astype(jnp.bfloat16)
            total = total + jnp.dot(
                resid,
                pair_ref[tile, :, q * rank : (q + 1) * rank],
                preferred_element_type=jnp.float32,
            )
        return total

    def add_total(slot, total):
        main, side = grad_places(slot)
        half = 0.5 * total
        grad_side_ref[side] += half[:SIDE_ROWS]
        grad_main_ref[main] += half[SIDE_ROWS:]

    lanes = lax.broadcasted_iota(jnp.int32, (rank, 2 * edge), 1)

    def step(slot, carry):
        start(slot + AHEAD)
        block_copy(slot).wait()
        at = lax.rem(slot, BUFFERS)
        before = jnp.maximum(slot - 1, 0)
        at_before = lax.rem(before, BUFFERS)
        places_b = row_places(1, slot)
        rows_a = rows_of(row_places(0, slot)).astype(jnp.float32) * 0.5
        twice_a = jnp.concatenate([rows_a, rows_a], axis=0).T
        for q in range(QUARTERS):
            keep = (lanes < edge) if q % 2 == 0 else (lanes >= edge)
            lane = q // 2 * 2 * edge
            weight_ref[q * rank : (q + 1) * rank, lane : lane + 2 * edge] = jnp.where(
                keep, twice_a, 0.0
            ).astype(jnp.bfloat16)
        rows_c = rows_of(row_places(2, slot))
        total_before = total_ref[...]
        total = jnp.zeros((edge, rank), jnp.float32)
        for tile in range(tiles):
            for q in range(QUARTERS):
                for j in range(TILE_J):
                    row = row_of(places_b, q * (edge // QUARTERS) + tile * TILE_J + j)
                    pair_ref[tile, j * edge : (j + 1) * edge, q * rank : (q + 1) * rank] = (
                        row * rows_c
                    )
            model_ref[tile] = jnp.dot(
                pair_ref[tile], weight_ref[...], preferred_element_type=jnp.float32
            )
            if tile == 0:
                total_before = finish(tiles - 1, at_before, total_before)
            else:
                total = finish(tile - 1, at, total)
        add_total(before, total_before)
        total_ref[...] = total
        return carry

    lax.fori_loop(0, count, step, 0)
    last = count - 1
    add_total(last, finish(tiles - 1, lax.rem(last, BUFFERS), total_ref[...]))
    drains = []
    for index, (grad, out, part) in enumerate(
        (
            (grad_main_ref, other_main_ref, 1),
            (grad_side_ref, other_side_ref, 1),
            (grad_main_ref, mine_main_ref, 0),
            (grad_side_ref, mine_side_ref, 0),
        )
    ):
        half = out.shape[0]
        drains.append(
            pltpu.make_async_copy(grad.at[pl.ds(part * half, half)], out, out_sems.at[index])
        )
    for drain in drains:
        drain.start()
    for drain in drains:
        drain.wait()


def per_device(tensor_blocks, block_coords, block_count, row_owner, factors, moment1, moment2):
    slot_count, edge, width = tensor_blocks.shape
    rank = factors.shape[2]
    local_blocks = moment1.shape[0] // edge
    row_blocks = row_owner.shape[1]
    dims = mesh_dims(lax.axis_size("blk"), lax.axis_size("grp"))
    shard = factors.astype(jnp.bfloat16).reshape(3 * local_blocks, edge, rank)
    mains, sides = gather_rows(shard, dims)
    pieces = mains + sides
    smem = pl.BlockSpec(memory_space=pltpu.SMEM)
    hbm = pl.BlockSpec(memory_space=pl.ANY)
    tiles = edge // (QUARTERS * TILE_J)
    main_rows = edge - SIDE_ROWS
    out_main = jax.ShapeDtypeStruct((row_blocks // 2, main_rows, rank), jnp.float32)
    out_side = jax.ShapeDtypeStruct((row_blocks // 2, SIDE_ROWS, rank), jnp.float32)
    mine_main, other_main, mine_side, other_side = pl.pallas_call(
        functools.partial(slots_kernel, dims, local_blocks, len(mains), len(pieces)),
        out_shape=(out_main, out_main, out_side, out_side),
        in_specs=[smem, smem, smem, hbm] + [hbm] * len(pieces),
        out_specs=(hbm, hbm, hbm, hbm),
        scratch_shapes=[
            pltpu.VMEM((3 * row_blocks, main_rows, rank), jnp.bfloat16),
            pltpu.VMEM((3 * row_blocks, SIDE_ROWS, rank), jnp.bfloat16),
            pltpu.VMEM((row_blocks, main_rows, rank), jnp.float32),
            pltpu.VMEM((row_blocks, SIDE_ROWS, rank), jnp.float32),
            pltpu.VMEM((BUFFERS, edge, width), jnp.bfloat16),
            pltpu.VMEM((QUARTERS * rank, QUARTERS * edge), jnp.bfloat16),
            pltpu.VMEM((tiles, TILE_J * edge, QUARTERS * rank), jnp.bfloat16),
            pltpu.VMEM((tiles, TILE_J * edge, QUARTERS * edge), jnp.float32),
            pltpu.VMEM((edge, rank), jnp.float32),
            pltpu.SemaphoreType.DMA((BUFFERS,)),
            pltpu.SemaphoreType.DMA((len(pieces),)),
            pltpu.SemaphoreType.DMA((4,)),
        ],
        compiler_params=pltpu.CompilerParams(vmem_limit_bytes=56 * 1024 * 1024),
        cost_estimate=pl.CostEstimate(
            flops=4 * slot_count * edge * width * rank,
            bytes_accessed=2 * slot_count * edge * width,
            transcendentals=slot_count * edge * width,
        ),
    )(block_coords, block_count, row_owner, tensor_blocks, *pieces)
    arrived_main = shift(other_main, dims, "core", 1)
    arrived_side = shift(other_side, dims, "core", 1)
    side_shape = tuple(dims[name] for name in SIDE_ORDER[::-1]) + (local_blocks, SIDE_ROWS, rank)
    side_grad = reduce_along(
        mine_side.reshape(side_shape), [arrived_side.reshape(side_shape)], dims, SIDE_ORDER[::-1]
    )
    main_grads = []
    for half, (first, second) in enumerate(ORDERS):
        shape = (2, dims[second], dims[first], dims["line"], local_blocks // 2, main_rows, rank)
        main_grads.append(
            reduce_along(
                mine_main.reshape(shape)[half],
                [arrived_main.reshape(shape)[half]],
                dims,
                (second, first, "line"),
            )
        )
    grad = jnp.concatenate([side_grad, jnp.concatenate(main_grads)], axis=1)
    grad = grad.reshape(local_blocks * edge, rank)
    new_moment1 = 0.9 * moment1 + 0.1 * grad
    new_moment2 = 0.999 * moment2 + 0.001 * grad * grad
    new_factor = factors[0] - 0.02 * (new_moment1 / (1.0 - 0.9**8)) / (
        jnp.sqrt(new_moment2 / (1.0 - 0.999**8)) + 1e-08
    )
    return (new_factor, new_moment1, new_moment2)


def solution(mesh):
    return jax.shard_map(
        per_device,
        mesh=mesh,
        in_specs=(
            P(AXES, None, None),
            P(None, AXES),
            P(AXES),
            P(),
            P(None, AXES, None),
            P(AXES, None),
            P(AXES, None),
        ),
        out_specs=(P(AXES, None), P(AXES, None), P(AXES, None)),
        check_vma=False,
    )
```

time: 154 us -> 171 us (1.11)
  Pallas kernels: 17.9 us -> 51.5 us
  starting transfers between devices: 73.4 us -> 40 us
  waiting for transfers between devices: 53.9 us -> 71 us
    pallas_call x1, Pallas kernels: 17.9 us -> 51.5 us  [per_device(): pl.pallas_call(functools.partial(slots_kernel, dims, local_blocks, len(ma...]
    ppermute x22 -> x37, starting transfers between devices: 73.4 us -> 40 us  [shift(): return lax.ppermute(values, AXES, perm)]
    ppermute x22 -> x37, waiting for transfers between devices: 53.9 us -> 71 us  [shift(): return lax.ppermute(values, AXES, perm)]
  transfers between devices with their start and end apart: 22 -> 37, of which waited for: 11 -> 19; matrix products, arithmetic and copies ran while one was open for 0% -> 1% of each run, Pallas kernels for 0% -> 0%
where the time goes in v3:
time: 171 us
  waiting for transfers between devices  71 us (42%)
  Pallas kernels  51.5 us (30%)
  starting transfers between devices  40 us (23%)
  other arithmetic  4.48 us (3%)
  local copies, waits for them, and re-layouts  2.21 us (1%)
    ppermute x37, waiting for transfers between devices, shift(): return lax.ppermute(values, AXES, perm)  71 us
    pallas_call x1, Pallas kernels, per_device(): pl.pallas_call(functools.partial(slots_kernel, dims, local_blocks, len(ma...  51.5 us
    ppermute x37, starting transfers between devices, shift(): return lax.ppermute(values, AXES, perm)  40 us
  transfers between devices with their start and end apart: 37, of which 19 were waited for; matrix products, arithmetic and copies ran while one was open for 1% of the time, Pallas kernels for 0%

profile of v3, /device:TPU:0, one launch (start us, length us, event | category | flops | bytes accessed | tf_op | source)
XLA Modules:
  0.0 170.9 jit_solution(7501039540414090839)
XLA Ops:
  1.7 5.1 %collective-permute-start.2 = (bf16[6,48,256]{2,1,0:T(8,128)(2,1)S(1)}, bf16[6,48,256]{2,1,0:T(8,128)(2,1)S(1)}, u32[]{:S(2)}, u32[]{:S(2)}) collective-permute-start(bf16[6,48,256]{2,1,0:T(8,128)(2,1)S(1)} %slice.351), channel_id=1, source_target_pairs={{0,3},{1,0},{2,1},{3,2},{4,7},{5,4},{6,5},{7,6},{8,11},{9,8},{10,9... | collective-permute-start | bytes 442376 | tf_op jit(solution)/shard_map/ppermute | solution.py:53
  7.8 9.4 %collective-permute-done = bf16[6,48,256]{2,1,0:T(8,128)(2,1)S(1)} collective-permute-done((bf16[6,48,256]{2,1,0:T(8,128)(2,1)S(1)}, bf16[6,48,256]{2,1,0:T(8,128)(2,1)S(1)}, u32[]{:S(2)}, u32[]{:S(2)}) %collective-permute-start) | collective-permute-done | bytes 147488 | tf_op jit(solution)/shard_map/ppermute | solution.py:53
  17.2 2.0 %collective-permute-done.1 = bf16[6,48,256]{2,1,0:T(8,128)(2,1)S(1)} collective-permute-done((bf16[6,48,256]{2,1,0:T(8,128)(2,1)S(1)}, bf16[6,48,256]{2,1,0:T(8,128)(2,1)S(1)}, u32[]{:S(2)}, u32[]{:S(2)}) %collective-permute-start.1) | collective-permute-done | bytes 147488 | tf_op jit(solution)/shard_map/ppermute | solution.py:53
  21.0 1.6 collective-permute-start.3
  23.1 7.0 %collective-permute-done.11 = bf16[6,16,256]{2,1,0:T(8,128)(2,1)S(1)} collective-permute-done((bf16[6,16,256]{2,1,0:T(8,128)(2,1)S(1)}, bf16[6,16,256]{2,1,0:T(8,128)(2,1)S(1)}, u32[]{:S(2)}, u32[]{:S(2)}) %collective-permute-start.11) | collective-permute-done | bytes 49184 | tf_op jit(solution)/shard_map/ppermute | solution.py:53
  30.8 1.6 collective-permute-start.8
  33.9 1.9 %collective-permute-done.12 = bf16[12,16,256]{2,1,0:T(8,128)(2,1)S(1)} collective-permute-done((bf16[12,16,256]{2,1,0:T(8,128)(2,1)S(1)}, bf16[12,16,256]{2,1,0:T(8,128)(2,1)S(1)}, u32[]{:S(2)}, u32[]{:S(2)}) %collective-permute-start.12) | collective-permute-done | bytes 98336 | tf_op jit(solution)/shard_map/ppermute | solution.py:53
  36.5 2.4 %collective-permute-start.14 = (bf16[24,16,256]{2,1,0:T(8,128)(2,1)S(1)}, bf16[24,16,256]{2,1,0:T(8,128)(2,1)S(1)}, u32[]{:S(2)}, u32[]{:S(2)}) collective-permute-start(bf16[24,16,256]{2,1,0:T(8,128)(2,1)S(1)} %pad_maximum_fusion.2.refs_12_), channel_id=1, source_target_pairs={{0,2},{1,3},{2,0},{3,1},{4,6},{5,7},{6,4},{7,5},{8,10},{9,11},{10,... | collective-permute-start | bytes 589832 | tf_op jit(solution)/shard_map/ppermute | solution.py:53
  38.8 1.9 %collective-permute-start.13 = (bf16[24,16,256]{2,1,0:T(8,128)(2,1)S(1)}, bf16[24,16,256]{2,1,0:T(8,128)(2,1)S(1)}, u32[]{:S(2)}, u32[]{:S(2)}) collective-permute-start(bf16[24,16,256]{2,1,0:T(8,128)(2,1)S(1)} %pad_maximum_fusion.2.refs_12_), channel_id=1, source_target_pairs={{0,1},{1,2},{2,3},{3,0},{4,5},{5,6},{6,7},{7,4},{8,9},{9,10},{10,1... | collective-permute-start | bytes 589832 | tf_op jit(solution)/shard_map/ppermute | solution.py:53
  40.8 2.5 %collective-permute-done.15.refs_15_ = bf16[24,16,256]{2,1,0:T(8,128)(2,1)S(1)} collective-permute-done((bf16[24,16,256]{2,1,0:T(8,128)(2,1)S(1)}, bf16[24,16,256]{2,1,0:T(8,128)(2,1)S(1)}, u32[]{:S(2)}, u32[]{:S(2)}) %collective-permute-start.15) | collective-permute-done | bytes 196640 | tf_op jit(solution)/shard_map/ppermute | solution.py:53
  43.3 13.6 %collective-permute-done.14.refs_14_ = bf16[24,16,256]{2,1,0:T(8,128)(2,1)S(1)} collective-permute-done((bf16[24,16,256]{2,1,0:T(8,128)(2,1)S(1)}, bf16[24,16,256]{2,1,0:T(8,128)(2,1)S(1)}, u32[]{:S(2)}, u32[]{:S(2)}) %collective-permute-start.14) | collective-permute-done | bytes 196640 | tf_op jit(solution)/shard_map/ppermute | solution.py:53
  58.0 3.7 %collective-permute-done.18.refs_18_ = bf16[24,16,256]{2,1,0:T(8,128)(2,1)S(1)} collective-permute-done((bf16[24,16,256]{2,1,0:T(8,128)(2,1)S(1)}, bf16[24,16,256]{2,1,0:T(8,128)(2,1)S(1)}, u32[]{:S(2)}, u32[]{:S(2)}) %collective-permute-start.18) | collective-permute-done | bytes 196640 | tf_op jit(solution)/shard_map/ppermute | solution.py:53
  65.3 51.5 %shard_map.94 = (f32[32,48,256]{2,1,0:T(8,128)}, f32[32,48,256]{2,1,0:T(8,128)}, f32[32,16,256]{2,1,0:T(8,128)}, f32[32,16,256]{2,1,0:T(8,128)}) custom-call(s32[3,36]{1,0:T(4,128)} %refs_0_.1, s32[1]{0:T(128)S(6)} %copy.26.refs_1_, s32[3,64]{1,0:T(4,128)} %refs_2_.1, bf16[36,64,4096]{2,1,0:T(8,128)(2,1)} %refs_3_.1, bf16[24,48,256]{2,1,0:T(8,128)(2,1)} %copy-done.4, ...), custom_call_target="tpu_custom_call" | custom-call | flops 9663676416 | bytes 18874368 | tf_op jit(solution)/shard_map/pallas_call | solution.py:300
  117.4 3.9 %collective-permute-done.20 = f32[32,16,256]{2,1,0:T(8,128)S(1)} collective-permute-done((f32[32,16,256]{2,1,0:T(8,128)}, f32[32,16,256]{2,1,0:T(8,128)S(1)}, u32[]{:S(2)}, u32[]{:S(2)}) %collective-permute-start.20) | collective-permute-done | bytes 524320 | tf_op jit(solution)/shard_map/ppermute | solution.py:53
  122.6 2.0 %collective-permute-start.21 = (f32[2,2,2,16,256]{4,3,2,1,0:T(8,128)S(1)}, f32[2,2,2,16,256]{4,3,2,1,0:T(8,128)S(1)}, u32[]{:S(2)}, u32[]{:S(2)}) collective-permute-start(f32[2,2,2,16,256]{4,3,2,1,0:T(8,128)S(1)} %bitcast.138), channel_id=1, source_target_pairs={{0,1},{1,2},{2,3},{3,0},{4,5},{5,6},{6,7},{7,4},{8,9},{9,10},{10,1... | collective-permute-start | bytes 393224 | tf_op jit(solution)/shard_map/ppermute | solution.py:53
  124.6 3.7 %collective-permute-start.22 = (f32[2,2,2,16,256]{4,3,2,1,0:T(8,128)S(1)}, f32[2,2,2,16,256]{4,3,2,1,0:T(8,128)S(1)}, u32[]{:S(2)}, u32[]{:S(2)}) collective-permute-start(f32[2,2,2,16,256]{4,3,2,1,0:T(8,128)S(1)} %bitcast.137), channel_id=1, source_target_pairs={{0,2},{1,3},{2,0},{3,1},{4,6},{5,7},{6,4},{7,5},{8,10},{9,11},{10,... | collective-permute-start | bytes 393224 | tf_op jit(solution)/shard_map/ppermute | solution.py:53
  128.3 6.6 %collective-permute-done.21 = f32[2,2,2,16,256]{4,3,2,1,0:T(8,128)S(1)} collective-permute-done((f32[2,2,2,16,256]{4,3,2,1,0:T(8,128)S(1)}, f32[2,2,2,16,256]{4,3,2,1,0:T(8,128)S(1)}, u32[]{:S(2)}, u32[]{:S(2)}) %collective-permute-start.21) | collective-permute-done | bytes 131104 | tf_op jit(solution)/shard_map/ppermute | solution.py:53
  134.9 3.5 %collective-permute-done.22 = f32[2,2,2,16,256]{4,3,2,1,0:T(8,128)S(1)} collective-permute-done((f32[2,2,2,16,256]{4,3,2,1,0:T(8,128)S(1)}, f32[2,2,2,16,256]{4,3,2,1,0:T(8,128)S(1)}, u32[]{:S(2)}, u32[]{:S(2)}) %collective-permute-start.22) | collective-permute-done | bytes 131104 | tf_op jit(solution)/shard_map/ppermute | solution.py:53
  139.3 3.6 %collective-permute-done.24 = f32[2,2,16,256]{3,2,1,0:T(8,128)S(1)} collective-permute-done((f32[2,2,16,256]{3,2,1,0:T(8,128)S(1)}, f32[2,2,16,256]{3,2,1,0:T(8,128)S(1)}, u32[]{:S(2)}, u32[]{:S(2)}) %collective-permute-start.24) | collective-permute-done | bytes 65568 | tf_op jit(solution)/shard_map/ppermute | solution.py:53
  143.3 7.4 %collective-permute-done.25 = f32[2,16,256]{2,1,0:T(8,128)S(1)} collective-permute-done((f32[2,16,256]{2,1,0:T(8,128)S(1)}, f32[2,16,256]{2,1,0:T(8,128)S(1)}, u32[]{:S(2)}, u32[]{:S(2)}) %collective-permute-start.25) | collective-permute-done | bytes 32800 | tf_op jit(solution)/shard_map/ppermute | solution.py:53
  152.5 2.8 %collective-permute-start.28 = (f32[4,1,48,256]{3,2,1,0:T(8,128)S(1)}, f32[4,1,48,256]{3,2,1,0:T(8,128)S(1)}, u32[]{:S(2)}, u32[]{:S(2)}) collective-permute-start(f32[4,1,48,256]{3,2,1,0:T(8,128)S(1)} %get-tuple-element.23), channel_id=1, source_target_pairs={{0,16},{1,17},{2,18},{3,19},{4,20},{5,21},{6,22},{7,23},{8,24},{9,... | collective-permute-start | bytes 589832 | tf_op jit(solution)/shard_map/ppermute | solution.py:53
  156.6 3.0 %collective-permute-start.36 = (f32[1,48,256]{2,1,0:T(8,128)S(1)}, f32[1,48,256]{2,1,0:T(8,128)S(1)}, u32[]{:S(2)}, u32[]{:S(2)}) collective-permute-start(f32[1,48,256]{2,1,0:T(8,128)S(1)} %fusion.6), channel_id=1, source_target_pairs={{0,3},{1,0},{2,1},{3,2},{4,7},{5,4},{6,5},{7,6},{8,11},{9,8},{10,9... | collective-permute-start | bytes 147464 | tf_op jit(solution)/shard_map/ppermute | solution.py:53
  160.3 3.9 %collective-permute-start.29 = (f32[1,48,256]{2,1,0:T(8,128)S(1)}, f32[1,48,256]{2,1,0:T(8,128)S(1)}, u32[]{:S(2)}, u32[]{:S(2)}) collective-permute-start(f32[1,48,256]{2,1,0:T(8,128)S(1)} %get-tuple-element.26), channel_id=1, source_target_pairs={{0,1},{1,2},{2,3},{3,0},{4,5},{5,6},{6,7},{7,4},{8,9},{9,10},{10,1... | collective-permute-start | bytes 147464 | tf_op jit(solution)/shard_map/ppermute | solution.py:53
  169.2 1.7 bitcast_subtract_fusion
  (118 shorter events, 22.9 us)
Async XLA Ops:
  1.7 17.6 %collective-permute-start.2 = (bf16[6,48,256]{2,1,0:T(8,128)(2,1)S(1)}, bf16[6,48,256]{2,1,0:T(8,128)(2,1)S(1)}, u32[]{:S(2)}, u32[]{:S(2)}) collective-permute-start(bf16[6,48,256]{2,1,0:T(8,128)(2,1)S(1)} %slice.351), channel_id=1, source_target_pairs={{0,3},{1,0},{2,1},{3,2},{4,7},{5,4},{6,5},{7,6},{8,11},{9,8},{10,9... | collective-permute-start | bytes 442376 | tf_op jit(solution)/shard_map/ppermute | solution.py:53
  6.8 12.5 %collective-permute-start.1 = (bf16[6,48,256]{2,1,0:T(8,128)(2,1)S(1)}, bf16[6,48,256]{2,1,0:T(8,128)(2,1)S(1)}, u32[]{:S(2)}, u32[]{:S(2)}) collective-permute-start(bf16[6,48,256]{2,1,0:T(8,128)(2,1)S(1)} %slice.351), channel_id=1, source_target_pairs={{0,2},{1,3},{2,0},{3,1},{4,6},{5,7},{6,4},{7,5},{8,10},{9,11},{10,... | collective-permute-start | bytes 442376 | tf_op jit(solution)/shard_map/ppermute | solution.py:53
  6.8 10.4 %collective-permute-start = (bf16[6,48,256]{2,1,0:T(8,128)(2,1)S(1)}, bf16[6,48,256]{2,1,0:T(8,128)(2,1)S(1)}, u32[]{:S(2)}, u32[]{:S(2)}) collective-permute-start(bf16[6,48,256]{2,1,0:T(8,128)(2,1)S(1)} %slice.351), channel_id=1, source_target_pairs={{0,1},{1,2},{2,3},{3,0},{4,5},{5,6},{6,7},{7,4},{8,9},{9,10},{10,1... | collective-permute-start | bytes 442376 | tf_op jit(solution)/shard_map/ppermute | solution.py:53
  19.4 11.4 %collective-permute-start.7 = (bf16[12,48,256]{2,1,0:T(8,128)(2,1)S(1)}, bf16[12,48,256]{2,1,0:T(8,128)(2,1)S(1)}, u32[]{:S(2)}, u32[]{:S(2)}) collective-permute-start(bf16[12,48,256]{2,1,0:T(8,128)(2,1)S(1)} %pad_maximum_fusion.1), channel_id=1, source_target_pairs={{0,8},{1,9},{2,10},{3,11},{4,12},{5,13},{6,14},{7,15},{8,0},{9,1},... | collective-permute-start | bytes 884744 | tf_op jit(solution)/shard_map/ppermute | solution.py:53
  21.0 11.4 %collective-permute-start.3 = (bf16[12,48,256]{2,1,0:T(8,128)(2,1)S(1)}, bf16[12,48,256]{2,1,0:T(8,128)(2,1)S(1)}, u32[]{:S(2)}, u32[]{:S(2)}) collective-permute-start(bf16[12,48,256]{2,1,0:T(8,128)(2,1)S(1)} %pad_maximum_fusion), channel_id=1, source_target_pairs={{0,16},{1,17},{2,18},{3,19},{4,20},{5,21},{6,22},{7,23},{8,24},{9,... | collective-permute-start | bytes 884744 | tf_op jit(solution)/shard_map/ppermute | solution.py:53
  22.6 7.6 %collective-permute-start.11 = (bf16[6,16,256]{2,1,0:T(8,128)(2,1)S(1)}, bf16[6,16,256]{2,1,0:T(8,128)(2,1)S(1)}, u32[]{:S(2)}, u32[]{:S(2)}) collective-permute-start(bf16[6,16,256]{2,1,0:T(8,128)(2,1)S(1)} %slice.359), channel_id=1, source_target_pairs={{0,16},{1,17},{2,18},{3,19},{4,20},{5,21},{6,22},{7,23},{8,24},{9,... | collective-permute-start | bytes 147464 | tf_op jit(solution)/shard_map/ppermute | solution.py:53
  30.8 26.6 %collective-permute-start.8 = (bf16[24,48,256]{2,1,0:T(8,128)(2,1)S(1)}, bf16[24,48,256]{2,1,0:T(8,128)(2,1)S(1)}, u32[]{:S(2)}, u32[]{:S(2)}) collective-permute-start(bf16[24,48,256]{2,1,0:T(8,128)(2,1)S(1)} %constant_dynamic-update-slice_fusion.5.refs_8_), channel_id=1, source_target_pairs={{0,16},{1,17},{2,18},{3,19},{4,20},{5,21},{6,22},{7,23},{8,24},{9,... | collective-permute-start | bytes 1769480 | tf_op jit(solution)/shard_map/ppermute | solution.py:53
  32.4 25.1 %collective-permute-start.4 = (bf16[24,48,256]{2,1,0:T(8,128)(2,1)S(1)}, bf16[24,48,256]{2,1,0:T(8,128)(2,1)S(1)}, u32[]{:S(2)}, u32[]{:S(2)}) collective-permute-start(bf16[24,48,256]{2,1,0:T(8,128)(2,1)S(1)} %constant_dynamic-update-slice_fusion.refs_4_), channel_id=1, source_target_pairs={{0,8},{1,9},{2,10},{3,11},{4,12},{5,13},{6,14},{7,15},{8,0},{9,1},... | collective-permute-start | bytes 1769480 | tf_op jit(solution)/shard_map/ppermute | solution.py:53
  36.0 7.3 %collective-permute-start.15 = (bf16[24,16,256]{2,1,0:T(8,128)(2,1)S(1)}, bf16[24,16,256]{2,1,0:T(8,128)(2,1)S(1)}, u32[]{:S(2)}, u32[]{:S(2)}) collective-permute-start(bf16[24,16,256]{2,1,0:T(8,128)(2,1)S(1)} %pad_maximum_fusion.2.refs_12_), channel_id=1, source_target_pairs={{0,3},{1,0},{2,1},{3,2},{4,7},{5,4},{6,5},{7,6},{8,11},{9,8},{10,9... | collective-permute-start | bytes 589832 | tf_op jit(solution)/shard_map/ppermute | solution.py:53
  36.5 20.4 %collective-permute-start.14 = (bf16[24,16,256]{2,1,0:T(8,128)(2,1)S(1)}, bf16[24,16,256]{2,1,0:T(8,128)(2,1)S(1)}, u32[]{:S(2)}, u32[]{:S(2)}) collective-permute-start(bf16[24,16,256]{2,1,0:T(8,128)(2,1)S(1)} %pad_maximum_fusion.2.refs_12_), channel_id=1, source_target_pairs={{0,2},{1,3},{2,0},{3,1},{4,6},{5,7},{6,4},{7,5},{8,10},{9,11},{10,... | collective-permute-start | bytes 589832 | tf_op jit(solution)/shard_map/ppermute | solution.py:53
  38.8 18.1 %collective-permute-start.13 = (bf16[24,16,256]{2,1,0:T(8,128)(2,1)S(1)}, bf16[24,16,256]{2,1,0:T(8,128)(2,1)S(1)}, u32[]{:S(2)}, u32[]{:S(2)}) collective-permute-start(bf16[24,16,256]{2,1,0:T(8,128)(2,1)S(1)} %pad_maximum_fusion.2.refs_12_), channel_id=1, source_target_pairs={{0,1},{1,2},{2,3},{3,0},{4,5},{5,6},{6,7},{7,4},{8,9},{9,10},{10,1... | collective-permute-start | bytes 589832 | tf_op jit(solution)/shard_map/ppermute | solution.py:53
  43.3 14.6 %collective-permute-start.19 = (bf16[24,16,256]{2,1,0:T(8,128)(2,1)S(1)}, bf16[24,16,256]{2,1,0:T(8,128)(2,1)S(1)}, u32[]{:S(2)}, u32[]{:S(2)}) collective-permute-start(bf16[24,16,256]{2,1,0:T(8,128)(2,1)S(1)} %collective-permute-done.15.refs_15_), channel_id=1, source_target_pairs={{0,4},{1,5},{2,6},{3,7},{4,0},{5,1},{6,2},{7,3},{8,12},{9,13},{10,... | collective-permute-start | bytes 589832 | tf_op jit(solution)/shard_map/ppermute | solution.py:53
  56.9 6.3 %collective-permute-start.9 = (bf16[24,48,256]{2,1,0:T(8,128)(2,1)S(1)}, bf16[24,48,256]{2,1,0:T(8,128)(2,1)S(1)}, u32[]{:S(2)}, u32[]{:S(2)}) collective-permute-start(bf16[24,48,256]{2,1,0:T(8,128)(2,1)S(1)} %constant_dynamic-update-slice_fusion.5.refs_8_), channel_id=1, source_target_pairs={{0,4},{1,5},{2,6},{3,7},{4,0},{5,1},{6,2},{7,3},{8,12},{9,13},{10,... | collective-permute-start | bytes 1769480 | tf_op jit(solution)/shard_map/ppermute | solution.py:53
  116.9 22.1 %collective-permute-start.26 = (f32[32,48,256]{2,1,0:T(8,128)}, f32[32,48,256]{2,1,0:T(8,128)S(1)}, u32[]{:S(2)}, u32[]{:S(2)}) collective-permute-start(f32[32,48,256]{2,1,0:T(8,128)} %get-tuple-element.10), channel_id=1, source_target_pairs={{0,4},{1,5},{2,6},{3,7},{4,0},{5,1},{6,2},{7,3},{8,12},{9,13},{10,... | collective-permute-start | bytes 4718600 | tf_op jit(solution)/shard_map/ppermute | solution.py:53
  122.6 12.4 %collective-permute-start.21 = (f32[2,2,2,16,256]{4,3,2,1,0:T(8,128)S(1)}, f32[2,2,2,16,256]{4,3,2,1,0:T(8,128)S(1)}, u32[]{:S(2)}, u32[]{:S(2)}) collective-permute-start(f32[2,2,2,16,256]{4,3,2,1,0:T(8,128)S(1)} %bitcast.138), channel_id=1, source_target_pairs={{0,1},{1,2},{2,3},{3,0},{4,5},{5,6},{6,7},{7,4},{8,9},{9,10},{10,1... | collective-permute-start | bytes 393224 | tf_op jit(solution)/shard_map/ppermute | solution.py:53
  124.6 13.9 %collective-permute-start.22 = (f32[2,2,2,16,256]{4,3,2,1,0:T(8,128)S(1)}, f32[2,2,2,16,256]{4,3,2,1,0:T(8,128)S(1)}, u32[]{:S(2)}, u32[]{:S(2)}) collective-permute-start(f32[2,2,2,16,256]{4,3,2,1,0:T(8,128)S(1)} %bitcast.137), channel_id=1, source_target_pairs={{0,2},{1,3},{2,0},{3,1},{4,6},{5,7},{6,4},{7,5},{8,10},{9,11},{10,... | collective-permute-start | bytes 393224 | tf_op jit(solution)/shard_map/ppermute | solution.py:53
  139.2 11.5 %collective-permute-start.32 = (f32[2,4,1,48,256]{4,3,2,1,0:T(8,128)S(1)}, f32[2,4,1,48,256]{4,3,2,1,0:T(8,128)S(1)}, u32[]{:S(2)}, u32[]{:S(2)}) collective-permute-start(f32[2,4,1,48,256]{4,3,2,1,0:T(8,128)S(1)} %bitcast.132), channel_id=1, source_target_pairs={{0,16},{1,17},{2,18},{3,19},{4,20},{5,21},{6,22},{7,23},{8,24},{9,... | collective-permute-start | bytes 1179656 | tf_op jit(solution)/shard_map/ppermute | solution.py:53
  142.8 7.9 %collective-permute-start.25 = (f32[2,16,256]{2,1,0:T(8,128)S(1)}, f32[2,16,256]{2,1,0:T(8,128)S(1)}, u32[]{:S(2)}, u32[]{:S(2)}) collective-permute-start(f32[2,16,256]{2,1,0:T(8,128)S(1)} %fusion.20), channel_id=1, source_target_pairs={{0,16},{1,17},{2,18},{3,19},{4,20},{5,21},{6,22},{7,23},{8,24},{9,... | collective-permute-start | bytes 98312 | tf_op jit(solution)/shard_map/ppermute | solution.py:53
  142.8 9.6 %collective-permute-start.27 = (f32[2,4,1,48,256]{4,3,2,1,0:T(8,128)S(1)}, f32[2,4,1,48,256]{4,3,2,1,0:T(8,128)S(1)}, u32[]{:S(2)}, u32[]{:S(2)}) collective-permute-start(f32[2,4,1,48,256]{4,3,2,1,0:T(8,128)S(1)} %bitcast.131), channel_id=1, source_target_pairs={{0,8},{1,9},{2,10},{3,11},{4,12},{5,13},{6,14},{7,15},{8,0},{9,1},... | collective-permute-start | bytes 1179656 | tf_op jit(solution)/shard_map/ppermute | solution.py:53
  152.5 7.7 %collective-permute-start.28 = (f32[4,1,48,256]{3,2,1,0:T(8,128)S(1)}, f32[4,1,48,256]{3,2,1,0:T(8,128)S(1)}, u32[]{:S(2)}, u32[]{:S(2)}) collective-permute-start(f32[4,1,48,256]{3,2,1,0:T(8,128)S(1)} %get-tuple-element.23), channel_id=1, source_target_pairs={{0,16},{1,17},{2,18},{3,19},{4,20},{5,21},{6,22},{7,23},{8,24},{9,... | collective-permute-start | bytes 589832 | tf_op jit(solution)/shard_map/ppermute | solution.py:53
  156.6 7.5 %collective-permute-start.36 = (f32[1,48,256]{2,1,0:T(8,128)S(1)}, f32[1,48,256]{2,1,0:T(8,128)S(1)}, u32[]{:S(2)}, u32[]{:S(2)}) collective-permute-start(f32[1,48,256]{2,1,0:T(8,128)S(1)} %fusion.6), channel_id=1, source_target_pairs={{0,3},{1,0},{2,1},{3,2},{4,7},{5,4},{6,5},{7,6},{8,11},{9,8},{10,9... | collective-permute-start | bytes 147464 | tf_op jit(solution)/shard_map/ppermute | solution.py:53
  159.6 6.3 %collective-permute-start.34 = (f32[1,48,256]{2,1,0:T(8,128)S(1)}, f32[1,48,256]{2,1,0:T(8,128)S(1)}, u32[]{:S(2)}, u32[]{:S(2)}) collective-permute-start(f32[1,48,256]{2,1,0:T(8,128)S(1)} %get-tuple-element.29), channel_id=1, source_target_pairs={{0,1},{1,2},{2,3},{3,0},{4,5},{5,6},{6,7},{7,4},{8,9},{9,10},{10,1... | collective-permute-start | bytes 147464 | tf_op jit(solution)/shard_map/ppermute | solution.py:53
  159.7 7.6 %collective-permute-start.35 = (f32[1,48,256]{2,1,0:T(8,128)S(1)}, f32[1,48,256]{2,1,0:T(8,128)S(1)}, u32[]{:S(2)}, u32[]{:S(2)}) collective-permute-start(f32[1,48,256]{2,1,0:T(8,128)S(1)} %get-tuple-element.30), channel_id=1, source_target_pairs={{0,2},{1,3},{2,0},{3,1},{4,6},{5,7},{6,4},{7,5},{8,10},{9,11},{10,... | collective-permute-start | bytes 147464 | tf_op jit(solution)/shard_map/ppermute | solution.py:53
  160.3 7.1 %collective-permute-start.29 = (f32[1,48,256]{2,1,0:T(8,128)S(1)}, f32[1,48,256]{2,1,0:T(8,128)S(1)}, u32[]{:S(2)}, u32[]{:S(2)}) collective-permute-start(f32[1,48,256]{2,1,0:T(8,128)S(1)} %get-tuple-element.26), channel_id=1, source_target_pairs={{0,1},{1,2},{2,3},{3,0},{4,5},{5,6},{6,7},{7,4},{8,9},{9,10},{10,1... | collective-permute-start | bytes 147464 | tf_op jit(solution)/shard_map/ppermute | solution.py:53
  (32 other events, 287.7 us)

commit v4 on v2

--- a/solution.py
+++ b/solution.py
@@ -9,10 +9,11 @@
 
 AXES = ("blk", "grp")
 CORES = 2
-BUFFERS = 4
-AHEAD = 2
-TILE_J = 4
-LAG = 2
+BUFFERS = 5
+AHEAD = 3
+COPY_PARTS = 4
+TILE_J = 16
+LAG = 1
 
 
 def mesh_dims(blk, grp):
@@ -130,14 +131,23 @@
         spot = spot * dims["line"] + away["line"]
         return spot * half_blocks + jnp.where(late, local - half_blocks, local)
 
-    def block_copy(slot):
+    def block_copies(slot):
         at = lax.rem(slot, BUFFERS)
-        return pltpu.make_async_copy(blocks_ref.at[slot], blocks_buf.at[at], block_sems.at[at])
+        span = edge // COPY_PARTS
+        return [
+            pltpu.make_async_copy(
+                blocks_ref.at[slot, pl.ds(part * span, span)],
+                blocks_buf.at[at, pl.ds(part * span, span)],
+                block_sems.at[at, part],
+            )
+            for part in range(COPY_PARTS)
+        ]
 
     def start(slot):
         @pl.when(slot < count)
         def _():
-            block_copy(slot).start()
+            for copy in block_copies(slot):
+                copy.start()
 
     fills = []
     offset = 0
@@ -168,7 +178,8 @@
 
     def step(slot, carry):
         start(slot + AHEAD)
-        block_copy(slot).wait()
+        for copy in block_copies(slot):
+            copy.wait()
         at = lax.rem(slot, BUFFERS)
         before = jnp.maximum(slot - 1, 0)
         at_before = lax.rem(before, BUFFERS)
@@ -239,7 +250,7 @@
             pltpu.VMEM((tiles, TILE_J * edge, rank), jnp.bfloat16),
             pltpu.VMEM((tiles, edge, TILE_J * edge), jnp.float32),
             pltpu.VMEM((edge, rank), jnp.float32),
-            pltpu.SemaphoreType.DMA((BUFFERS,)),
+            pltpu.SemaphoreType.DMA((BUFFERS, COPY_PARTS)),
             pltpu.SemaphoreType.DMA((len(pieces),)),
             pltpu.SemaphoreType.DMA((2,)),
         ],
@@ -264,17 +275,20 @@
 
     arrived = by_half(shift(other, dims, "core", 1))
     kept_halves = by_half(mine)
-    grads = []
+    sums = []
     for half, (first, second) in enumerate(ORDERS):
         kept, got = kept_halves[half], [arrived[half]]
-        for name in (second, first, "line"):
-            sums = [
+        for name in (second, first):
+            terms = [
                 functools.reduce(jnp.add, [g[k] for g in got], kept[k]) for k in range(dims[name])
             ]
-            kept = sums[0]
-            got = [shift(sums[k], dims, name, k) for k in range(1, dims[name])]
-        grads.append(functools.reduce(jnp.add, got, kept))
-    grad = jnp.concatenate(grads)
+            kept = terms[0]
+            got = [shift(terms[k], dims, name, k) for k in range(1, dims[name])]
+        sums.append(functools.reduce(jnp.add, got, kept))
+    rows = [jnp.concatenate([part[k] for part in sums]) for k in range(dims["line"])]
+    grad = rows[0]
+    for k in range(1, dims["line"]):
+        grad = grad + shift(rows[k], dims, "line", k)
     new_moment1 = 0.9 * moment1 + 0.1 * grad
     new_moment2 = 0.999 * moment2 + 0.001 * grad * grad
     new_factor = factors[0] - 0.02 * (new_moment1 / (1.0 - 0.9**8)) / (

time: 154 us -> 144 us (0.935); the launches traced: 153 us -> 146 us
  starting transfers between devices: 73.4 us -> 41.4 us
  waiting for transfers between devices: 53.9 us -> 68.3 us
  Pallas kernels: 17.9 us -> 29.1 us
    ppermute x22 -> x19, starting transfers between devices: 73.4 us -> 41.4 us  [shift(): return lax.ppermute(values, AXES, perm)]
    ppermute x22 -> x19, waiting for transfers between devices: 53.9 us -> 68.3 us  [shift(): return lax.ppermute(values, AXES, perm)]
    pallas_call x1, Pallas kernels: 17.9 us -> 29.1 us  [per_device(): pl.pallas_call(functools.partial(slots_kernel, dims, local_blocks, len(pi...]
  transfers between devices with their start and end apart: 22 -> 19, of which waited for: 11 -> 13; matrix products, arithmetic and copies ran while one was open for 0% -> 0% of each run, Pallas kernels for 0% -> 0%
where the time goes in v4:
time: 144 us; the launch traced here: 146 us
  waiting for transfers between devices  68.3 us (47%)
  starting transfers between devices  41.4 us (29%)
  Pallas kernels  29.1 us (20%)
  other arithmetic  4.93 us (3%)
  between operations  1.57 us (1%)
    ppermute x19, waiting for transfers between devices, shift(): return lax.ppermute(values, AXES, perm)  68.3 us
    ppermute x19, starting transfers between devices, shift(): return lax.ppermute(values, AXES, perm)  41.4 us
    pallas_call x1, Pallas kernels, per_device(): pl.pallas_call(functools.partial(slots_kernel, dims, local_blocks, len(pi...  29.1 us
  transfers between devices with their start and end apart: 19, of which 13 were waited for; matrix products, arithmetic and copies ran while one was open for 0% of the time, Pallas kernels for 0%

profile of v4, /device:TPU:0, one launch (start us, length us, event | category | flops | bytes accessed | tf_op | source)
XLA Modules:
  0.0 146.4 jit_solution(2340799228668730134)
XLA Ops:
  0.6 1.0 convert_element_type.3
  1.7 5.1 %collective-permute-start.2 = (bf16[6,64,256]{2,1,0:T(8,128)(2,1)S(1)}, bf16[6,64,256]{2,1,0:T(8,128)(2,1)S(1)}, u32[]{:S(2)}, u32[]{:S(2)}) collective-permute-start(bf16[6,64,256]{2,1,0:T(8,128)(2,1)S(1)} %bitcast.49), channel_id=1, source_target_pairs={{0,3},{1,0},{2,1},{3,2},{4,7},{5,4},{6,5},{7,6},{8,11},{9,8},{10,9... | collective-permute-start | bytes 589832 | tf_op jit(solution)/shard_map/ppermute | solution.py:54
  7.8 12.5 %collective-permute-done = bf16[6,64,256]{2,1,0:T(8,128)(2,1)S(1)} collective-permute-done((bf16[6,64,256]{2,1,0:T(8,128)(2,1)S(1)}, bf16[6,64,256]{2,1,0:T(8,128)(2,1)S(1)}, u32[]{:S(2)}, u32[]{:S(2)}) %collective-permute-start) | collective-permute-done | bytes 196640 | tf_op jit(solution)/shard_map/ppermute | solution.py:54
  20.4 3.1 %collective-permute-done.1 = bf16[6,64,256]{2,1,0:T(8,128)(2,1)S(1)} collective-permute-done((bf16[6,64,256]{2,1,0:T(8,128)(2,1)S(1)}, bf16[6,64,256]{2,1,0:T(8,128)(2,1)S(1)}, u32[]{:S(2)}, u32[]{:S(2)}) %collective-permute-start.1) | collective-permute-done | bytes 196640 | tf_op jit(solution)/shard_map/ppermute | solution.py:54
  23.6 1.6 %collective-permute-start.7 = (bf16[12,64,256]{2,1,0:T(8,128)(2,1)S(1)}, bf16[12,64,256]{2,1,0:T(8,128)(2,1)S(1)}, u32[]{:S(2)}, u32[]{:S(2)}) collective-permute-start(bf16[12,64,256]{2,1,0:T(8,128)(2,1)S(1)} %pad_maximum_fusion.1), channel_id=1, source_target_pairs={{0,8},{1,9},{2,10},{3,11},{4,12},{5,13},{6,14},{7,15},{8,0},{9,1},... | collective-permute-start | bytes 1179656 | tf_op jit(solution)/shard_map/ppermute | solution.py:54
  25.2 1.6 %collective-permute-start.3 = (bf16[12,64,256]{2,1,0:T(8,128)(2,1)S(1)}, bf16[12,64,256]{2,1,0:T(8,128)(2,1)S(1)}, u32[]{:S(2)}, u32[]{:S(2)}) collective-permute-start(bf16[12,64,256]{2,1,0:T(8,128)(2,1)S(1)} %pad_maximum_fusion), channel_id=1, source_target_pairs={{0,16},{1,17},{2,18},{3,19},{4,20},{5,21},{6,22},{7,23},{8,24},{9,... | collective-permute-start | bytes 1179656 | tf_op jit(solution)/shard_map/ppermute | solution.py:54
  26.8 7.1 %collective-permute-done.7 = bf16[12,64,256]{2,1,0:T(8,128)(2,1)S(1)} collective-permute-done((bf16[12,64,256]{2,1,0:T(8,128)(2,1)S(1)}, bf16[12,64,256]{2,1,0:T(8,128)(2,1)S(1)}, u32[]{:S(2)}, u32[]{:S(2)}) %collective-permute-start.7) | collective-permute-done | bytes 393248 | tf_op jit(solution)/shard_map/ppermute | solution.py:54
  33.9 1.6 %collective-permute-start.8 = (bf16[24,64,256]{2,1,0:T(8,128)(2,1)S(1)}, bf16[24,64,256]{2,1,0:T(8,128)(2,1)S(1)}, u32[]{:S(2)}, u32[]{:S(2)}) collective-permute-start(bf16[24,64,256]{2,1,0:T(8,128)(2,1)S(1)} %constant_dynamic-update-slice_fusion.5.refs_8_), channel_id=1, source_target_pairs={{0,16},{1,17},{2,18},{3,19},{4,20},{5,21},{6,22},{7,23},{8,24},{9,... | collective-permute-start | bytes 2359304 | tf_op jit(solution)/shard_map/ppermute | solution.py:54
  35.5 1.5 %collective-permute-start.4 = (bf16[24,64,256]{2,1,0:T(8,128)(2,1)S(1)}, bf16[24,64,256]{2,1,0:T(8,128)(2,1)S(1)}, u32[]{:S(2)}, u32[]{:S(2)}) collective-permute-start(bf16[24,64,256]{2,1,0:T(8,128)(2,1)S(1)} %constant_dynamic-update-slice_fusion.refs_4_), channel_id=1, source_target_pairs={{0,8},{1,9},{2,10},{3,11},{4,12},{5,13},{6,14},{7,15},{8,0},{9,1},... | collective-permute-start | bytes 2359304 | tf_op jit(solution)/shard_map/ppermute | solution.py:54
  37.6 14.4 %collective-permute-done.8.refs_9_ = bf16[24,64,256]{2,1,0:T(8,128)(2,1)S(1)} collective-permute-done((bf16[24,64,256]{2,1,0:T(8,128)(2,1)S(1)}, bf16[24,64,256]{2,1,0:T(8,128)(2,1)S(1)}, u32[]{:S(2)}, u32[]{:S(2)}) %collective-permute-start.8) | collective-permute-done | bytes 786464 | tf_op jit(solution)/shard_map/ppermute | solution.py:54
  54.3 1.1 collective-permute-done.6.refs_7_
  56.4 29.1 %shard_map.94 = (f32[32,64,256]{2,1,0:T(8,128)}, f32[32,64,256]{2,1,0:T(8,128)}) custom-call(s32[3,36]{1,0:T(4,128)} %refs_0_.1, s32[1]{0:T(128)S(6)} %copy.18.refs_1_, s32[3,64]{1,0:T(4,128)} %refs_2_.1, bf16[36,64,4096]{2,1,0:T(8,128)(2,1)} %refs_3_.1, bf16[24,64,256]{2,1,0:T(8,128)(2,1)} %copy-done.2, bf16[24,64,256]{2,1,0:T(8,128)(2,1)} %copy-done.5, ...), custom_call_target="tpu_custom_call" | custom-call | flops 9663676416 | bytes 18874368 | tf_op jit(solution)/shard_map/pallas_call | solution.py:241
  85.5 18.3 %collective-permute-start.11 = (f32[32,64,256]{2,1,0:T(8,128)}, f32[32,64,256]{2,1,0:T(8,128)S(1)}, u32[]{:S(2)}, u32[]{:S(2)}) collective-permute-start(f32[32,64,256]{2,1,0:T(8,128)} %get-tuple-element.6), channel_id=1, source_target_pairs={{0,4},{1,5},{2,6},{3,7},{4,0},{5,1},{6,2},{7,3},{8,12},{9,13},{10,... | collective-permute-start | bytes 6291464 | tf_op jit(solution)/shard_map/ppermute | solution.py:54
  103.9 4.0 %collective-permute-done.11 = f32[32,64,256]{2,1,0:T(8,128)S(1)} collective-permute-done((f32[32,64,256]{2,1,0:T(8,128)}, f32[32,64,256]{2,1,0:T(8,128)S(1)}, u32[]{:S(2)}, u32[]{:S(2)}) %collective-permute-start.11) | collective-permute-done | bytes 2097184 | tf_op jit(solution)/shard_map/ppermute | solution.py:54
  107.9 1.9 %slice_add_fusion.3 = (f32[8,64,256]{2,1,0:T(8,128)S(1)}, f32[8,64,256]{2,1,0:T(8,128)S(1)}, f32[8,64,256]{2,1,0:T(8,128)S(1)}, f32[8,64,256]{2,1,0:T(8,128)S(1)}) fusion(f32[32,64,256]{2,1,0:T(8,128)S(1)} %collective-permute-done.11, f32[32,64,256]{2,1,0:T(8,128)} %get-tuple-element.5), kind=kLoop, calls=%fused_computation.3 | loop fusion | flops 524288 | bytes 6291456 | tf_op jit(solution)/shard_map/add | solution.py:283
  109.8 1.5 %collective-permute-start.14 = (f32[2,4,64,256]{3,2,1,0:T(8,128)S(1)}, f32[2,4,64,256]{3,2,1,0:T(8,128)S(1)}, u32[]{:S(2)}, u32[]{:S(2)}) collective-permute-start(f32[2,4,64,256]{3,2,1,0:T(8,128)S(1)} %bitcast.53), channel_id=1, source_target_pairs={{0,16},{1,17},{2,18},{3,19},{4,20},{5,21},{6,22},{7,23},{8,24},{9,... | collective-permute-start | bytes 1572872 | tf_op jit(solution)/shard_map/ppermute | solution.py:54
  111.3 12.7 %collective-permute-done.12 = f32[2,4,64,256]{3,2,1,0:T(8,128)S(1)} collective-permute-done((f32[2,4,64,256]{3,2,1,0:T(8,128)S(1)}, f32[2,4,64,256]{3,2,1,0:T(8,128)S(1)}, u32[]{:S(2)}, u32[]{:S(2)}) %collective-permute-start.12) | collective-permute-done | bytes 524320 | tf_op jit(solution)/shard_map/ppermute | solution.py:54
  124.2 1.7 %collective-permute-start.15 = (f32[4,64,256]{2,1,0:T(8,128)S(1)}, f32[4,64,256]{2,1,0:T(8,128)S(1)}, u32[]{:S(2)}, u32[]{:S(2)}) collective-permute-start(f32[4,64,256]{2,1,0:T(8,128)S(1)} %fusion), channel_id=1, source_target_pairs={{0,8},{1,9},{2,10},{3,11},{4,12},{5,13},{6,14},{7,15},{8,0},{9,1},... | collective-permute-start | bytes 786440 | tf_op jit(solution)/shard_map/ppermute | solution.py:54
  125.9 6.0 %collective-permute-done.13 = f32[4,64,256]{2,1,0:T(8,128)S(1)} collective-permute-done((f32[4,64,256]{2,1,0:T(8,128)S(1)}, f32[4,64,256]{2,1,0:T(8,128)S(1)}, u32[]{:S(2)}, u32[]{:S(2)}) %collective-permute-start.13) | collective-permute-done | bytes 262176 | tf_op jit(solution)/shard_map/ppermute | solution.py:54
  132.2 3.9 %collective-permute-start.17 = (f32[128,256]{1,0:T(8,128)S(1)}, f32[128,256]{1,0:T(8,128)S(1)}, u32[]{:S(2)}, u32[]{:S(2)}) collective-permute-start(f32[128,256]{1,0:T(8,128)S(1)} %pad_maximum_fusion.3), channel_id=1, source_target_pairs={{0,2},{1,3},{2,0},{3,1},{4,6},{5,7},{6,4},{7,5},{8,10},{9,11},{10,... | collective-permute-start | bytes 393224 | tf_op jit(solution)/shard_map/ppermute | solution.py:54
  136.1 3.0 %collective-permute-start.18 = (f32[128,256]{1,0:T(8,128)S(1)}, f32[128,256]{1,0:T(8,128)S(1)}, u32[]{:S(2)}, u32[]{:S(2)}) collective-permute-start(f32[128,256]{1,0:T(8,128)S(1)} %pad_maximum_fusion.4), channel_id=1, source_target_pairs={{0,3},{1,0},{2,1},{3,2},{4,7},{5,4},{6,5},{7,6},{8,11},{9,8},{10,9... | collective-permute-start | bytes 393224 | tf_op jit(solution)/shard_map/ppermute | solution.py:54
  139.1 1.1 collective-permute-done.16
  140.1 4.6 %collective-permute-done.17 = f32[128,256]{1,0:T(8,128)S(1)} collective-permute-done((f32[128,256]{1,0:T(8,128)S(1)}, f32[128,256]{1,0:T(8,128)S(1)}, u32[]{:S(2)}, u32[]{:S(2)}) %collective-permute-start.17) | collective-permute-done | bytes 131104 | tf_op jit(solution)/shard_map/ppermute | solution.py:54
  144.7 1.7 %bitcast_subtract_fusion = (f32[128,256]{1,0:T(8,128)}, f32[128,256]{1,0:T(8,128)}, f32[128,256]{1,0:T(8,128)}) fusion(f32[3,128,256]{2,1,0:T(8,128)} %param.11, f32[128,256]{1,0:T(8,128)S(1)} %copy-done, f32[128,256]{1,0:T(8,128)S(1)} %copy-done.1, f32[128,256]{1,0:T(8,128)S(1)} %collective-permute-done.18, f32[128,256]{1,0:T(8,128)S(1)} %collective-permute-done.17, ...), kind=kLoop, calls=%fused_computation.28 | loop fusion | flops 524288 | bytes 1310720 | tf_op jit(solution)/shard_map/sub | solution.py:294
  (55 shorter events, 4.8 us)
Async XLA Ops:
  1.7 21.8 %collective-permute-start.2 = (bf16[6,64,256]{2,1,0:T(8,128)(2,1)S(1)}, bf16[6,64,256]{2,1,0:T(8,128)(2,1)S(1)}, u32[]{:S(2)}, u32[]{:S(2)}) collective-permute-start(bf16[6,64,256]{2,1,0:T(8,128)(2,1)S(1)} %bitcast.49), channel_id=1, source_target_pairs={{0,3},{1,0},{2,1},{3,2},{4,7},{5,4},{6,5},{7,6},{8,11},{9,8},{10,9... | collective-permute-start | bytes 589832 | tf_op jit(solution)/shard_map/ppermute | solution.py:54
  6.8 16.7 %collective-permute-start.1 = (bf16[6,64,256]{2,1,0:T(8,128)(2,1)S(1)}, bf16[6,64,256]{2,1,0:T(8,128)(2,1)S(1)}, u32[]{:S(2)}, u32[]{:S(2)}) collective-permute-start(bf16[6,64,256]{2,1,0:T(8,128)(2,1)S(1)} %bitcast.50), channel_id=1, source_target_pairs={{0,2},{1,3},{2,0},{3,1},{4,6},{5,7},{6,4},{7,5},{8,10},{9,11},{10,... | collective-permute-start | bytes 589832 | tf_op jit(solution)/shard_map/ppermute | solution.py:54
  6.8 13.6 %collective-permute-start = (bf16[6,64,256]{2,1,0:T(8,128)(2,1)S(1)}, bf16[6,64,256]{2,1,0:T(8,128)(2,1)S(1)}, u32[]{:S(2)}, u32[]{:S(2)}) collective-permute-start(bf16[6,64,256]{2,1,0:T(8,128)(2,1)S(1)} %bitcast.51), channel_id=1, source_target_pairs={{0,1},{1,2},{2,3},{3,0},{4,5},{5,6},{6,7},{7,4},{8,9},{9,10},{10,1... | collective-permute-start | bytes 589832 | tf_op jit(solution)/shard_map/ppermute | solution.py:54
  23.6 10.3 %collective-permute-start.7 = (bf16[12,64,256]{2,1,0:T(8,128)(2,1)S(1)}, bf16[12,64,256]{2,1,0:T(8,128)(2,1)S(1)}, u32[]{:S(2)}, u32[]{:S(2)}) collective-permute-start(bf16[12,64,256]{2,1,0:T(8,128)(2,1)S(1)} %pad_maximum_fusion.1), channel_id=1, source_target_pairs={{0,8},{1,9},{2,10},{3,11},{4,12},{5,13},{6,14},{7,15},{8,0},{9,1},... | collective-permute-start | bytes 1179656 | tf_op jit(solution)/shard_map/ppermute | solution.py:54
  25.2 10.3 %collective-permute-start.3 = (bf16[12,64,256]{2,1,0:T(8,128)(2,1)S(1)}, bf16[12,64,256]{2,1,0:T(8,128)(2,1)S(1)}, u32[]{:S(2)}, u32[]{:S(2)}) collective-permute-start(bf16[12,64,256]{2,1,0:T(8,128)(2,1)S(1)} %pad_maximum_fusion), channel_id=1, source_target_pairs={{0,16},{1,17},{2,18},{3,19},{4,20},{5,21},{6,22},{7,23},{8,24},{9,... | collective-permute-start | bytes 1179656 | tf_op jit(solution)/shard_map/ppermute | solution.py:54
  33.9 21.6 %copy-start.3 = (bf16[24,64,256]{2,1,0:T(8,128)(2,1)}, bf16[24,64,256]{2,1,0:T(8,128)(2,1)S(1)}, u32[]{:S(2)}) copy-start(bf16[24,64,256]{2,1,0:T(8,128)(2,1)S(1)} %constant_dynamic-update-slice_fusion.5.refs_8_) | copy-start | bytes 2359300
  33.9 18.1 %collective-permute-start.8 = (bf16[24,64,256]{2,1,0:T(8,128)(2,1)S(1)}, bf16[24,64,256]{2,1,0:T(8,128)(2,1)S(1)}, u32[]{:S(2)}, u32[]{:S(2)}) collective-permute-start(bf16[24,64,256]{2,1,0:T(8,128)(2,1)S(1)} %constant_dynamic-update-slice_fusion.5.refs_8_), channel_id=1, source_target_pairs={{0,16},{1,17},{2,18},{3,19},{4,20},{5,21},{6,22},{7,23},{8,24},{9,... | collective-permute-start | bytes 2359304 | tf_op jit(solution)/shard_map/ppermute | solution.py:54
  35.5 19.9 %copy-start.2 = (bf16[24,64,256]{2,1,0:T(8,128)(2,1)}, bf16[24,64,256]{2,1,0:T(8,128)(2,1)S(1)}, u32[]{:S(2)}) copy-start(bf16[24,64,256]{2,1,0:T(8,128)(2,1)S(1)} %constant_dynamic-update-slice_fusion.refs_4_) | copy-start | bytes 2359300
  35.5 17.5 %collective-permute-start.4 = (bf16[24,64,256]{2,1,0:T(8,128)(2,1)S(1)}, bf16[24,64,256]{2,1,0:T(8,128)(2,1)S(1)}, u32[]{:S(2)}, u32[]{:S(2)}) collective-permute-start(bf16[24,64,256]{2,1,0:T(8,128)(2,1)S(1)} %constant_dynamic-update-slice_fusion.refs_4_), channel_id=1, source_target_pairs={{0,8},{1,9},{2,10},{3,11},{4,12},{5,13},{6,14},{7,15},{8,0},{9,1},... | collective-permute-start | bytes 2359304 | tf_op jit(solution)/shard_map/ppermute | solution.py:54
  37.1 16.6 %collective-permute-start.9 = (bf16[24,64,256]{2,1,0:T(8,128)(2,1)S(1)}, bf16[24,64,256]{2,1,0:T(8,128)(2,1)S(1)}, u32[]{:S(2)}, u32[]{:S(2)}) collective-permute-start(bf16[24,64,256]{2,1,0:T(8,128)(2,1)S(1)} %constant_dynamic-update-slice_fusion.5.refs_8_), channel_id=1, source_target_pairs={{0,4},{1,5},{2,6},{3,7},{4,0},{5,1},{6,2},{7,3},{8,12},{9,13},{10,... | collective-permute-start | bytes 2359304 | tf_op jit(solution)/shard_map/ppermute | solution.py:54
  37.1 16.6 %collective-permute-start.5 = (bf16[24,64,256]{2,1,0:T(8,128)(2,1)S(1)}, bf16[24,64,256]{2,1,0:T(8,128)(2,1)S(1)}, u32[]{:S(2)}, u32[]{:S(2)}) collective-permute-start(bf16[24,64,256]{2,1,0:T(8,128)(2,1)S(1)} %constant_dynamic-update-slice_fusion.refs_4_), channel_id=1, source_target_pairs={{0,4},{1,5},{2,6},{3,7},{4,0},{5,1},{6,2},{7,3},{8,12},{9,13},{10,... | collective-permute-start | bytes 2359304 | tf_op jit(solution)/shard_map/ppermute | solution.py:54
  52.0 3.4 %copy-start.4 = (bf16[24,64,256]{2,1,0:T(8,128)(2,1)}, bf16[24,64,256]{2,1,0:T(8,128)(2,1)S(1)}, u32[]{:S(2)}) copy-start(bf16[24,64,256]{2,1,0:T(8,128)(2,1)S(1)} %collective-permute-done.8.refs_9_) | copy-start | bytes 2359300
  52.0 2.3 %collective-permute-start.10 = (bf16[24,64,256]{2,1,0:T(8,128)(2,1)S(1)}, bf16[24,64,256]{2,1,0:T(8,128)(2,1)S(1)}, u32[]{:S(2)}, u32[]{:S(2)}) collective-permute-start(bf16[24,64,256]{2,1,0:T(8,128)(2,1)S(1)} %collective-permute-done.8.refs_9_), channel_id=1, source_target_pairs={{0,4},{1,5},{2,6},{3,7},{4,0},{5,1},{6,2},{7,3},{8,12},{9,13},{10,... | collective-permute-start | bytes 2359304 | tf_op jit(solution)/shard_map/ppermute | solution.py:54
  53.0 2.4 %collective-permute-start.6 = (bf16[24,64,256]{2,1,0:T(8,128)(2,1)S(1)}, bf16[24,64,256]{2,1,0:T(8,128)(2,1)S(1)}, u32[]{:S(2)}, u32[]{:S(2)}) collective-permute-start(bf16[24,64,256]{2,1,0:T(8,128)(2,1)S(1)} %collective-permute-done.4.refs_5_), channel_id=1, source_target_pairs={{0,4},{1,5},{2,6},{3,7},{4,0},{5,1},{6,2},{7,3},{8,12},{9,13},{10,... | collective-permute-start | bytes 2359304 | tf_op jit(solution)/shard_map/ppermute | solution.py:54
  85.5 22.3 %collective-permute-start.11 = (f32[32,64,256]{2,1,0:T(8,128)}, f32[32,64,256]{2,1,0:T(8,128)S(1)}, u32[]{:S(2)}, u32[]{:S(2)}) collective-permute-start(f32[32,64,256]{2,1,0:T(8,128)} %get-tuple-element.6), channel_id=1, source_target_pairs={{0,4},{1,5},{2,6},{3,7},{4,0},{5,1},{6,2},{7,3},{8,12},{9,13},{10,... | collective-permute-start | bytes 6291464 | tf_op jit(solution)/shard_map/ppermute | solution.py:54
  109.7 14.3 %collective-permute-start.12 = (f32[2,4,64,256]{3,2,1,0:T(8,128)S(1)}, f32[2,4,64,256]{3,2,1,0:T(8,128)S(1)}, u32[]{:S(2)}, u32[]{:S(2)}) collective-permute-start(f32[2,4,64,256]{3,2,1,0:T(8,128)S(1)} %bitcast.54), channel_id=1, source_target_pairs={{0,8},{1,9},{2,10},{3,11},{4,12},{5,13},{6,14},{7,15},{8,0},{9,1},... | collective-permute-start | bytes 1572872 | tf_op jit(solution)/shard_map/ppermute | solution.py:54
  109.8 14.3 %collective-permute-start.14 = (f32[2,4,64,256]{3,2,1,0:T(8,128)S(1)}, f32[2,4,64,256]{3,2,1,0:T(8,128)S(1)}, u32[]{:S(2)}, u32[]{:S(2)}) collective-permute-start(f32[2,4,64,256]{3,2,1,0:T(8,128)S(1)} %bitcast.53), channel_id=1, source_target_pairs={{0,16},{1,17},{2,18},{3,19},{4,20},{5,21},{6,22},{7,23},{8,24},{9,... | collective-permute-start | bytes 1572872 | tf_op jit(solution)/shard_map/ppermute | solution.py:54
  124.0 7.8 %collective-permute-start.13 = (f32[4,64,256]{2,1,0:T(8,128)S(1)}, f32[4,64,256]{2,1,0:T(8,128)S(1)}, u32[]{:S(2)}, u32[]{:S(2)}) collective-permute-start(f32[4,64,256]{2,1,0:T(8,128)S(1)} %fusion.3), channel_id=1, source_target_pairs={{0,16},{1,17},{2,18},{3,19},{4,20},{5,21},{6,22},{7,23},{8,24},{9,... | collective-permute-start | bytes 786440 | tf_op jit(solution)/shard_map/ppermute | solution.py:54
  124.2 20.5 %copy-start = (f32[128,256]{1,0:T(8,128)S(1)}, f32[128,256]{1,0:T(8,128)}, u32[]{:S(2)}) copy-start(f32[128,256]{1,0:T(8,128)} %param.12) | copy-start | bytes 393220
  124.2 20.5 %copy-start.1 = (f32[128,256]{1,0:T(8,128)S(1)}, f32[128,256]{1,0:T(8,128)}, u32[]{:S(2)}) copy-start(f32[128,256]{1,0:T(8,128)} %param.13) | copy-start | bytes 393220
  124.2 7.8 %collective-permute-start.15 = (f32[4,64,256]{2,1,0:T(8,128)S(1)}, f32[4,64,256]{2,1,0:T(8,128)S(1)}, u32[]{:S(2)}, u32[]{:S(2)}) collective-permute-start(f32[4,64,256]{2,1,0:T(8,128)S(1)} %fusion), channel_id=1, source_target_pairs={{0,8},{1,9},{2,10},{3,11},{4,12},{5,13},{6,14},{7,15},{8,0},{9,1},... | collective-permute-start | bytes 786440 | tf_op jit(solution)/shard_map/ppermute | solution.py:54
  132.1 8.0 %collective-permute-start.16 = (f32[128,256]{1,0:T(8,128)S(1)}, f32[128,256]{1,0:T(8,128)S(1)}, u32[]{:S(2)}, u32[]{:S(2)}) collective-permute-start(f32[128,256]{1,0:T(8,128)S(1)} %pad_maximum_fusion.2), channel_id=1, source_target_pairs={{0,1},{1,2},{2,3},{3,0},{4,5},{5,6},{6,7},{7,4},{8,9},{9,10},{10,1... | collective-permute-start | bytes 393224 | tf_op jit(solution)/shard_map/ppermute | solution.py:54
  132.2 12.5 %collective-permute-start.17 = (f32[128,256]{1,0:T(8,128)S(1)}, f32[128,256]{1,0:T(8,128)S(1)}, u32[]{:S(2)}, u32[]{:S(2)}) collective-permute-start(f32[128,256]{1,0:T(8,128)S(1)} %pad_maximum_fusion.3), channel_id=1, source_target_pairs={{0,2},{1,3},{2,0},{3,1},{4,6},{5,7},{6,4},{7,5},{8,10},{9,11},{10,... | collective-permute-start | bytes 393224 | tf_op jit(solution)/shard_map/ppermute | solution.py:54
  136.1 8.6 %collective-permute-start.18 = (f32[128,256]{1,0:T(8,128)S(1)}, f32[128,256]{1,0:T(8,128)S(1)}, u32[]{:S(2)}, u32[]{:S(2)}) collective-permute-start(f32[128,256]{1,0:T(8,128)S(1)} %pad_maximum_fusion.4), channel_id=1, source_target_pairs={{0,3},{1,0},{2,1},{3,2},{4,7},{5,4},{6,5},{7,6},{8,11},{9,8},{10,9... | collective-permute-start | bytes 393224 | tf_op jit(solution)/shard_map/ppermute | solution.py:54
  (5 other events, 8.1 us)

commit v5 on v4

--- a/solution.py
+++ b/solution.py
@@ -12,7 +12,8 @@
 BUFFERS = 5
 AHEAD = 3
 COPY_PARTS = 4
-TILE_J = 16
+TILE_J = 32
+SIDE_ROWS = 16
 LAG = 1
 
 
@@ -58,26 +59,27 @@
 
 
 def gather_rows(shard, dims):
-    count = shard.shape[0]
-    cut = count // 2
-    line = [shard] + [shift(shard, dims, "line", k) for k in range(1, dims["line"])]
-    halves = []
-    for part, (first, second) in zip((slice(0, cut), slice(cut, count)), ORDERS):
+    cut = shard.shape[0] // 2
+    side = lax.all_gather(shard[:, :SIDE_ROWS], AXES, axis=0, tiled=True)
+    main = shard[:, SIDE_ROWS:]
+    line = [main] + [shift(main, dims, "line", k) for k in range(1, dims["line"])]
+    mains = []
+    for part, (first, second) in zip((slice(0, cut), slice(cut, None)), ORDERS):
         own = jnp.concatenate([piece[part] for piece in line])
         own = jnp.concatenate([own] + [shift(own, dims, first, k) for k in range(1, dims[first])])
-        pieces = [own] + [shift(own, dims, second, k) for k in range(1, dims[second])]
-        pieces = pieces + [shift(piece, dims, "core", 1) for piece in pieces]
-        halves.append(pieces)
-    return halves
-
-
-def slots_kernel(dims, local_blocks, piece_count, *refs):
+        mains.append([own] + [shift(own, dims, second, k) for k in range(1, dims[second])])
+    mains = [pieces + [shift(piece, dims, "core", 1) for piece in pieces] for pieces in mains]
+    return mains[0] + mains[1], [side]
+
+
+def slots_kernel(dims, local_blocks, main_count, piece_count, *refs):
     coords_ref, count_ref, owner_ref, blocks_ref = refs[:4]
     pieces = refs[4 : 4 + piece_count]
     (
         mine_ref,
         other_ref,
-        table_ref,
+        main_ref,
+        side_ref,
         grad_ref,
         blocks_buf,
         pair_ref,
@@ -95,7 +97,7 @@
     here = split_index(lax.axis_index("blk") * dims["line"] + lax.axis_index("grp"), dims)
     columns = dims["core"] * dims["outer"] * dims["inner"] * dims["line"]
 
-    def row_place(mode, slot):
+    def row_places(mode, slot):
         pos = owner_ref[mode, coords_ref[mode, slot]]
         there = split_index(lax.div(pos, local_blocks), dims)
         away = {
@@ -110,8 +112,19 @@
         spot = ((away["core"] * size_second + second) * size_first + first) * dims["line"]
         spot = spot + away["line"]
         blocks_of = jnp.where(late, 3 * local_blocks - cut, cut)
-        base = jnp.where(late, columns * cut, 0)
-        return base + spot * blocks_of + jnp.where(late, block - cut, block)
+        main = jnp.where(late, columns * cut + block - cut, block) + spot * blocks_of
+        side = lax.div(pos, local_blocks) * (3 * local_blocks) + block
+        return main, side
+
+    def rows_of(places):
+        main, side = places
+        return jnp.concatenate([side_ref[side], main_ref[main]], axis=0)
+
+    def row_of(places, j):
+        main, side = places
+        if j < SIDE_ROWS:
+            return side_ref[side, pl.ds(j, 1), :]
+        return main_ref[main, pl.ds(j - SIDE_ROWS, 1), :]
 
     def grad_place(slot):
         pos = owner_ref[0, coords_ref[0, slot]]
@@ -150,15 +163,16 @@
                 copy.start()
 
     fills = []
-    offset = 0
-    for index, piece in enumerate(pieces):
-        size = piece.shape[0]
-        fills.append(
-            pltpu.make_async_copy(
-                piece, table_ref.at[pl.ds(offset, size)], piece_sems.at[index]
-            )
-        )
-        offset += size
+    for table, group in ((main_ref, range(main_count)), (side_ref, range(main_count, piece_count))):
+        offset = 0
+        for index in group:
+            size = pieces[index].shape[0]
+            fills.append(
+                pltpu.make_async_copy(
+                    pieces[index], table.at[pl.ds(offset, size)], piece_sems.at[index]
+                )
+            )
+            offset += size
     for fill in fills:
         fill.start()
     for slot in range(AHEAD):
@@ -174,7 +188,10 @@
     def finish(tile, at, total):
         twice = blocks_buf[at, :, tile * width : (tile + 1) * width].astype(jnp.float32) * 2.0
         resid = ((jnp.tanh(model_ref[tile]) + 1.0) - twice).astype(jnp.bfloat16)
-        return total + jnp.dot(resid, pair_ref[tile], preferred_element_type=jnp.float32)
+        middle = width // 2
+        low = jnp.dot(resid[:, :middle], pair_ref[tile, :middle], preferred_element_type=jnp.float32)
+        high = jnp.dot(resid[:, middle:], pair_ref[tile, middle:], preferred_element_type=jnp.float32)
+        return total + (low + high)
 
     def step(slot, carry):
         start(slot + AHEAD)
@@ -183,9 +200,9 @@
         at = lax.rem(slot, BUFFERS)
         before = jnp.maximum(slot - 1, 0)
         at_before = lax.rem(before, BUFFERS)
-        place_b = row_place(1, slot)
-        rows_a = table_ref[row_place(0, slot)] * jnp.asarray(0.5, jnp.bfloat16)
-        rows_c = table_ref[row_place(2, slot)]
+        places_b = row_places(1, slot)
+        rows_a = rows_of(row_places(0, slot)) * jnp.asarray(0.5, jnp.bfloat16)
+        rows_c = rows_of(row_places(2, slot))
         total_before = total_ref[...]
         total = jnp.zeros((edge, rank), jnp.float32)
         for tile in range(tiles):
@@ -195,7 +212,7 @@
                 total_before = finish(tiles - LAG + tile, at_before, total_before)
             pair = jnp.concatenate(
                 [
-                    table_ref[place_b, pl.ds(tile * TILE_J + j, 1), :] * rows_c
+                    row_of(places_b, tile * TILE_J + j) * rows_c
                     for j in range(TILE_J)
                 ],
                 axis=0,
@@ -232,19 +249,20 @@
     row_blocks = row_owner.shape[1]
     dims = mesh_dims(lax.axis_size("blk"), lax.axis_size("grp"))
     shard = factors.astype(jnp.bfloat16).reshape(3 * local_blocks, edge, rank)
-    halves = gather_rows(shard, dims)
-    pieces = halves[0] + halves[1]
+    mains, sides = gather_rows(shard, dims)
+    pieces = mains + sides
     smem = pl.BlockSpec(memory_space=pltpu.SMEM)
     hbm = pl.BlockSpec(memory_space=pl.ANY)
     tiles = edge // TILE_J
     outgoing = jax.ShapeDtypeStruct((row_blocks // 2, edge, rank), jnp.float32)
     mine, other = pl.pallas_call(
-        functools.partial(slots_kernel, dims, local_blocks, len(pieces)),
+        functools.partial(slots_kernel, dims, local_blocks, len(mains), len(pieces)),
         out_shape=(outgoing, outgoing),
         in_specs=[smem, smem, smem, hbm] + [hbm] * len(pieces),
         out_specs=(hbm, hbm),
         scratch_shapes=[
-            pltpu.VMEM((3 * row_blocks, edge, rank), jnp.bfloat16),
+            pltpu.VMEM((3 * row_blocks, edge - SIDE_ROWS, rank), jnp.bfloat16),
+            pltpu.VMEM((3 * row_blocks, SIDE_ROWS, rank), jnp.bfloat16),
             pltpu.VMEM((row_blocks, edge, rank), jnp.float32),
             pltpu.VMEM((BUFFERS, edge, width), jnp.bfloat16),
             pltpu.VMEM((tiles, TILE_J * edge, rank), jnp.bfloat16),

time: 144 us -> 167 us (1.16); the launches traced: 146 us -> 167 us
  between operations: 1.57 us -> 14.9 us
  starting transfers between devices: 41.4 us -> 34.6 us
  waiting for transfers between devices: 68.3 us -> 74.6 us
  Pallas kernels: 29.1 us -> 35.2 us
    all_gather x0 -> x1, waiting for transfers between devices: none -> 16.4 us  [gather_rows(): side = lax.all_gather(shard[:, :SIDE_ROWS], AXES, axis=0, tiled=True)]
    ppermute x19, waiting for transfers between devices: 68.3 us -> 58.2 us  [shift(): return lax.ppermute(values, AXES, perm)]
    ppermute x19, starting transfers between devices: 41.4 us -> 34.6 us  [shift(): return lax.ppermute(values, AXES, perm)]
    pallas_call x1, Pallas kernels: 29.1 us -> 35.2 us  [per_device(): pl.pallas_call(functools.partial(slots_kernel, dims, local_blocks, len(ma...]
  transfers between devices with their start and end apart: 19 -> 20, of which waited for: 13 -> 12; matrix products, arithmetic and copies ran while one was open for 0% -> 0% of each run, Pallas kernels for 0% -> 0%
where the time goes in v5:
time: 167 us
  waiting for transfers between devices  74.6 us (45%)
  Pallas kernels  35.2 us (21%)
  starting transfers between devices  34.6 us (21%)
  between operations  14.9 us (9%)
  other arithmetic  4.9 us (3%)
  local copies, waits for them, and re-layouts  2.52 us (2%)
    ppermute x19, waiting for transfers between devices, shift(): return lax.ppermute(values, AXES, perm)  58.2 us
    pallas_call x1, Pallas kernels, per_device(): pl.pallas_call(functools.partial(slots_kernel, dims, local_blocks, len(ma...  35.2 us
    ppermute x19, starting transfers between devices, shift(): return lax.ppermute(values, AXES, perm)  34.6 us
    all_gather x1, waiting for transfers between devices, gather_rows(): side = lax.all_gather(shard[:, :SIDE_ROWS], AXES, axis=0, tiled=True)  16.4 us
  transfers between devices with their start and end apart: 20, of which 12 were waited for; matrix products, arithmetic and copies ran while one was open for 0% of the time, Pallas kernels for 0%

profile of v5, /device:TPU:0, one launch (start us, length us, event | category | flops | bytes accessed | tf_op | source)
XLA Modules:
  0.0 166.8 jit_solution(4825749634263663415)
XLA Ops:
  8.9 5.1 %collective-permute-start.2 = (bf16[6,48,256]{2,1,0:T(8,128)(2,1)S(1)}, bf16[6,48,256]{2,1,0:T(8,128)(2,1)S(1)}, u32[]{:S(2)}, u32[]{:S(2)}) collective-permute-start(bf16[6,48,256]{2,1,0:T(8,128)(2,1)S(1)} %slice.183), channel_id=1, source_target_pairs={{0,3},{1,0},{2,1},{3,2},{4,7},{5,4},{6,5},{7,6},{8,11},{9,8},{10,9... | collective-permute-start | bytes 442376 | tf_op jit(solution)/shard_map/ppermute | solution.py:55
  15.0 9.4 %collective-permute-done = bf16[6,48,256]{2,1,0:T(8,128)(2,1)S(1)} collective-permute-done((bf16[6,48,256]{2,1,0:T(8,128)(2,1)S(1)}, bf16[6,48,256]{2,1,0:T(8,128)(2,1)S(1)}, u32[]{:S(2)}, u32[]{:S(2)}) %collective-permute-start) | collective-permute-done | bytes 147488 | tf_op jit(solution)/shard_map/ppermute | solution.py:55
  24.5 2.1 %collective-permute-done.1 = bf16[6,48,256]{2,1,0:T(8,128)(2,1)S(1)} collective-permute-done((bf16[6,48,256]{2,1,0:T(8,128)(2,1)S(1)}, bf16[6,48,256]{2,1,0:T(8,128)(2,1)S(1)}, u32[]{:S(2)}, u32[]{:S(2)}) %collective-permute-start.1) | collective-permute-done | bytes 147488 | tf_op jit(solution)/shard_map/ppermute | solution.py:55
  26.7 1.6 collective-permute-start.7
  28.3 1.6 collective-permute-start.3
  29.9 5.1 %collective-permute-done.7 = bf16[12,48,256]{2,1,0:T(8,128)(2,1)S(1)} collective-permute-done((bf16[12,48,256]{2,1,0:T(8,128)(2,1)S(1)}, bf16[12,48,256]{2,1,0:T(8,128)(2,1)S(1)}, u32[]{:S(2)}, u32[]{:S(2)}) %collective-permute-start.7) | collective-permute-done | bytes 294944 | tf_op jit(solution)/shard_map/ppermute | solution.py:55
  35.0 1.6 collective-permute-start.8
  36.6 1.6 collective-permute-start.4
  38.7 10.9 %collective-permute-done.8.refs_9_ = bf16[24,48,256]{2,1,0:T(8,128)(2,1)S(1)} collective-permute-done((bf16[24,48,256]{2,1,0:T(8,128)(2,1)S(1)}, bf16[24,48,256]{2,1,0:T(8,128)(2,1)S(1)}, u32[]{:S(2)}, u32[]{:S(2)}) %collective-permute-start.8) | collective-permute-done | bytes 589856 | tf_op jit(solution)/shard_map/ppermute | solution.py:55
  49.6 1.9 %collective-permute-done.4.refs_5_ = bf16[24,48,256]{2,1,0:T(8,128)(2,1)S(1)} collective-permute-done((bf16[24,48,256]{2,1,0:T(8,128)(2,1)S(1)}, bf16[24,48,256]{2,1,0:T(8,128)(2,1)S(1)}, u32[]{:S(2)}, u32[]{:S(2)}) %collective-permute-start.4) | collective-permute-done | bytes 589856 | tf_op jit(solution)/shard_map/ppermute | solution.py:55
  53.9 16.4 %all-gather.2.cloned.1.call-done.refs_12_ = bf16[192,16,256]{2,1,0:T(8,128)(2,1)} async-done(((bf16[6,16,256]{2,1,0:T(8,128)(2,1)}), bf16[192,16,256]{2,1,0:T(8,128)(2,1)}) %all-gather.2.cloned.1.call-update) | async-done | bytes 1572880 | tf_op jit(solution)/shard_map/all_gather | solution.py:63
  70.3 35.2 %shard_map.94 = (f32[32,64,256]{2,1,0:T(8,128)}, f32[32,64,256]{2,1,0:T(8,128)}) custom-call(s32[3,36]{1,0:T(4,128)} %refs_0_.1, s32[1]{0:T(128)S(6)} %copy.18.refs_1_, s32[3,64]{1,0:T(4,128)} %refs_2_.1, bf16[36,64,4096]{2,1,0:T(8,128)(2,1)} %refs_3_.1, bf16[24,48,256]{2,1,0:T(8,128)(2,1)} %copy-done.2, bf16[24,48,256]{2,1,0:T(8,128)(2,1)} %copy-done.5, ...), custom_call_target="tpu_custom_call" | custom-call | flops 9663676416 | bytes 18874368 | tf_op jit(solution)/shard_map/pallas_call | solution.py:258
  105.7 4.4 %collective-permute-done.11 = f32[32,64,256]{2,1,0:T(8,128)S(1)} collective-permute-done((f32[32,64,256]{2,1,0:T(8,128)}, f32[32,64,256]{2,1,0:T(8,128)S(1)}, u32[]{:S(2)}, u32[]{:S(2)}) %collective-permute-start.11) | collective-permute-done | bytes 2097184 | tf_op jit(solution)/shard_map/ppermute | solution.py:55
  110.0 1.9 %slice_add_fusion.3 = (f32[8,64,256]{2,1,0:T(8,128)S(1)}, f32[8,64,256]{2,1,0:T(8,128)S(1)}, f32[8,64,256]{2,1,0:T(8,128)S(1)}, f32[8,64,256]{2,1,0:T(8,128)S(1)}) fusion(f32[32,64,256]{2,1,0:T(8,128)S(1)} %collective-permute-done.11, f32[32,64,256]{2,1,0:T(8,128)} %get-tuple-element.5), kind=kLoop, calls=%fused_computation.3 | loop fusion | flops 524288 | bytes 6291456 | tf_op jit(solution)/shard_map/add | solution.py:301
  111.9 10.7 %collective-permute-start.12 = (f32[2,4,64,256]{3,2,1,0:T(8,128)S(1)}, f32[2,4,64,256]{3,2,1,0:T(8,128)S(1)}, u32[]{:S(2)}, u32[]{:S(2)}) collective-permute-start(f32[2,4,64,256]{3,2,1,0:T(8,128)S(1)} %bitcast.53), channel_id=1, source_target_pairs={{0,8},{1,9},{2,10},{3,11},{4,12},{5,13},{6,14},{7,15},{8,0},{9,1},... | collective-permute-start | bytes 1572872 | tf_op jit(solution)/shard_map/ppermute | solution.py:55
  122.6 2.3 %collective-permute-start.14 = (f32[2,4,64,256]{3,2,1,0:T(8,128)S(1)}, f32[2,4,64,256]{3,2,1,0:T(8,128)S(1)}, u32[]{:S(2)}, u32[]{:S(2)}) collective-permute-start(f32[2,4,64,256]{3,2,1,0:T(8,128)S(1)} %bitcast.52), channel_id=1, source_target_pairs={{0,16},{1,17},{2,18},{3,19},{4,20},{5,21},{6,22},{7,23},{8,24},{9,... | collective-permute-start | bytes 1572872 | tf_op jit(solution)/shard_map/ppermute | solution.py:55
  124.9 9.9 %collective-permute-done.12 = f32[2,4,64,256]{3,2,1,0:T(8,128)S(1)} collective-permute-done((f32[2,4,64,256]{3,2,1,0:T(8,128)S(1)}, f32[2,4,64,256]{3,2,1,0:T(8,128)S(1)}, u32[]{:S(2)}, u32[]{:S(2)}) %collective-permute-start.12) | collective-permute-done | bytes 524320 | tf_op jit(solution)/shard_map/ppermute | solution.py:55
  134.8 4.3 %collective-permute-start.13 = (f32[4,64,256]{2,1,0:T(8,128)S(1)}, f32[4,64,256]{2,1,0:T(8,128)S(1)}, u32[]{:S(2)}, u32[]{:S(2)}) collective-permute-start(f32[4,64,256]{2,1,0:T(8,128)S(1)} %fusion.3), channel_id=1, source_target_pairs={{0,16},{1,17},{2,18},{3,19},{4,20},{5,21},{6,22},{7,23},{8,24},{9,... | collective-permute-start | bytes 786440 | tf_op jit(solution)/shard_map/ppermute | solution.py:55
  139.5 5.6 %collective-permute-done.13 = f32[4,64,256]{2,1,0:T(8,128)S(1)} collective-permute-done((f32[4,64,256]{2,1,0:T(8,128)S(1)}, f32[4,64,256]{2,1,0:T(8,128)S(1)}, u32[]{:S(2)}, u32[]{:S(2)}) %collective-permute-start.13) | collective-permute-done | bytes 262176 | tf_op jit(solution)/shard_map/ppermute | solution.py:55
  145.2 1.5 collective-permute-done.15
  147.4 2.0 %collective-permute-start.17 = (f32[128,256]{1,0:T(8,128)S(1)}, f32[128,256]{1,0:T(8,128)S(1)}, u32[]{:S(2)}, u32[]{:S(2)}) collective-permute-start(f32[128,256]{1,0:T(8,128)S(1)} %pad_maximum_fusion.3), channel_id=1, source_target_pairs={{0,2},{1,3},{2,0},{3,1},{4,6},{5,7},{6,4},{7,5},{8,10},{9,11},{10,... | collective-permute-start | bytes 393224 | tf_op jit(solution)/shard_map/ppermute | solution.py:55
  150.9 4.3 %collective-permute-done.16 = f32[128,256]{1,0:T(8,128)S(1)} collective-permute-done((f32[128,256]{1,0:T(8,128)S(1)}, f32[128,256]{1,0:T(8,128)S(1)}, u32[]{:S(2)}, u32[]{:S(2)}) %collective-permute-start.16) | collective-permute-done | bytes 131104 | tf_op jit(solution)/shard_map/ppermute | solution.py:55
  155.2 3.1 %collective-permute-done.17 = f32[128,256]{1,0:T(8,128)S(1)} collective-permute-done((f32[128,256]{1,0:T(8,128)S(1)}, f32[128,256]{1,0:T(8,128)S(1)}, u32[]{:S(2)}, u32[]{:S(2)}) %collective-permute-start.17) | collective-permute-done | bytes 131104 | tf_op jit(solution)/shard_map/ppermute | solution.py:55
  158.3 1.7 %bitcast_subtract_fusion = (f32[128,256]{1,0:T(8,128)}, f32[128,256]{1,0:T(8,128)}, f32[128,256]{1,0:T(8,128)}) fusion(f32[3,128,256]{2,1,0:T(8,128)} %param.11, f32[128,256]{1,0:T(8,128)S(1)} %copy-done, f32[128,256]{1,0:T(8,128)S(1)} %copy-done.1, f32[128,256]{1,0:T(8,128)S(1)} %collective-permute-done.18, f32[128,256]{1,0:T(8,128)S(1)} %collective-permute-done.17, ...), kind=kLoop, calls=%fused_computation.28 | loop fusion | flops 524288 | bytes 1310720 | tf_op jit(solution)/shard_map/sub | solution.py:312
  (58 shorter events, 7.9 us)
Async XLA Ops:
  7.2 63.2 %all-gather.2.cloned.1.call-start = ((), (), s32[]{:S(2)}) async-start(), calls=%async_computation | async-start | bytes 1622016 | tf_op jit(solution)/shard_map/all_gather | solution.py:63
  8.9 17.7 %collective-permute-start.2 = (bf16[6,48,256]{2,1,0:T(8,128)(2,1)S(1)}, bf16[6,48,256]{2,1,0:T(8,128)(2,1)S(1)}, u32[]{:S(2)}, u32[]{:S(2)}) collective-permute-start(bf16[6,48,256]{2,1,0:T(8,128)(2,1)S(1)} %slice.183), channel_id=1, source_target_pairs={{0,3},{1,0},{2,1},{3,2},{4,7},{5,4},{6,5},{7,6},{8,11},{9,8},{10,9... | collective-permute-start | bytes 442376 | tf_op jit(solution)/shard_map/ppermute | solution.py:55
  14.0 12.6 %collective-permute-start.1 = (bf16[6,48,256]{2,1,0:T(8,128)(2,1)S(1)}, bf16[6,48,256]{2,1,0:T(8,128)(2,1)S(1)}, u32[]{:S(2)}, u32[]{:S(2)}) collective-permute-start(bf16[6,48,256]{2,1,0:T(8,128)(2,1)S(1)} %slice.183), channel_id=1, source_target_pairs={{0,2},{1,3},{2,0},{3,1},{4,6},{5,7},{6,4},{7,5},{8,10},{9,11},{10,... | collective-permute-start | bytes 442376 | tf_op jit(solution)/shard_map/ppermute | solution.py:55
  14.0 10.4 %collective-permute-start = (bf16[6,48,256]{2,1,0:T(8,128)(2,1)S(1)}, bf16[6,48,256]{2,1,0:T(8,128)(2,1)S(1)}, u32[]{:S(2)}, u32[]{:S(2)}) collective-permute-start(bf16[6,48,256]{2,1,0:T(8,128)(2,1)S(1)} %slice.183), channel_id=1, source_target_pairs={{0,1},{1,2},{2,3},{3,0},{4,5},{5,6},{6,7},{7,4},{8,9},{9,10},{10,1... | collective-permute-start | bytes 442376 | tf_op jit(solution)/shard_map/ppermute | solution.py:55
  26.7 8.2 %collective-permute-start.7 = (bf16[12,48,256]{2,1,0:T(8,128)(2,1)S(1)}, bf16[12,48,256]{2,1,0:T(8,128)(2,1)S(1)}, u32[]{:S(2)}, u32[]{:S(2)}) collective-permute-start(bf16[12,48,256]{2,1,0:T(8,128)(2,1)S(1)} %pad_maximum_fusion.1), channel_id=1, source_target_pairs={{0,8},{1,9},{2,10},{3,11},{4,12},{5,13},{6,14},{7,15},{8,0},{9,1},... | collective-permute-start | bytes 884744 | tf_op jit(solution)/shard_map/ppermute | solution.py:55
  28.3 8.3 %collective-permute-start.3 = (bf16[12,48,256]{2,1,0:T(8,128)(2,1)S(1)}, bf16[12,48,256]{2,1,0:T(8,128)(2,1)S(1)}, u32[]{:S(2)}, u32[]{:S(2)}) collective-permute-start(bf16[12,48,256]{2,1,0:T(8,128)(2,1)S(1)} %pad_maximum_fusion), channel_id=1, source_target_pairs={{0,16},{1,17},{2,18},{3,19},{4,20},{5,21},{6,22},{7,23},{8,24},{9,... | collective-permute-start | bytes 884744 | tf_op jit(solution)/shard_map/ppermute | solution.py:55
  35.0 35.3 %copy-start.3 = (bf16[24,48,256]{2,1,0:T(8,128)(2,1)}, bf16[24,48,256]{2,1,0:T(8,128)(2,1)S(1)}, u32[]{:S(2)}) copy-start(bf16[24,48,256]{2,1,0:T(8,128)(2,1)S(1)} %constant_dynamic-update-slice_fusion.5.refs_8_) | copy-start | bytes 1769476
  35.0 14.6 %collective-permute-start.8 = (bf16[24,48,256]{2,1,0:T(8,128)(2,1)S(1)}, bf16[24,48,256]{2,1,0:T(8,128)(2,1)S(1)}, u32[]{:S(2)}, u32[]{:S(2)}) collective-permute-start(bf16[24,48,256]{2,1,0:T(8,128)(2,1)S(1)} %constant_dynamic-update-slice_fusion.5.refs_8_), channel_id=1, source_target_pairs={{0,16},{1,17},{2,18},{3,19},{4,20},{5,21},{6,22},{7,23},{8,24},{9,... | collective-permute-start | bytes 1769480 | tf_op jit(solution)/shard_map/ppermute | solution.py:55
  36.6 33.7 %copy-start.2 = (bf16[24,48,256]{2,1,0:T(8,128)(2,1)}, bf16[24,48,256]{2,1,0:T(8,128)(2,1)S(1)}, u32[]{:S(2)}) copy-start(bf16[24,48,256]{2,1,0:T(8,128)(2,1)S(1)} %constant_dynamic-update-slice_fusion.refs_4_) | copy-start | bytes 1769476
  36.6 14.9 %collective-permute-start.4 = (bf16[24,48,256]{2,1,0:T(8,128)(2,1)S(1)}, bf16[24,48,256]{2,1,0:T(8,128)(2,1)S(1)}, u32[]{:S(2)}, u32[]{:S(2)}) collective-permute-start(bf16[24,48,256]{2,1,0:T(8,128)(2,1)S(1)} %constant_dynamic-update-slice_fusion.refs_4_), channel_id=1, source_target_pairs={{0,8},{1,9},{2,10},{3,11},{4,12},{5,13},{6,14},{7,15},{8,0},{9,1},... | collective-permute-start | bytes 1769480 | tf_op jit(solution)/shard_map/ppermute | solution.py:55
  38.2 14.0 %collective-permute-start.9 = (bf16[24,48,256]{2,1,0:T(8,128)(2,1)S(1)}, bf16[24,48,256]{2,1,0:T(8,128)(2,1)S(1)}, u32[]{:S(2)}, u32[]{:S(2)}) collective-permute-start(bf16[24,48,256]{2,1,0:T(8,128)(2,1)S(1)} %constant_dynamic-update-slice_fusion.5.refs_8_), channel_id=1, source_target_pairs={{0,4},{1,5},{2,6},{3,7},{4,0},{5,1},{6,2},{7,3},{8,12},{9,13},{10,... | collective-permute-start | bytes 1769480 | tf_op jit(solution)/shard_map/ppermute | solution.py:55
  38.2 14.0 %collective-permute-start.5 = (bf16[24,48,256]{2,1,0:T(8,128)(2,1)S(1)}, bf16[24,48,256]{2,1,0:T(8,128)(2,1)S(1)}, u32[]{:S(2)}, u32[]{:S(2)}) collective-permute-start(bf16[24,48,256]{2,1,0:T(8,128)(2,1)S(1)} %constant_dynamic-update-slice_fusion.refs_4_), channel_id=1, source_target_pairs={{0,4},{1,5},{2,6},{3,7},{4,0},{5,1},{6,2},{7,3},{8,12},{9,13},{10,... | collective-permute-start | bytes 1769480 | tf_op jit(solution)/shard_map/ppermute | solution.py:55
  49.6 20.7 %copy-start.4 = (bf16[24,48,256]{2,1,0:T(8,128)(2,1)}, bf16[24,48,256]{2,1,0:T(8,128)(2,1)S(1)}, u32[]{:S(2)}) copy-start(bf16[24,48,256]{2,1,0:T(8,128)(2,1)S(1)} %collective-permute-done.8.refs_9_) | copy-start | bytes 1769476
  49.6 2.6 %collective-permute-start.10 = (bf16[24,48,256]{2,1,0:T(8,128)(2,1)S(1)}, bf16[24,48,256]{2,1,0:T(8,128)(2,1)S(1)}, u32[]{:S(2)}, u32[]{:S(2)}) collective-permute-start(bf16[24,48,256]{2,1,0:T(8,128)(2,1)S(1)} %collective-permute-done.8.refs_9_), channel_id=1, source_target_pairs={{0,4},{1,5},{2,6},{3,7},{4,0},{5,1},{6,2},{7,3},{8,12},{9,13},{10,... | collective-permute-start | bytes 1769480 | tf_op jit(solution)/shard_map/ppermute | solution.py:55
  51.5 2.4 %collective-permute-start.6 = (bf16[24,48,256]{2,1,0:T(8,128)(2,1)S(1)}, bf16[24,48,256]{2,1,0:T(8,128)(2,1)}, u32[]{:S(2)}, u32[]{:S(2)}) collective-permute-start(bf16[24,48,256]{2,1,0:T(8,128)(2,1)S(1)} %collective-permute-done.4.refs_5_), channel_id=1, source_target_pairs={{0,4},{1,5},{2,6},{3,7},{4,0},{5,1},{6,2},{7,3},{8,12},{9,13},{10,... | collective-permute-start | bytes 1769480 | tf_op jit(solution)/shard_map/ppermute | solution.py:55
  105.6 4.4 %collective-permute-start.11 = (f32[32,64,256]{2,1,0:T(8,128)}, f32[32,64,256]{2,1,0:T(8,128)S(1)}, u32[]{:S(2)}, u32[]{:S(2)}) collective-permute-start(f32[32,64,256]{2,1,0:T(8,128)} %get-tuple-element.6), channel_id=1, source_target_pairs={{0,4},{1,5},{2,6},{3,7},{4,0},{5,1},{6,2},{7,3},{8,12},{9,13},{10,... | collective-permute-start | bytes 6291464 | tf_op jit(solution)/shard_map/ppermute | solution.py:55
  111.9 22.9 %collective-permute-start.12 = (f32[2,4,64,256]{3,2,1,0:T(8,128)S(1)}, f32[2,4,64,256]{3,2,1,0:T(8,128)S(1)}, u32[]{:S(2)}, u32[]{:S(2)}) collective-permute-start(f32[2,4,64,256]{3,2,1,0:T(8,128)S(1)} %bitcast.53), channel_id=1, source_target_pairs={{0,8},{1,9},{2,10},{3,11},{4,12},{5,13},{6,14},{7,15},{8,0},{9,1},... | collective-permute-start | bytes 1572872 | tf_op jit(solution)/shard_map/ppermute | solution.py:55
  122.6 16.5 %collective-permute-start.14 = (f32[2,4,64,256]{3,2,1,0:T(8,128)S(1)}, f32[2,4,64,256]{3,2,1,0:T(8,128)S(1)}, u32[]{:S(2)}, u32[]{:S(2)}) collective-permute-start(f32[2,4,64,256]{3,2,1,0:T(8,128)S(1)} %bitcast.52), channel_id=1, source_target_pairs={{0,16},{1,17},{2,18},{3,19},{4,20},{5,21},{6,22},{7,23},{8,24},{9,... | collective-permute-start | bytes 1572872 | tf_op jit(solution)/shard_map/ppermute | solution.py:55
  134.8 10.3 %collective-permute-start.13 = (f32[4,64,256]{2,1,0:T(8,128)S(1)}, f32[4,64,256]{2,1,0:T(8,128)S(1)}, u32[]{:S(2)}, u32[]{:S(2)}) collective-permute-start(f32[4,64,256]{2,1,0:T(8,128)S(1)} %fusion.3), channel_id=1, source_target_pairs={{0,16},{1,17},{2,18},{3,19},{4,20},{5,21},{6,22},{7,23},{8,24},{9,... | collective-permute-start | bytes 786440 | tf_op jit(solution)/shard_map/ppermute | solution.py:55
  139.1 19.1 %copy-start = (f32[128,256]{1,0:T(8,128)S(1)}, f32[128,256]{1,0:T(8,128)}, u32[]{:S(2)}) copy-start(f32[128,256]{1,0:T(8,128)} %param.12) | copy-start | bytes 393220
  139.2 7.6 %collective-permute-start.15 = (f32[4,64,256]{2,1,0:T(8,128)S(1)}, f32[4,64,256]{2,1,0:T(8,128)S(1)}, u32[]{:S(2)}, u32[]{:S(2)}) collective-permute-start(f32[4,64,256]{2,1,0:T(8,128)S(1)} %fusion), channel_id=1, source_target_pairs={{0,8},{1,9},{2,10},{3,11},{4,12},{5,13},{6,14},{7,15},{8,0},{9,1},... | collective-permute-start | bytes 786440 | tf_op jit(solution)/shard_map/ppermute | solution.py:55
  146.8 8.3 %collective-permute-start.16 = (f32[128,256]{1,0:T(8,128)S(1)}, f32[128,256]{1,0:T(8,128)S(1)}, u32[]{:S(2)}, u32[]{:S(2)}) collective-permute-start(f32[128,256]{1,0:T(8,128)S(1)} %pad_maximum_fusion.2), channel_id=1, source_target_pairs={{0,1},{1,2},{2,3},{3,0},{4,5},{5,6},{6,7},{7,4},{8,9},{9,10},{10,1... | collective-permute-start | bytes 393224 | tf_op jit(solution)/shard_map/ppermute | solution.py:55
  147.4 10.9 %collective-permute-start.17 = (f32[128,256]{1,0:T(8,128)S(1)}, f32[128,256]{1,0:T(8,128)S(1)}, u32[]{:S(2)}, u32[]{:S(2)}) collective-permute-start(f32[128,256]{1,0:T(8,128)S(1)} %pad_maximum_fusion.3), channel_id=1, source_target_pairs={{0,2},{1,3},{2,0},{3,1},{4,6},{5,7},{6,4},{7,5},{8,10},{9,11},{10,... | collective-permute-start | bytes 393224 | tf_op jit(solution)/shard_map/ppermute | solution.py:55
  149.4 8.9 %collective-permute-start.18 = (f32[128,256]{1,0:T(8,128)S(1)}, f32[128,256]{1,0:T(8,128)S(1)}, u32[]{:S(2)}, u32[]{:S(2)}) collective-permute-start(f32[128,256]{1,0:T(8,128)S(1)} %pad_maximum_fusion.4), channel_id=1, source_target_pairs={{0,3},{1,0},{2,1},{3,2},{4,7},{5,4},{6,5},{7,6},{8,11},{9,8},{10,9... | collective-permute-start | bytes 393224 | tf_op jit(solution)/shard_map/ppermute | solution.py:55
  (5 other events, 57.8 us)
Sparse Core Ops, SparseCore 0:
  11.4 58.8 all-gather.1

commit v6 on v4

--- a/solution.py
+++ b/solution.py
@@ -12,8 +12,8 @@
 BUFFERS = 5
 AHEAD = 3
 COPY_PARTS = 4
-TILE_J = 16
-LAG = 1
+TILE_J = 8
+QUARTERS = 4
 
 
 def mesh_dims(blk, grp):
@@ -81,6 +81,7 @@
         grad_ref,
         blocks_buf,
         pair_ref,
+        weight_ref,
         model_ref,
         total_ref,
         block_sems,
@@ -89,7 +90,7 @@
     ) = refs[4 + piece_count :]
     edge, rank = grad_ref.shape[1], grad_ref.shape[2]
     width = TILE_J * edge
-    tiles = edge // TILE_J
+    tiles = edge // (QUARTERS * TILE_J)
     count = count_ref[0]
     cut = 3 * local_blocks // 2
     here = split_index(lax.axis_index("blk") * dims["line"] + lax.axis_index("grp"), dims)
@@ -164,17 +165,28 @@
     for slot in range(AHEAD):
         start(slot)
     grad_ref[...] = jnp.zeros_like(grad_ref)
-    for tile in range(tiles - LAG, tiles):
-        pair_ref[tile] = jnp.zeros((width, rank), jnp.bfloat16)
-        model_ref[tile] = jnp.zeros((edge, width), jnp.float32)
+    pair_ref[tiles - 1] = jnp.zeros(pair_ref.shape[1:], pair_ref.dtype)
+    model_ref[tiles - 1] = jnp.zeros(model_ref.shape[1:], model_ref.dtype)
+    weight_ref[...] = jnp.zeros_like(weight_ref)
     total_ref[...] = jnp.zeros_like(total_ref)
     for fill in fills:
         fill.wait()
 
+    quarter = edge * edge // QUARTERS
+    lanes = lax.broadcasted_iota(jnp.int32, (rank, 2 * edge), 1)
+
     def finish(tile, at, total):
-        twice = blocks_buf[at, :, tile * width : (tile + 1) * width].astype(jnp.float32) * 2.0
-        resid = ((jnp.tanh(model_ref[tile]) + 1.0) - twice).astype(jnp.bfloat16)
-        return total + jnp.dot(resid, pair_ref[tile], preferred_element_type=jnp.float32)
+        model = model_ref[tile].T
+        for q in range(QUARTERS):
+            begin = q * quarter + tile * width
+            twice = blocks_buf[at, :, begin : begin + width].astype(jnp.float32) * 2.0
+            resid = ((jnp.tanh(model[q * edge : (q + 1) * edge]) + 1.0) - twice).astype(jnp.bfloat16)
+            total = total + jnp.dot(
+                resid,
+                pair_ref[tile, :, q * rank : (q + 1) * rank],
+                preferred_element_type=jnp.float32,
+            )
+        return total
 
     def step(slot, carry):
         start(slot + AHEAD)
@@ -184,25 +196,32 @@
         before = jnp.maximum(slot - 1, 0)
         at_before = lax.rem(before, BUFFERS)
         place_b = row_place(1, slot)
-        rows_a = table_ref[row_place(0, slot)] * jnp.asarray(0.5, jnp.bfloat16)
+        rows_a = table_ref[row_place(0, slot)].astype(jnp.float32) * 0.5
+        twice_a = jnp.concatenate([rows_a, rows_a], axis=0).T
+        for q in range(QUARTERS):
+            keep = (lanes < edge) if q % 2 == 0 else (lanes >= edge)
+            lane = q // 2 * 2 * edge
+            weight_ref[q * rank : (q + 1) * rank, lane : lane + 2 * edge] = jnp.where(
+                keep, twice_a, 0.0
+            ).astype(jnp.bfloat16)
         rows_c = table_ref[row_place(2, slot)]
         total_before = total_ref[...]
         total = jnp.zeros((edge, rank), jnp.float32)
         for tile in range(tiles):
-            if tile >= LAG:
-                total = finish(tile - LAG, at, total)
+            if tile == 0:
+                total_before = finish(tiles - 1, at_before, total_before)
             else:
-                total_before = finish(tiles - LAG + tile, at_before, total_before)
-            pair = jnp.concatenate(
-                [
-                    table_ref[place_b, pl.ds(tile * TILE_J + j, 1), :] * rows_c
-                    for j in range(TILE_J)
-                ],
-                axis=0,
-            )
-            pair_ref[tile] = pair
-            model_ref[tile] = lax.dot_general(
-                rows_a, pair, (((1,), (1,)), ((), ())), preferred_element_type=jnp.float32
+                total = finish(tile - 1, at, total)
+            for q in range(QUARTERS):
+                for j in range(TILE_J):
+                    row = table_ref[
+                        place_b, pl.ds(q * (edge // QUARTERS) + tile * TILE_J + j, 1), :
+                    ]
+                    pair_ref[tile, j * edge : (j + 1) * edge, q * rank : (q + 1) * rank] = (
+                        row * rows_c
+                    )
+            model_ref[tile] = jnp.dot(
+                pair_ref[tile], weight_ref[...], preferred_element_type=jnp.float32
             )
         grad_ref[grad_place(before)] += 0.5 * total_before
         total_ref[...] = total
@@ -210,10 +229,7 @@
 
     lax.fori_loop(0, count, step, 0)
     last = count - 1
-    total = total_ref[...]
-    for tile in range(tiles - LAG, tiles):
-        total = finish(tile, lax.rem(last, BUFFERS), total)
-    grad_ref[grad_place(last)] += 0.5 * total
+    grad_ref[grad_place(last)] += 0.5 * finish(tiles - 1, lax.rem(last, BUFFERS), total_ref[...])
     half = grad_ref.shape[0] // 2
     for index, out in enumerate((mine_ref, other_ref)):
         pltpu.make_async_copy(
@@ -236,7 +252,7 @@
     pieces = halves[0] + halves[1]
     smem = pl.BlockSpec(memory_space=pltpu.SMEM)
     hbm = pl.BlockSpec(memory_space=pl.ANY)
-    tiles = edge // TILE_J
+    tiles = edge // (QUARTERS * TILE_J)
     outgoing = jax.ShapeDtypeStruct((row_blocks // 2, edge, rank), jnp.float32)
     mine, other = pl.pallas_call(
         functools.partial(slots_kernel, dims, local_blocks, len(pieces)),
@@ -247,8 +263,9 @@
             pltpu.VMEM((3 * row_blocks, edge, rank), jnp.bfloat16),
             pltpu.VMEM((row_blocks, edge, rank), jnp.float32),
             pltpu.VMEM((BUFFERS, edge, width), jnp.bfloat16),
-            pltpu.VMEM((tiles, TILE_J * edge, rank), jnp.bfloat16),
-            pltpu.VMEM((tiles, edge, TILE_J * edge), jnp.float32),
+            pltpu.VMEM((tiles, TILE_J * edge, QUARTERS * rank), jnp.bfloat16),
+            pltpu.VMEM((QUARTERS * rank, QUARTERS * edge), jnp.bfloat16),
+            pltpu.VMEM((tiles, TILE_J * edge, QUARTERS * edge), jnp.float32),
             pltpu.VMEM((edge, rank), jnp.float32),
             pltpu.SemaphoreType.DMA((BUFFERS, COPY_PARTS)),
             pltpu.SemaphoreType.DMA((len(pieces),)),

time: 144 us -> 163 us (1.13); the launches traced: 146 us -> 162 us
  Pallas kernels: 29.1 us -> 48.5 us
  starting transfers between devices: 41.4 us -> 38.2 us
    pallas_call x1, Pallas kernels: 29.1 us -> 48.5 us  [per_device(): pl.pallas_call(functools.partial(slots_kernel, dims, local_blocks, len(pi...]
    ppermute x19, starting transfers between devices: 41.4 us -> 38.2 us  [shift(): return lax.ppermute(values, AXES, perm)]
where the time goes in v6:
time: 163 us; the launch traced here: 162 us
  waiting for transfers between devices  67.5 us (41%)
  Pallas kernels  48.5 us (30%)
  starting transfers between devices  38.2 us (23%)
  other arithmetic  4.92 us (3%)
    ppermute x19, waiting for transfers between devices, shift(): return lax.ppermute(values, AXES, perm)  67.5 us
    pallas_call x1, Pallas kernels, per_device(): pl.pallas_call(functools.partial(slots_kernel, dims, local_blocks, len(pi...  48.5 us
    ppermute x19, starting transfers between devices, shift(): return lax.ppermute(values, AXES, perm)  38.2 us
  transfers between devices with their start and end apart: 19, of which 13 were waited for; matrix products, arithmetic and copies ran while one was open for 0% of the time, Pallas kernels for 0%

profile of v6, /device:TPU:0, one launch (start us, length us, event | category | flops | bytes accessed | tf_op | source)
XLA Modules:
  0.0 161.8 jit_solution(4798556931345930315)
XLA Ops:
  0.6 1.0 convert_element_type.3
  1.7 5.1 %collective-permute-start.2 = (bf16[6,64,256]{2,1,0:T(8,128)(2,1)S(1)}, bf16[6,64,256]{2,1,0:T(8,128)(2,1)S(1)}, u32[]{:S(2)}, u32[]{:S(2)}) collective-permute-start(bf16[6,64,256]{2,1,0:T(8,128)(2,1)S(1)} %bitcast.49), channel_id=1, source_target_pairs={{0,3},{1,0},{2,1},{3,2},{4,7},{5,4},{6,5},{7,6},{8,11},{9,8},{10,9... | collective-permute-start | bytes 589832 | tf_op jit(solution)/shard_map/ppermute | solution.py:54
  7.8 12.5 %collective-permute-done = bf16[6,64,256]{2,1,0:T(8,128)(2,1)S(1)} collective-permute-done((bf16[6,64,256]{2,1,0:T(8,128)(2,1)S(1)}, bf16[6,64,256]{2,1,0:T(8,128)(2,1)S(1)}, u32[]{:S(2)}, u32[]{:S(2)}) %collective-permute-start) | collective-permute-done | bytes 196640 | tf_op jit(solution)/shard_map/ppermute | solution.py:54
  20.4 3.1 %collective-permute-done.1 = bf16[6,64,256]{2,1,0:T(8,128)(2,1)S(1)} collective-permute-done((bf16[6,64,256]{2,1,0:T(8,128)(2,1)S(1)}, bf16[6,64,256]{2,1,0:T(8,128)(2,1)S(1)}, u32[]{:S(2)}, u32[]{:S(2)}) %collective-permute-start.1) | collective-permute-done | bytes 196640 | tf_op jit(solution)/shard_map/ppermute | solution.py:54
  23.6 1.6 collective-permute-start.7
  25.2 1.6 collective-permute-start.3
  26.8 7.1 %collective-permute-done.7 = bf16[12,64,256]{2,1,0:T(8,128)(2,1)S(1)} collective-permute-done((bf16[12,64,256]{2,1,0:T(8,128)(2,1)S(1)}, bf16[12,64,256]{2,1,0:T(8,128)(2,1)S(1)}, u32[]{:S(2)}, u32[]{:S(2)}) %collective-permute-start.7) | collective-permute-done | bytes 393248 | tf_op jit(solution)/shard_map/ppermute | solution.py:54
  33.9 1.6 collective-permute-start.8
  35.5 1.5 collective-permute-start.4
  37.6 14.4 %collective-permute-done.8.refs_9_ = bf16[24,64,256]{2,1,0:T(8,128)(2,1)S(1)} collective-permute-done((bf16[24,64,256]{2,1,0:T(8,128)(2,1)S(1)}, bf16[24,64,256]{2,1,0:T(8,128)(2,1)S(1)}, u32[]{:S(2)}, u32[]{:S(2)}) %collective-permute-start.8) | collective-permute-done | bytes 786464 | tf_op jit(solution)/shard_map/ppermute | solution.py:54
  54.3 1.1 collective-permute-done.6.refs_7_
  56.4 48.5 %shard_map.94 = (f32[32,64,256]{2,1,0:T(8,128)}, f32[32,64,256]{2,1,0:T(8,128)}) custom-call(s32[3,36]{1,0:T(4,128)} %refs_0_.1, s32[1]{0:T(128)S(6)} %copy.18.refs_1_, s32[3,64]{1,0:T(4,128)} %refs_2_.1, bf16[36,64,4096]{2,1,0:T(8,128)(2,1)} %refs_3_.1, bf16[24,64,256]{2,1,0:T(8,128)(2,1)} %copy-done.2, bf16[24,64,256]{2,1,0:T(8,128)(2,1)} %copy-done.5, ...), custom_call_target="tpu_custom_call" | custom-call | flops 9663676416 | bytes 18874368 | tf_op jit(solution)/shard_map/pallas_call | solution.py:257
  104.9 3.4 %collective-permute-start.11 = (f32[32,64,256]{2,1,0:T(8,128)}, f32[32,64,256]{2,1,0:T(8,128)S(1)}, u32[]{:S(2)}, u32[]{:S(2)}) collective-permute-start(f32[32,64,256]{2,1,0:T(8,128)} %get-tuple-element.6), channel_id=1, source_target_pairs={{0,4},{1,5},{2,6},{3,7},{4,0},{5,1},{6,2},{7,3},{8,12},{9,13},{10,... | collective-permute-start | bytes 6291464 | tf_op jit(solution)/shard_map/ppermute | solution.py:54
  108.3 4.0 %collective-permute-done.11 = f32[32,64,256]{2,1,0:T(8,128)S(1)} collective-permute-done((f32[32,64,256]{2,1,0:T(8,128)}, f32[32,64,256]{2,1,0:T(8,128)S(1)}, u32[]{:S(2)}, u32[]{:S(2)}) %collective-permute-start.11) | collective-permute-done | bytes 2097184 | tf_op jit(solution)/shard_map/ppermute | solution.py:54
  112.3 1.9 %slice_add_fusion.3 = (f32[8,64,256]{2,1,0:T(8,128)S(1)}, f32[8,64,256]{2,1,0:T(8,128)S(1)}, f32[8,64,256]{2,1,0:T(8,128)S(1)}, f32[8,64,256]{2,1,0:T(8,128)S(1)}) fusion(f32[32,64,256]{2,1,0:T(8,128)S(1)} %collective-permute-done.11, f32[32,64,256]{2,1,0:T(8,128)} %get-tuple-element.5), kind=kLoop, calls=%fused_computation.3 | loop fusion | flops 524288 | bytes 6291456 | tf_op jit(solution)/shard_map/add | solution.py:300
  114.1 6.5 %collective-permute-start.12 = (f32[2,4,64,256]{3,2,1,0:T(8,128)S(1)}, f32[2,4,64,256]{3,2,1,0:T(8,128)S(1)}, u32[]{:S(2)}, u32[]{:S(2)}) collective-permute-start(f32[2,4,64,256]{3,2,1,0:T(8,128)S(1)} %bitcast.54), channel_id=1, source_target_pairs={{0,8},{1,9},{2,10},{3,11},{4,12},{5,13},{6,14},{7,15},{8,0},{9,1},... | collective-permute-start | bytes 1572872 | tf_op jit(solution)/shard_map/ppermute | solution.py:54
  120.6 12.2 %collective-permute-done.12 = f32[2,4,64,256]{3,2,1,0:T(8,128)S(1)} collective-permute-done((f32[2,4,64,256]{3,2,1,0:T(8,128)S(1)}, f32[2,4,64,256]{3,2,1,0:T(8,128)S(1)}, u32[]{:S(2)}, u32[]{:S(2)}) %collective-permute-start.12) | collective-permute-done | bytes 524320 | tf_op jit(solution)/shard_map/ppermute | solution.py:54
  133.0 1.3 collective-permute-done.14
  134.8 5.9 %collective-permute-done.13 = f32[4,64,256]{2,1,0:T(8,128)S(1)} collective-permute-done((f32[4,64,256]{2,1,0:T(8,128)S(1)}, f32[4,64,256]{2,1,0:T(8,128)S(1)}, u32[]{:S(2)}, u32[]{:S(2)}) %collective-permute-start.13) | collective-permute-done | bytes 262176 | tf_op jit(solution)/shard_map/ppermute | solution.py:54
  141.7 8.3 %collective-permute-start.16 = (f32[128,256]{1,0:T(8,128)S(1)}, f32[128,256]{1,0:T(8,128)S(1)}, u32[]{:S(2)}, u32[]{:S(2)}) collective-permute-start(f32[128,256]{1,0:T(8,128)S(1)} %pad_maximum_fusion.2), channel_id=1, source_target_pairs={{0,1},{1,2},{2,3},{3,0},{4,5},{5,6},{6,7},{7,4},{8,9},{9,10},{10,1... | collective-permute-start | bytes 393224 | tf_op jit(solution)/shard_map/ppermute | solution.py:54
  150.1 3.6 %collective-permute-start.17 = (f32[128,256]{1,0:T(8,128)S(1)}, f32[128,256]{1,0:T(8,128)S(1)}, u32[]{:S(2)}, u32[]{:S(2)}) collective-permute-start(f32[128,256]{1,0:T(8,128)S(1)} %pad_maximum_fusion.3), channel_id=1, source_target_pairs={{0,2},{1,3},{2,0},{3,1},{4,6},{5,7},{6,4},{7,5},{8,10},{9,11},{10,... | collective-permute-start | bytes 393224 | tf_op jit(solution)/shard_map/ppermute | solution.py:54
  153.7 3.0 %collective-permute-start.18 = (f32[128,256]{1,0:T(8,128)S(1)}, f32[128,256]{1,0:T(8,128)S(1)}, u32[]{:S(2)}, u32[]{:S(2)}) collective-permute-start(f32[128,256]{1,0:T(8,128)S(1)} %pad_maximum_fusion.4), channel_id=1, source_target_pairs={{0,3},{1,0},{2,1},{3,2},{4,7},{5,4},{6,5},{7,6},{8,11},{9,8},{10,9... | collective-permute-start | bytes 393224 | tf_op jit(solution)/shard_map/ppermute | solution.py:54
  156.7 3.4 %collective-permute-done.17 = f32[128,256]{1,0:T(8,128)S(1)} collective-permute-done((f32[128,256]{1,0:T(8,128)S(1)}, f32[128,256]{1,0:T(8,128)S(1)}, u32[]{:S(2)}, u32[]{:S(2)}) %collective-permute-start.17) | collective-permute-done | bytes 131104 | tf_op jit(solution)/shard_map/ppermute | solution.py:54
  160.1 1.7 %bitcast_subtract_fusion = (f32[128,256]{1,0:T(8,128)}, f32[128,256]{1,0:T(8,128)}, f32[128,256]{1,0:T(8,128)}) fusion(f32[3,128,256]{2,1,0:T(8,128)} %param.11, f32[128,256]{1,0:T(8,128)S(1)} %copy-done, f32[128,256]{1,0:T(8,128)S(1)} %copy-done.1, f32[128,256]{1,0:T(8,128)S(1)} %collective-permute-done.18, f32[128,256]{1,0:T(8,128)S(1)} %collective-permute-done.17, ...), kind=kLoop, calls=%fused_computation.28 | loop fusion | flops 524288 | bytes 1310720 | tf_op jit(solution)/shard_map/sub | solution.py:311
  (55 shorter events, 5.9 us)
Async XLA Ops:
  1.7 21.8 %collective-permute-start.2 = (bf16[6,64,256]{2,1,0:T(8,128)(2,1)S(1)}, bf16[6,64,256]{2,1,0:T(8,128)(2,1)S(1)}, u32[]{:S(2)}, u32[]{:S(2)}) collective-permute-start(bf16[6,64,256]{2,1,0:T(8,128)(2,1)S(1)} %bitcast.49), channel_id=1, source_target_pairs={{0,3},{1,0},{2,1},{3,2},{4,7},{5,4},{6,5},{7,6},{8,11},{9,8},{10,9... | collective-permute-start | bytes 589832 | tf_op jit(solution)/shard_map/ppermute | solution.py:54
  6.8 16.7 %collective-permute-start.1 = (bf16[6,64,256]{2,1,0:T(8,128)(2,1)S(1)}, bf16[6,64,256]{2,1,0:T(8,128)(2,1)S(1)}, u32[]{:S(2)}, u32[]{:S(2)}) collective-permute-start(bf16[6,64,256]{2,1,0:T(8,128)(2,1)S(1)} %bitcast.50), channel_id=1, source_target_pairs={{0,2},{1,3},{2,0},{3,1},{4,6},{5,7},{6,4},{7,5},{8,10},{9,11},{10,... | collective-permute-start | bytes 589832 | tf_op jit(solution)/shard_map/ppermute | solution.py:54
  6.8 13.6 %collective-permute-start = (bf16[6,64,256]{2,1,0:T(8,128)(2,1)S(1)}, bf16[6,64,256]{2,1,0:T(8,128)(2,1)S(1)}, u32[]{:S(2)}, u32[]{:S(2)}) collective-permute-start(bf16[6,64,256]{2,1,0:T(8,128)(2,1)S(1)} %bitcast.51), channel_id=1, source_target_pairs={{0,1},{1,2},{2,3},{3,0},{4,5},{5,6},{6,7},{7,4},{8,9},{9,10},{10,1... | collective-permute-start | bytes 589832 | tf_op jit(solution)/shard_map/ppermute | solution.py:54
  23.6 10.3 %collective-permute-start.7 = (bf16[12,64,256]{2,1,0:T(8,128)(2,1)S(1)}, bf16[12,64,256]{2,1,0:T(8,128)(2,1)S(1)}, u32[]{:S(2)}, u32[]{:S(2)}) collective-permute-start(bf16[12,64,256]{2,1,0:T(8,128)(2,1)S(1)} %pad_maximum_fusion.1), channel_id=1, source_target_pairs={{0,8},{1,9},{2,10},{3,11},{4,12},{5,13},{6,14},{7,15},{8,0},{9,1},... | collective-permute-start | bytes 1179656 | tf_op jit(solution)/shard_map/ppermute | solution.py:54
  25.2 10.3 %collective-permute-start.3 = (bf16[12,64,256]{2,1,0:T(8,128)(2,1)S(1)}, bf16[12,64,256]{2,1,0:T(8,128)(2,1)S(1)}, u32[]{:S(2)}, u32[]{:S(2)}) collective-permute-start(bf16[12,64,256]{2,1,0:T(8,128)(2,1)S(1)} %pad_maximum_fusion), channel_id=1, source_target_pairs={{0,16},{1,17},{2,18},{3,19},{4,20},{5,21},{6,22},{7,23},{8,24},{9,... | collective-permute-start | bytes 1179656 | tf_op jit(solution)/shard_map/ppermute | solution.py:54
  33.9 21.6 %copy-start.3 = (bf16[24,64,256]{2,1,0:T(8,128)(2,1)}, bf16[24,64,256]{2,1,0:T(8,128)(2,1)S(1)}, u32[]{:S(2)}) copy-start(bf16[24,64,256]{2,1,0:T(8,128)(2,1)S(1)} %constant_dynamic-update-slice_fusion.5.refs_8_) | copy-start | bytes 2359300
  33.9 18.1 %collective-permute-start.8 = (bf16[24,64,256]{2,1,0:T(8,128)(2,1)S(1)}, bf16[24,64,256]{2,1,0:T(8,128)(2,1)S(1)}, u32[]{:S(2)}, u32[]{:S(2)}) collective-permute-start(bf16[24,64,256]{2,1,0:T(8,128)(2,1)S(1)} %constant_dynamic-update-slice_fusion.5.refs_8_), channel_id=1, source_target_pairs={{0,16},{1,17},{2,18},{3,19},{4,20},{5,21},{6,22},{7,23},{8,24},{9,... | collective-permute-start | bytes 2359304 | tf_op jit(solution)/shard_map/ppermute | solution.py:54
  35.5 19.9 %copy-start.2 = (bf16[24,64,256]{2,1,0:T(8,128)(2,1)}, bf16[24,64,256]{2,1,0:T(8,128)(2,1)S(1)}, u32[]{:S(2)}) copy-start(bf16[24,64,256]{2,1,0:T(8,128)(2,1)S(1)} %constant_dynamic-update-slice_fusion.refs_4_) | copy-start | bytes 2359300
  35.5 17.5 %collective-permute-start.4 = (bf16[24,64,256]{2,1,0:T(8,128)(2,1)S(1)}, bf16[24,64,256]{2,1,0:T(8,128)(2,1)S(1)}, u32[]{:S(2)}, u32[]{:S(2)}) collective-permute-start(bf16[24,64,256]{2,1,0:T(8,128)(2,1)S(1)} %constant_dynamic-update-slice_fusion.refs_4_), channel_id=1, source_target_pairs={{0,8},{1,9},{2,10},{3,11},{4,12},{5,13},{6,14},{7,15},{8,0},{9,1},... | collective-permute-start | bytes 2359304 | tf_op jit(solution)/shard_map/ppermute | solution.py:54
  37.1 16.6 %collective-permute-start.9 = (bf16[24,64,256]{2,1,0:T(8,128)(2,1)S(1)}, bf16[24,64,256]{2,1,0:T(8,128)(2,1)S(1)}, u32[]{:S(2)}, u32[]{:S(2)}) collective-permute-start(bf16[24,64,256]{2,1,0:T(8,128)(2,1)S(1)} %constant_dynamic-update-slice_fusion.5.refs_8_), channel_id=1, source_target_pairs={{0,4},{1,5},{2,6},{3,7},{4,0},{5,1},{6,2},{7,3},{8,12},{9,13},{10,... | collective-permute-start | bytes 2359304 | tf_op jit(solution)/shard_map/ppermute | solution.py:54
  37.1 16.6 %collective-permute-start.5 = (bf16[24,64,256]{2,1,0:T(8,128)(2,1)S(1)}, bf16[24,64,256]{2,1,0:T(8,128)(2,1)S(1)}, u32[]{:S(2)}, u32[]{:S(2)}) collective-permute-start(bf16[24,64,256]{2,1,0:T(8,128)(2,1)S(1)} %constant_dynamic-update-slice_fusion.refs_4_), channel_id=1, source_target_pairs={{0,4},{1,5},{2,6},{3,7},{4,0},{5,1},{6,2},{7,3},{8,12},{9,13},{10,... | collective-permute-start | bytes 2359304 | tf_op jit(solution)/shard_map/ppermute | solution.py:54
  52.0 3.4 %copy-start.4 = (bf16[24,64,256]{2,1,0:T(8,128)(2,1)}, bf16[24,64,256]{2,1,0:T(8,128)(2,1)S(1)}, u32[]{:S(2)}) copy-start(bf16[24,64,256]{2,1,0:T(8,128)(2,1)S(1)} %collective-permute-done.8.refs_9_) | copy-start | bytes 2359300
  52.0 2.3 %collective-permute-start.10 = (bf16[24,64,256]{2,1,0:T(8,128)(2,1)S(1)}, bf16[24,64,256]{2,1,0:T(8,128)(2,1)S(1)}, u32[]{:S(2)}, u32[]{:S(2)}) collective-permute-start(bf16[24,64,256]{2,1,0:T(8,128)(2,1)S(1)} %collective-permute-done.8.refs_9_), channel_id=1, source_target_pairs={{0,4},{1,5},{2,6},{3,7},{4,0},{5,1},{6,2},{7,3},{8,12},{9,13},{10,... | collective-permute-start | bytes 2359304 | tf_op jit(solution)/shard_map/ppermute | solution.py:54
  53.0 2.4 %collective-permute-start.6 = (bf16[24,64,256]{2,1,0:T(8,128)(2,1)S(1)}, bf16[24,64,256]{2,1,0:T(8,128)(2,1)S(1)}, u32[]{:S(2)}, u32[]{:S(2)}) collective-permute-start(bf16[24,64,256]{2,1,0:T(8,128)(2,1)S(1)} %collective-permute-done.4.refs_5_), channel_id=1, source_target_pairs={{0,4},{1,5},{2,6},{3,7},{4,0},{5,1},{6,2},{7,3},{8,12},{9,13},{10,... | collective-permute-start | bytes 2359304 | tf_op jit(solution)/shard_map/ppermute | solution.py:54
  104.9 7.4 %collective-permute-start.11 = (f32[32,64,256]{2,1,0:T(8,128)}, f32[32,64,256]{2,1,0:T(8,128)S(1)}, u32[]{:S(2)}, u32[]{:S(2)}) collective-permute-start(f32[32,64,256]{2,1,0:T(8,128)} %get-tuple-element.6), channel_id=1, source_target_pairs={{0,4},{1,5},{2,6},{3,7},{4,0},{5,1},{6,2},{7,3},{8,12},{9,13},{10,... | collective-permute-start | bytes 6291464 | tf_op jit(solution)/shard_map/ppermute | solution.py:54
  114.1 18.7 %collective-permute-start.12 = (f32[2,4,64,256]{3,2,1,0:T(8,128)S(1)}, f32[2,4,64,256]{3,2,1,0:T(8,128)S(1)}, u32[]{:S(2)}, u32[]{:S(2)}) collective-permute-start(f32[2,4,64,256]{3,2,1,0:T(8,128)S(1)} %bitcast.54), channel_id=1, source_target_pairs={{0,8},{1,9},{2,10},{3,11},{4,12},{5,13},{6,14},{7,15},{8,0},{9,1},... | collective-permute-start | bytes 1572872 | tf_op jit(solution)/shard_map/ppermute | solution.py:54
  120.6 13.7 %collective-permute-start.14 = (f32[2,4,64,256]{3,2,1,0:T(8,128)S(1)}, f32[2,4,64,256]{3,2,1,0:T(8,128)S(1)}, u32[]{:S(2)}, u32[]{:S(2)}) collective-permute-start(f32[2,4,64,256]{3,2,1,0:T(8,128)S(1)} %bitcast.53), channel_id=1, source_target_pairs={{0,16},{1,17},{2,18},{3,19},{4,20},{5,21},{6,22},{7,23},{8,24},{9,... | collective-permute-start | bytes 1572872 | tf_op jit(solution)/shard_map/ppermute | solution.py:54
  132.9 7.9 %collective-permute-start.13 = (f32[4,64,256]{2,1,0:T(8,128)S(1)}, f32[4,64,256]{2,1,0:T(8,128)S(1)}, u32[]{:S(2)}, u32[]{:S(2)}) collective-permute-start(f32[4,64,256]{2,1,0:T(8,128)S(1)} %fusion.3), channel_id=1, source_target_pairs={{0,16},{1,17},{2,18},{3,19},{4,20},{5,21},{6,22},{7,23},{8,24},{9,... | collective-permute-start | bytes 786440 | tf_op jit(solution)/shard_map/ppermute | solution.py:54
  134.3 25.7 %copy-start = (f32[128,256]{1,0:T(8,128)S(1)}, f32[128,256]{1,0:T(8,128)}, u32[]{:S(2)}) copy-start(f32[128,256]{1,0:T(8,128)} %param.12) | copy-start | bytes 393220
  134.3 25.7 %copy-start.1 = (f32[128,256]{1,0:T(8,128)S(1)}, f32[128,256]{1,0:T(8,128)}, u32[]{:S(2)}) copy-start(f32[128,256]{1,0:T(8,128)} %param.13) | copy-start | bytes 393220
  134.4 7.3 %collective-permute-start.15 = (f32[4,64,256]{2,1,0:T(8,128)S(1)}, f32[4,64,256]{2,1,0:T(8,128)S(1)}, u32[]{:S(2)}, u32[]{:S(2)}) collective-permute-start(f32[4,64,256]{2,1,0:T(8,128)S(1)} %fusion), channel_id=1, source_target_pairs={{0,8},{1,9},{2,10},{3,11},{4,12},{5,13},{6,14},{7,15},{8,0},{9,1},... | collective-permute-start | bytes 786440 | tf_op jit(solution)/shard_map/ppermute | solution.py:54
  141.7 14.9 %collective-permute-start.16 = (f32[128,256]{1,0:T(8,128)S(1)}, f32[128,256]{1,0:T(8,128)S(1)}, u32[]{:S(2)}, u32[]{:S(2)}) collective-permute-start(f32[128,256]{1,0:T(8,128)S(1)} %pad_maximum_fusion.2), channel_id=1, source_target_pairs={{0,1},{1,2},{2,3},{3,0},{4,5},{5,6},{6,7},{7,4},{8,9},{9,10},{10,1... | collective-permute-start | bytes 393224 | tf_op jit(solution)/shard_map/ppermute | solution.py:54
  150.1 10.0 %collective-permute-start.17 = (f32[128,256]{1,0:T(8,128)S(1)}, f32[128,256]{1,0:T(8,128)S(1)}, u32[]{:S(2)}, u32[]{:S(2)}) collective-permute-start(f32[128,256]{1,0:T(8,128)S(1)} %pad_maximum_fusion.3), channel_id=1, source_target_pairs={{0,2},{1,3},{2,0},{3,1},{4,6},{5,7},{6,4},{7,5},{8,10},{9,11},{10,... | collective-permute-start | bytes 393224 | tf_op jit(solution)/shard_map/ppermute | solution.py:54
  153.7 6.3 %collective-permute-start.18 = (f32[128,256]{1,0:T(8,128)S(1)}, f32[128,256]{1,0:T(8,128)S(1)}, u32[]{:S(2)}, u32[]{:S(2)}) collective-permute-start(f32[128,256]{1,0:T(8,128)S(1)} %pad_maximum_fusion.4), channel_id=1, source_target_pairs={{0,3},{1,0},{2,1},{3,2},{4,7},{5,4},{6,5},{7,6},{8,11},{9,8},{10,9... | collective-permute-start | bytes 393224 | tf_op jit(solution)/shard_map/ppermute | solution.py:54
  (5 other events, 8.1 us)

commit v7 on v4

--- a/solution.py
+++ b/solution.py
@@ -57,23 +57,40 @@
 ORDERS = (("outer", "inner"), ("inner", "outer"))
 
 
-def gather_rows(shard, dims):
-    count = shard.shape[0]
-    cut = count // 2
-    line = [shard] + [shift(shard, dims, "line", k) for k in range(1, dims["line"])]
-    halves = []
-    for part, (first, second) in zip((slice(0, cut), slice(cut, count)), ORDERS):
+def spread(own, dims, names):
+    first, second = names
+    own = jnp.concatenate([own] + [shift(own, dims, first, k) for k in range(1, dims[first])])
+    return [own] + [shift(own, dims, second, k) for k in range(1, dims[second])]
+
+
+def gather_rows(shard, dims, extra):
+    cut = shard.shape[0] // 2
+    parts = (slice(0, cut), slice(cut, None))
+    line = [shift(shard, dims, "line", k) for k in range(1, dims["line"])]
+    near = [
+        jnp.concatenate(spread(shard[part], dims, names)) for part, names in zip(parts, ORDERS)
+    ]
+    near = [[own, shift(own, dims, "core", 1)] for own in near]
+    line, near = lax.optimization_barrier((line, near))
+    mids = []
+    for part, (first, _) in zip(parts, ORDERS):
         own = jnp.concatenate([piece[part] for piece in line])
-        own = jnp.concatenate([own] + [shift(own, dims, first, k) for k in range(1, dims[first])])
-        pieces = [own] + [shift(own, dims, second, k) for k in range(1, dims[second])]
-        pieces = pieces + [shift(piece, dims, "core", 1) for piece in pieces]
-        halves.append(pieces)
-    return halves
+        mids.append(
+            jnp.concatenate([own] + [shift(own, dims, first, k) for k in range(1, dims[first])])
+        )
+    mids, extra = lax.optimization_barrier((mids, extra))
+    far = []
+    for own, (_, second) in zip(mids, ORDERS):
+        far.append([own] + [shift(own, dims, second, k) for k in range(1, dims[second])])
+    pieces = near[0] + near[1]
+    for group in far:
+        pieces += group + [shift(piece, dims, "core", 1) for piece in group]
+    return pieces, extra
 
 
 def slots_kernel(dims, local_blocks, piece_count, *refs):
-    coords_ref, count_ref, owner_ref, blocks_ref = refs[:4]
-    pieces = refs[4 : 4 + piece_count]
+    coords_ref, count_ref, owner_ref, peer_ref, blocks_ref, extra_ref = refs[:6]
+    pieces = refs[6 : 6 + piece_count]
     (
         mine_ref,
         other_ref,
@@ -86,17 +103,34 @@
         block_sems,
         piece_sems,
         out_sems,
-    ) = refs[4 + piece_count :]
+    ) = refs[6 + piece_count :]
     edge, rank = grad_ref.shape[1], grad_ref.shape[2]
     width = TILE_J * edge
     tiles = edge // TILE_J
-    count = count_ref[0]
+    slot_count = blocks_ref.shape[0]
+    kept = slot_count - extra_ref.shape[0]
+    live = count_ref[0]
+    peer_live = peer_ref[3 * slot_count]
+    give = jnp.minimum(lax.div(jnp.maximum(live - peer_live, 0), 2), jnp.maximum(live - kept, 0))
+    take = jnp.minimum(
+        lax.div(jnp.maximum(peer_live - live, 0), 2), jnp.maximum(peer_live - kept, 0)
+    )
+    mine = live - give
+    count = mine + take
     cut = 3 * local_blocks // 2
     here = split_index(lax.axis_index("blk") * dims["line"] + lax.axis_index("grp"), dims)
     columns = dims["core"] * dims["outer"] * dims["inner"] * dims["line"]
 
-    def row_place(mode, slot):
-        pos = owner_ref[mode, coords_ref[mode, slot]]
+    def position(mode, item):
+        own = jnp.minimum(item, slot_count - 1)
+        other = jnp.clip(item - mine + peer_live - take, 0, slot_count - 1)
+        coord = jnp.where(
+            item < mine, coords_ref[mode, own], peer_ref[mode * slot_count + other]
+        )
+        return owner_ref[mode, coord]
+
+    def row_place(mode, item):
+        pos = position(mode, item)
         there = split_index(lax.div(pos, local_blocks), dims)
         away = {
             name: lax.rem(here[name] - there[name] + dims[name], dims[name]) for name in dims
@@ -107,14 +141,18 @@
         first = jnp.where(late, away["inner"], away["outer"])
         size_first = jnp.where(late, dims["inner"], dims["outer"])
         size_second = jnp.where(late, dims["outer"], dims["inner"])
-        spot = ((away["core"] * size_second + second) * size_first + first) * dims["line"]
-        spot = spot + away["line"]
+        spot = (away["core"] * size_second + second) * size_first + first
         blocks_of = jnp.where(late, 3 * local_blocks - cut, cut)
-        base = jnp.where(late, columns * cut, 0)
-        return base + spot * blocks_of + jnp.where(late, block - cut, block)
-
-    def grad_place(slot):
-        pos = owner_ref[0, coords_ref[0, slot]]
+        inside = jnp.where(late, block - cut, block)
+        per_line = columns // dims["line"]
+        near = jnp.where(late, per_line * cut, 0) + spot * blocks_of + inside
+        others = dims["line"] - 1
+        far = jnp.where(late, per_line * others * cut, 0) + per_line * 3 * local_blocks
+        far = far + (spot * others + away["line"] - 1) * blocks_of + inside
+        return jnp.where(away["line"] == 0, near, far)
+
+    def grad_place(item):
+        pos = position(0, item)
         there = split_index(lax.div(pos, local_blocks), dims)
         away = {
             name: lax.rem(there[name] - here[name] + dims[name], dims[name]) for name in dims
@@ -131,22 +169,28 @@
         spot = spot * dims["line"] + away["line"]
         return spot * half_blocks + jnp.where(late, local - half_blocks, local)
 
-    def block_copies(slot):
-        at = lax.rem(slot, BUFFERS)
+    def block_copies(source, slot, item):
+        at = lax.rem(item, BUFFERS)
         span = edge // COPY_PARTS
         return [
             pltpu.make_async_copy(
-                blocks_ref.at[slot, pl.ds(part * span, span)],
+                source.at[slot, pl.ds(part * span, span)],
                 blocks_buf.at[at, pl.ds(part * span, span)],
                 block_sems.at[at, part],
             )
             for part in range(COPY_PARTS)
         ]
 
-    def start(slot):
-        @pl.when(slot < count)
+    def start(item):
+        @pl.when(item < mine)
         def _():
-            for copy in block_copies(slot):
+            for copy in block_copies(blocks_ref, item, item):
+                copy.start()
+
+        @pl.when((item >= mine) & (item < count))
+        def _():
+            slot = item - mine + peer_live - take - kept
+            for copy in block_copies(extra_ref, slot, item):
                 copy.start()
 
     fills = []
@@ -178,7 +222,7 @@
 
     def step(slot, carry):
         start(slot + AHEAD)
-        for copy in block_copies(slot):
+        for copy in block_copies(blocks_ref, 0, slot):
             copy.wait()
         at = lax.rem(slot, BUFFERS)
         before = jnp.maximum(slot - 1, 0)
@@ -232,8 +276,12 @@
     row_blocks = row_owner.shape[1]
     dims = mesh_dims(lax.axis_size("blk"), lax.axis_size("grp"))
     shard = factors.astype(jnp.bfloat16).reshape(3 * local_blocks, edge, rank)
-    halves = gather_rows(shard, dims)
-    pieces = halves[0] + halves[1]
+    sent = slot_count * 7 // 18
+    peer = shift(jnp.concatenate([block_coords.reshape(-1), block_count]), dims, "core", 1)
+    begin = slot_count - sent + jnp.minimum(peer[3 * slot_count], 0)
+    extra = lax.dynamic_slice_in_dim(tensor_blocks, begin, sent, axis=0)
+    extra = shift(extra, dims, "core", 1)
+    pieces, (extra, peer) = gather_rows(shard, dims, (extra, peer))
     smem = pl.BlockSpec(memory_space=pltpu.SMEM)
     hbm = pl.BlockSpec(memory_space=pl.ANY)
     tiles = edge // TILE_J
@@ -241,7 +289,7 @@
     mine, other = pl.pallas_call(
         functools.partial(slots_kernel, dims, local_blocks, len(pieces)),
         out_shape=(outgoing, outgoing),
-        in_specs=[smem, smem, smem, hbm] + [hbm] * len(pieces),
+        in_specs=[smem, smem, smem, smem, hbm, hbm] + [hbm] * len(pieces),
         out_specs=(hbm, hbm),
         scratch_shapes=[
             pltpu.VMEM((3 * row_blocks, edge, rank), jnp.bfloat16),
@@ -260,7 +308,7 @@
             bytes_accessed=2 * slot_count * edge * width,
             transcendentals=slot_count * edge * width,
         ),
-    )(block_coords, block_count, row_owner, tensor_blocks, *pieces)
+    )(block_coords, block_count, row_owner, peer, tensor_blocks, extra, *pieces)
 
     def by_half(values):
         values = values.reshape(2, row_blocks // 4, edge, rank)

time: 144 us -> 152 us (1.056); the launches traced: 146 us -> 152 us
  starting transfers between devices: 41.4 us -> 60.7 us
  waiting for transfers between devices: 68.3 us -> 58.9 us
  Pallas kernels: 29.1 us -> 20.3 us
  local copies, waits for them, and re-layouts: 1.11 us -> 6.42 us
  other arithmetic: 4.93 us -> 3.31 us
    ppermute x19 -> x27, starting transfers between devices: 41.4 us -> 60.7 us  [shift(): return lax.ppermute(values, AXES, perm)]
    ppermute x19 -> x27, waiting for transfers between devices: 68.3 us -> 58.9 us  [shift(): return lax.ppermute(values, AXES, perm)]
    pallas_call x1, Pallas kernels: 29.1 us -> 20.3 us  [per_device(): pl.pallas_call(functools.partial(slots_kernel, dims, local_blocks, len(pi...]
    dynamic_slice x0 -> x1, local copies, waits for them, and re-layouts: none -> 4.07 us  [per_device(): extra = lax.dynamic_slice_in_dim(tensor_blocks, begin, sent, axis=0)]
  transfers between devices with their start and end apart: 19 -> 27, of which waited for: 13 -> 16; matrix products, arithmetic and copies ran while one was open for 0% -> 0% of each run, Pallas kernels for 0% -> 0%
where the time goes in v7:
time: 152 us
  starting transfers between devices  60.7 us (40%)
  waiting for transfers between devices  58.9 us (39%)
  Pallas kernels  20.3 us (13%)
  local copies, waits for them, and re-layouts  6.42 us (4%)
  other arithmetic  3.31 us (2%)
  between operations  2.32 us (2%)
    ppermute x27, starting transfers between devices, shift(): return lax.ppermute(values, AXES, perm)  60.7 us
    ppermute x27, waiting for transfers between devices, shift(): return lax.ppermute(values, AXES, perm)  58.9 us
    pallas_call x1, Pallas kernels, per_device(): pl.pallas_call(functools.partial(slots_kernel, dims, local_blocks, len(pi...  20.3 us
    dynamic_slice x1, local copies, waits for them, and re-layouts, per_device(): extra = lax.dynamic_slice_in_dim(tensor_blocks, begin, sent, axis=0)  4.07 us
  transfers between devices with their start and end apart: 27, of which 16 were waited for; matrix products, arithmetic and copies ran while one was open for 0% of the time, Pallas kernels for 0%

profile of v7, /device:TPU:0, one launch (start us, length us, event | category | flops | bytes accessed | tf_op | source)
XLA Modules:
  0.0 151.9 jit_solution(10417213527402632500)
XLA Ops:
  4.6 4.1 %constant_dynamic-slice_fusion = bf16[14,64,4096]{2,1,0:T(8,128)(2,1)S(1)} fusion(bf16[36,64,4096]{2,1,0:T(8,128)(2,1)} %refs_4_.1, s32[]{:T(128)S(6)} %select_n.3), kind=kLoop, calls=%fused_computation.45 | loop fusion | bytes 14680068 | tf_op jit(solution)/shard_map/dynamic_slice | solution.py:282
  9.2 2.8 %collective-permute-start.3 = (bf16[3,64,256]{2,1,0:T(8,128)(2,1)S(1)}, bf16[3,64,256]{2,1,0:T(8,128)(2,1)S(1)}, u32[]{:S(2)}, u32[]{:S(2)}) collective-permute-start(bf16[3,64,256]{2,1,0:T(8,128)(2,1)S(1)} %get-tuple-element.51), channel_id=1, source_target_pairs={{0,16},{1,17},{2,18},{3,19},{4,20},{5,21},{6,22},{7,23},{8,24},{9,... | collective-permute-start | bytes 294920 | tf_op jit(solution)/shard_map/ppermute | solution.py:54
  13.4 1.8 %collective-permute-done.3 = bf16[3,64,256]{2,1,0:T(8,128)(2,1)S(1)} collective-permute-done((bf16[3,64,256]{2,1,0:T(8,128)(2,1)S(1)}, bf16[3,64,256]{2,1,0:T(8,128)(2,1)S(1)}, u32[]{:S(2)}, u32[]{:S(2)}) %collective-permute-start.3) | collective-permute-done | bytes 98336 | tf_op jit(solution)/shard_map/ppermute | solution.py:54
  15.2 1.8 %collective-permute-start.4 = (bf16[6,64,256]{2,1,0:T(8,128)(2,1)S(1)}, bf16[6,64,256]{2,1,0:T(8,128)(2,1)S(1)}, u32[]{:S(2)}, u32[]{:S(2)}) collective-permute-start(bf16[6,64,256]{2,1,0:T(8,128)(2,1)S(1)} %pad_maximum_fusion.6), channel_id=1, source_target_pairs={{0,8},{1,9},{2,10},{3,11},{4,12},{5,13},{6,14},{7,15},{8,0},{9,1},... | collective-permute-start | bytes 589832 | tf_op jit(solution)/shard_map/ppermute | solution.py:54
  17.0 1.6 %collective-permute-start.7 = (bf16[6,64,256]{2,1,0:T(8,128)(2,1)S(1)}, bf16[6,64,256]{2,1,0:T(8,128)(2,1)S(1)}, u32[]{:S(2)}, u32[]{:S(2)}) collective-permute-start(bf16[6,64,256]{2,1,0:T(8,128)(2,1)S(1)} %pad_maximum_fusion.7), channel_id=1, source_target_pairs={{0,16},{1,17},{2,18},{3,19},{4,20},{5,21},{6,22},{7,23},{8,24},{9,... | collective-permute-start | bytes 589832 | tf_op jit(solution)/shard_map/ppermute | solution.py:54
  18.6 3.6 %collective-permute-start.2 = (bf16[6,64,256]{2,1,0:T(8,128)(2,1)S(1)}, bf16[6,64,256]{2,1,0:T(8,128)(2,1)S(1)}, u32[]{:S(2)}, u32[]{:S(2)}) collective-permute-start(bf16[6,64,256]{2,1,0:T(8,128)(2,1)S(1)} %bitcast.52), channel_id=1, source_target_pairs={{0,3},{1,0},{2,1},{3,2},{4,7},{5,4},{6,5},{7,6},{8,11},{9,8},{10,9... | collective-permute-start | bytes 589832 | tf_op jit(solution)/shard_map/ppermute | solution.py:54
  23.3 2.7 %collective-permute-start.1 = (bf16[6,64,256]{2,1,0:T(8,128)(2,1)S(1)}, bf16[6,64,256]{2,1,0:T(8,128)(2,1)S(1)}, u32[]{:S(2)}, u32[]{:S(2)}) collective-permute-start(bf16[6,64,256]{2,1,0:T(8,128)(2,1)S(1)} %bitcast.53), channel_id=1, source_target_pairs={{0,2},{1,3},{2,0},{3,1},{4,6},{5,7},{6,4},{7,5},{8,10},{9,11},{10,... | collective-permute-start | bytes 589832 | tf_op jit(solution)/shard_map/ppermute | solution.py:54
  25.9 1.6 %collective-permute-start = (bf16[6,64,256]{2,1,0:T(8,128)(2,1)S(1)}, bf16[6,64,256]{2,1,0:T(8,128)(2,1)S(1)}, u32[]{:S(2)}, u32[]{:S(2)}) collective-permute-start(bf16[6,64,256]{2,1,0:T(8,128)(2,1)S(1)} %bitcast.54), channel_id=1, source_target_pairs={{0,1},{1,2},{2,3},{3,0},{4,5},{5,6},{6,7},{7,4},{8,9},{9,10},{10,1... | collective-permute-start | bytes 589832 | tf_op jit(solution)/shard_map/ppermute | solution.py:54
  27.5 12.4 %collective-permute-done.1 = bf16[6,64,256]{2,1,0:T(8,128)(2,1)S(1)} collective-permute-done((bf16[6,64,256]{2,1,0:T(8,128)(2,1)S(1)}, bf16[6,64,256]{2,1,0:T(8,128)(2,1)S(1)}, u32[]{:S(2)}, u32[]{:S(2)}) %collective-permute-start.1) | collective-permute-done | bytes 196640 | tf_op jit(solution)/shard_map/ppermute | solution.py:54
  40.0 1.6 %collective-permute-start.9 = (bf16[9,64,256]{2,1,0:T(8,128)(2,1)S(1)}, bf16[9,64,256]{2,1,0:T(8,128)(2,1)S(1)}, u32[]{:S(2)}, u32[]{:S(2)}) collective-permute-start(bf16[9,64,256]{2,1,0:T(8,128)(2,1)S(1)} %pad_maximum_fusion.4), channel_id=1, source_target_pairs={{0,16},{1,17},{2,18},{3,19},{4,20},{5,21},{6,22},{7,23},{8,24},{9,... | collective-permute-start | bytes 884744 | tf_op jit(solution)/shard_map/ppermute | solution.py:54
  42.2 6.4 %collective-permute-done.9 = bf16[9,64,256]{2,1,0:T(8,128)(2,1)S(1)} collective-permute-done((bf16[9,64,256]{2,1,0:T(8,128)(2,1)S(1)}, bf16[9,64,256]{2,1,0:T(8,128)(2,1)S(1)}, u32[]{:S(2)}, u32[]{:S(2)}) %collective-permute-start.9) | collective-permute-done | bytes 294944 | tf_op jit(solution)/shard_map/ppermute | solution.py:54
  52.3 11.6 %collective-permute-done.13.refs_11_ = bf16[18,64,256]{2,1,0:T(8,128)(2,1)S(1)} collective-permute-done((bf16[18,64,256]{2,1,0:T(8,128)(2,1)S(1)}, bf16[18,64,256]{2,1,0:T(8,128)(2,1)S(1)}, u32[]{:S(2)}, u32[]{:S(2)}) %collective-permute-start.13) | collective-permute-done | bytes 589856 | tf_op jit(solution)/shard_map/ppermute | solution.py:54
  67.7 20.3 %shard_map.94 = (f32[32,64,256]{2,1,0:T(8,128)}, f32[32,64,256]{2,1,0:T(8,128)}) custom-call(s32[3,36]{1,0:T(4,128)} %refs_0_.1, s32[1]{0:T(128)S(6)} %copy.10.refs_1_, s32[3,64]{1,0:T(4,128)} %refs_2_.1, s32[109]{0:T(128)} %copy-done.16, bf16[36,64,4096]{2,1,0:T(8,128)(2,1)} %refs_4_.1, bf16[14,64,4096]{2,1,0:T(8,128)(2,1)} %copy-done.7, ...), custom_call_target="tpu_custom_call" | custom-call | flops 9663676416 | bytes 18874368 | tf_op jit(solution)/shard_map/pallas_call | solution.py:289
  88.1 4.4 %collective-permute-done.19 = f32[32,64,256]{2,1,0:T(8,128)S(1)} collective-permute-done((f32[32,64,256]{2,1,0:T(8,128)}, f32[32,64,256]{2,1,0:T(8,128)S(1)}, u32[]{:S(2)}, u32[]{:S(2)}) %collective-permute-start.19) | collective-permute-done | bytes 2097184 | tf_op jit(solution)/shard_map/ppermute | solution.py:54
  92.4 1.9 %slice_add_fusion.3 = (f32[8,64,256]{2,1,0:T(8,128)S(1)}, f32[8,64,256]{2,1,0:T(8,128)S(1)}, f32[8,64,256]{2,1,0:T(8,128)S(1)}, f32[8,64,256]{2,1,0:T(8,128)S(1)}) fusion(f32[32,64,256]{2,1,0:T(8,128)S(1)} %collective-permute-done.19, f32[32,64,256]{2,1,0:T(8,128)} %get-tuple-element.27), kind=kLoop, calls=%fused_computation.5 | loop fusion | flops 524288 | bytes 6291456 | tf_op jit(solution)/shard_map/add | solution.py:331
  94.3 10.1 %collective-permute-start.20 = (f32[2,4,64,256]{3,2,1,0:T(8,128)S(1)}, f32[2,4,64,256]{3,2,1,0:T(8,128)S(1)}, u32[]{:S(2)}, u32[]{:S(2)}) collective-permute-start(f32[2,4,64,256]{3,2,1,0:T(8,128)S(1)} %bitcast.56), channel_id=1, source_target_pairs={{0,8},{1,9},{2,10},{3,11},{4,12},{5,13},{6,14},{7,15},{8,0},{9,1},... | collective-permute-start | bytes 1572872 | tf_op jit(solution)/shard_map/ppermute | solution.py:54
  104.4 6.4 %collective-permute-start.22 = (f32[2,4,64,256]{3,2,1,0:T(8,128)S(1)}, f32[2,4,64,256]{3,2,1,0:T(8,128)S(1)}, u32[]{:S(2)}, u32[]{:S(2)}) collective-permute-start(f32[2,4,64,256]{3,2,1,0:T(8,128)S(1)} %bitcast.55), channel_id=1, source_target_pairs={{0,16},{1,17},{2,18},{3,19},{4,20},{5,21},{6,22},{7,23},{8,24},{9,... | collective-permute-start | bytes 1572872 | tf_op jit(solution)/shard_map/ppermute | solution.py:54
  110.8 5.8 %collective-permute-done.20 = f32[2,4,64,256]{3,2,1,0:T(8,128)S(1)} collective-permute-done((f32[2,4,64,256]{3,2,1,0:T(8,128)S(1)}, f32[2,4,64,256]{3,2,1,0:T(8,128)S(1)}, u32[]{:S(2)}, u32[]{:S(2)}) %collective-permute-start.20) | collective-permute-done | bytes 524320 | tf_op jit(solution)/shard_map/ppermute | solution.py:54
  116.7 6.5 %collective-permute-start.21 = (f32[4,64,256]{2,1,0:T(8,128)S(1)}, f32[4,64,256]{2,1,0:T(8,128)S(1)}, u32[]{:S(2)}, u32[]{:S(2)}) collective-permute-start(f32[4,64,256]{2,1,0:T(8,128)S(1)} %fusion.3), channel_id=1, source_target_pairs={{0,16},{1,17},{2,18},{3,19},{4,20},{5,21},{6,22},{7,23},{8,24},{9,... | collective-permute-start | bytes 786440 | tf_op jit(solution)/shard_map/ppermute | solution.py:54
  123.2 1.8 %collective-permute-start.23 = (f32[4,64,256]{2,1,0:T(8,128)S(1)}, f32[4,64,256]{2,1,0:T(8,128)S(1)}, u32[]{:S(2)}, u32[]{:S(2)}) collective-permute-start(f32[4,64,256]{2,1,0:T(8,128)S(1)} %fusion), channel_id=1, source_target_pairs={{0,8},{1,9},{2,10},{3,11},{4,12},{5,13},{6,14},{7,15},{8,0},{9,1},... | collective-permute-start | bytes 786440 | tf_op jit(solution)/shard_map/ppermute | solution.py:54
  125.0 4.2 %collective-permute-done.21 = f32[4,64,256]{2,1,0:T(8,128)S(1)} collective-permute-done((f32[4,64,256]{2,1,0:T(8,128)S(1)}, f32[4,64,256]{2,1,0:T(8,128)S(1)}, u32[]{:S(2)}, u32[]{:S(2)}) %collective-permute-start.21) | collective-permute-done | bytes 262176 | tf_op jit(solution)/shard_map/ppermute | solution.py:54
  130.9 12.1 %collective-permute-start.24 = (f32[128,256]{1,0:T(8,128)S(1)}, f32[128,256]{1,0:T(8,128)S(1)}, u32[]{:S(2)}, u32[]{:S(2)}) collective-permute-start(f32[128,256]{1,0:T(8,128)S(1)} %pad_maximum_fusion.8), channel_id=1, source_target_pairs={{0,1},{1,2},{2,3},{3,0},{4,5},{5,6},{6,7},{7,4},{8,9},{9,10},{10,1... | collective-permute-start | bytes 393224 | tf_op jit(solution)/shard_map/ppermute | solution.py:54
  143.1 2.4 %collective-permute-start.26 = (f32[128,256]{1,0:T(8,128)S(1)}, f32[128,256]{1,0:T(8,128)S(1)}, u32[]{:S(2)}, u32[]{:S(2)}) collective-permute-start(f32[128,256]{1,0:T(8,128)S(1)} %pad_maximum_fusion.10), channel_id=1, source_target_pairs={{0,3},{1,0},{2,1},{3,2},{4,7},{5,4},{6,5},{7,6},{8,11},{9,8},{10,9... | collective-permute-start | bytes 393224 | tf_op jit(solution)/shard_map/ppermute | solution.py:54
  146.9 4.3 %collective-permute-done.25 = f32[128,256]{1,0:T(8,128)S(1)} collective-permute-done((f32[128,256]{1,0:T(8,128)S(1)}, f32[128,256]{1,0:T(8,128)S(1)}, u32[]{:S(2)}, u32[]{:S(2)}) %collective-permute-start.25) | collective-permute-done | bytes 131104 | tf_op jit(solution)/shard_map/ppermute | solution.py:54
  (92 shorter events, 17.7 us)
Async XLA Ops:
  8.7 41.4 %collective-permute-start.12 = (bf16[14,64,4096]{2,1,0:T(8,128)(2,1)S(1)}, bf16[14,64,4096]{2,1,0:T(8,128)(2,1)S(1)}, u32[]{:S(2)}, u32[]{:S(2)}) collective-permute-start(bf16[14,64,4096]{2,1,0:T(8,128)(2,1)S(1)} %constant_dynamic-slice_fusion), channel_id=1, source_target_pairs={{0,4},{1,5},{2,6},{3,7},{4,0},{5,1},{6,2},{7,3},{8,12},{9,13},{10,... | collective-permute-start | bytes 22020104 | tf_op jit(solution)/shard_map/ppermute | solution.py:54
  9.2 6.0 %collective-permute-start.3 = (bf16[3,64,256]{2,1,0:T(8,128)(2,1)S(1)}, bf16[3,64,256]{2,1,0:T(8,128)(2,1)S(1)}, u32[]{:S(2)}, u32[]{:S(2)}) collective-permute-start(bf16[3,64,256]{2,1,0:T(8,128)(2,1)S(1)} %get-tuple-element.51), channel_id=1, source_target_pairs={{0,16},{1,17},{2,18},{3,19},{4,20},{5,21},{6,22},{7,23},{8,24},{9,... | collective-permute-start | bytes 294920 | tf_op jit(solution)/shard_map/ppermute | solution.py:54
  11.9 5.1 %collective-permute-start.6 = (bf16[3,64,256]{2,1,0:T(8,128)(2,1)S(1)}, bf16[3,64,256]{2,1,0:T(8,128)(2,1)S(1)}, u32[]{:S(2)}, u32[]{:S(2)}) collective-permute-start(bf16[3,64,256]{2,1,0:T(8,128)(2,1)S(1)} %get-tuple-element.50), channel_id=1, source_target_pairs={{0,8},{1,9},{2,10},{3,11},{4,12},{5,13},{6,14},{7,15},{8,0},{9,1},... | collective-permute-start | bytes 294920 | tf_op jit(solution)/shard_map/ppermute | solution.py:54
  15.2 7.0 %collective-permute-start.4 = (bf16[6,64,256]{2,1,0:T(8,128)(2,1)S(1)}, bf16[6,64,256]{2,1,0:T(8,128)(2,1)S(1)}, u32[]{:S(2)}, u32[]{:S(2)}) collective-permute-start(bf16[6,64,256]{2,1,0:T(8,128)(2,1)S(1)} %pad_maximum_fusion.6), channel_id=1, source_target_pairs={{0,8},{1,9},{2,10},{3,11},{4,12},{5,13},{6,14},{7,15},{8,0},{9,1},... | collective-permute-start | bytes 589832 | tf_op jit(solution)/shard_map/ppermute | solution.py:54
  17.0 6.1 %collective-permute-start.7 = (bf16[6,64,256]{2,1,0:T(8,128)(2,1)S(1)}, bf16[6,64,256]{2,1,0:T(8,128)(2,1)S(1)}, u32[]{:S(2)}, u32[]{:S(2)}) collective-permute-start(bf16[6,64,256]{2,1,0:T(8,128)(2,1)S(1)} %pad_maximum_fusion.7), channel_id=1, source_target_pairs={{0,16},{1,17},{2,18},{3,19},{4,20},{5,21},{6,22},{7,23},{8,24},{9,... | collective-permute-start | bytes 589832 | tf_op jit(solution)/shard_map/ppermute | solution.py:54
  18.6 7.3 %collective-permute-start.2 = (bf16[6,64,256]{2,1,0:T(8,128)(2,1)S(1)}, bf16[6,64,256]{2,1,0:T(8,128)(2,1)S(1)}, u32[]{:S(2)}, u32[]{:S(2)}) collective-permute-start(bf16[6,64,256]{2,1,0:T(8,128)(2,1)S(1)} %bitcast.52), channel_id=1, source_target_pairs={{0,3},{1,0},{2,1},{3,2},{4,7},{5,4},{6,5},{7,6},{8,11},{9,8},{10,9... | collective-permute-start | bytes 589832 | tf_op jit(solution)/shard_map/ppermute | solution.py:54
  22.3 17.6 %collective-permute-start.5 = (bf16[12,64,256]{2,1,0:T(8,128)(2,1)S(1)}, bf16[12,64,256]{2,1,0:T(8,128)(2,1)S(1)}, u32[]{:S(2)}, u32[]{:S(2)}) collective-permute-start(bf16[12,64,256]{2,1,0:T(8,128)(2,1)S(1)} %pad_maximum_fusion.2.refs_6_), channel_id=1, source_target_pairs={{0,4},{1,5},{2,6},{3,7},{4,0},{5,1},{6,2},{7,3},{8,12},{9,13},{10,... | collective-permute-start | bytes 1179656 | tf_op jit(solution)/shard_map/ppermute | solution.py:54
  23.2 16.7 %collective-permute-start.8 = (bf16[12,64,256]{2,1,0:T(8,128)(2,1)S(1)}, bf16[12,64,256]{2,1,0:T(8,128)(2,1)S(1)}, u32[]{:S(2)}, u32[]{:S(2)}) collective-permute-start(bf16[12,64,256]{2,1,0:T(8,128)(2,1)S(1)} %pad_maximum_fusion.3.refs_8_), channel_id=1, source_target_pairs={{0,4},{1,5},{2,6},{3,7},{4,0},{5,1},{6,2},{7,3},{8,12},{9,13},{10,... | collective-permute-start | bytes 1179656 | tf_op jit(solution)/shard_map/ppermute | solution.py:54
  23.3 16.6 %collective-permute-start.1 = (bf16[6,64,256]{2,1,0:T(8,128)(2,1)S(1)}, bf16[6,64,256]{2,1,0:T(8,128)(2,1)S(1)}, u32[]{:S(2)}, u32[]{:S(2)}) collective-permute-start(bf16[6,64,256]{2,1,0:T(8,128)(2,1)S(1)} %bitcast.53), channel_id=1, source_target_pairs={{0,2},{1,3},{2,0},{3,1},{4,6},{5,7},{6,4},{7,5},{8,10},{9,11},{10,... | collective-permute-start | bytes 589832 | tf_op jit(solution)/shard_map/ppermute | solution.py:54
  25.9 14.0 %collective-permute-start = (bf16[6,64,256]{2,1,0:T(8,128)(2,1)S(1)}, bf16[6,64,256]{2,1,0:T(8,128)(2,1)S(1)}, u32[]{:S(2)}, u32[]{:S(2)}) collective-permute-start(bf16[6,64,256]{2,1,0:T(8,128)(2,1)S(1)} %bitcast.54), channel_id=1, source_target_pairs={{0,1},{1,2},{2,3},{3,0},{4,5},{5,6},{6,7},{7,4},{8,9},{9,10},{10,1... | collective-permute-start | bytes 589832 | tf_op jit(solution)/shard_map/ppermute | solution.py:54
  40.0 8.6 %collective-permute-start.9 = (bf16[9,64,256]{2,1,0:T(8,128)(2,1)S(1)}, bf16[9,64,256]{2,1,0:T(8,128)(2,1)S(1)}, u32[]{:S(2)}, u32[]{:S(2)}) collective-permute-start(bf16[9,64,256]{2,1,0:T(8,128)(2,1)S(1)} %pad_maximum_fusion.4), channel_id=1, source_target_pairs={{0,16},{1,17},{2,18},{3,19},{4,20},{5,21},{6,22},{7,23},{8,24},{9,... | collective-permute-start | bytes 884744 | tf_op jit(solution)/shard_map/ppermute | solution.py:54
  41.7 8.4 %collective-permute-start.10 = (bf16[9,64,256]{2,1,0:T(8,128)(2,1)S(1)}, bf16[9,64,256]{2,1,0:T(8,128)(2,1)S(1)}, u32[]{:S(2)}, u32[]{:S(2)}) collective-permute-start(bf16[9,64,256]{2,1,0:T(8,128)(2,1)S(1)} %pad_maximum_fusion.5), channel_id=1, source_target_pairs={{0,8},{1,9},{2,10},{3,11},{4,12},{5,13},{6,14},{7,15},{8,0},{9,1},... | collective-permute-start | bytes 884744 | tf_op jit(solution)/shard_map/ppermute | solution.py:54
  50.1 13.8 %collective-permute-start.13 = (bf16[18,64,256]{2,1,0:T(8,128)(2,1)S(1)}, bf16[18,64,256]{2,1,0:T(8,128)(2,1)S(1)}, u32[]{:S(2)}, u32[]{:S(2)}) collective-permute-start(bf16[18,64,256]{2,1,0:T(8,128)(2,1)S(1)} %pad_maximum_fusion.refs_10_), channel_id=1, source_target_pairs={{0,8},{1,9},{2,10},{3,11},{4,12},{5,13},{6,14},{7,15},{8,0},{9,1},... | collective-permute-start | bytes 1769480 | tf_op jit(solution)/shard_map/ppermute | solution.py:54
  50.5 13.5 %collective-permute-start.16 = (bf16[18,64,256]{2,1,0:T(8,128)(2,1)S(1)}, bf16[18,64,256]{2,1,0:T(8,128)(2,1)S(1)}, u32[]{:S(2)}, u32[]{:S(2)}) collective-permute-start(bf16[18,64,256]{2,1,0:T(8,128)(2,1)S(1)} %pad_maximum_fusion.1.refs_14_), channel_id=1, source_target_pairs={{0,16},{1,17},{2,18},{3,19},{4,20},{5,21},{6,22},{7,23},{8,24},{9,... | collective-permute-start | bytes 1769480 | tf_op jit(solution)/shard_map/ppermute | solution.py:54
  51.8 12.6 %collective-permute-start.14 = (bf16[18,64,256]{2,1,0:T(8,128)(2,1)S(1)}, bf16[18,64,256]{2,1,0:T(8,128)(2,1)S(1)}, u32[]{:S(2)}, u32[]{:S(2)}) collective-permute-start(bf16[18,64,256]{2,1,0:T(8,128)(2,1)S(1)} %pad_maximum_fusion.refs_10_), channel_id=1, source_target_pairs={{0,4},{1,5},{2,6},{3,7},{4,0},{5,1},{6,2},{7,3},{8,12},{9,13},{10,... | collective-permute-start | bytes 1769480 | tf_op jit(solution)/shard_map/ppermute | solution.py:54
  51.8 12.6 %collective-permute-start.17 = (bf16[18,64,256]{2,1,0:T(8,128)(2,1)S(1)}, bf16[18,64,256]{2,1,0:T(8,128)(2,1)S(1)}, u32[]{:S(2)}, u32[]{:S(2)}) collective-permute-start(bf16[18,64,256]{2,1,0:T(8,128)(2,1)S(1)} %pad_maximum_fusion.1.refs_14_), channel_id=1, source_target_pairs={{0,4},{1,5},{2,6},{3,7},{4,0},{5,1},{6,2},{7,3},{8,12},{9,13},{10,... | collective-permute-start | bytes 1769480 | tf_op jit(solution)/shard_map/ppermute | solution.py:54
  88.0 4.4 %collective-permute-start.19 = (f32[32,64,256]{2,1,0:T(8,128)}, f32[32,64,256]{2,1,0:T(8,128)S(1)}, u32[]{:S(2)}, u32[]{:S(2)}) collective-permute-start(f32[32,64,256]{2,1,0:T(8,128)} %get-tuple-element.28), channel_id=1, source_target_pairs={{0,4},{1,5},{2,6},{3,7},{4,0},{5,1},{6,2},{7,3},{8,12},{9,13},{10,... | collective-permute-start | bytes 6291464 | tf_op jit(solution)/shard_map/ppermute | solution.py:54
  94.3 22.3 %collective-permute-start.20 = (f32[2,4,64,256]{3,2,1,0:T(8,128)S(1)}, f32[2,4,64,256]{3,2,1,0:T(8,128)S(1)}, u32[]{:S(2)}, u32[]{:S(2)}) collective-permute-start(f32[2,4,64,256]{3,2,1,0:T(8,128)S(1)} %bitcast.56), channel_id=1, source_target_pairs={{0,8},{1,9},{2,10},{3,11},{4,12},{5,13},{6,14},{7,15},{8,0},{9,1},... | collective-permute-start | bytes 1572872 | tf_op jit(solution)/shard_map/ppermute | solution.py:54
  104.4 18.8 %collective-permute-start.22 = (f32[2,4,64,256]{3,2,1,0:T(8,128)S(1)}, f32[2,4,64,256]{3,2,1,0:T(8,128)S(1)}, u32[]{:S(2)}, u32[]{:S(2)}) collective-permute-start(f32[2,4,64,256]{3,2,1,0:T(8,128)S(1)} %bitcast.55), channel_id=1, source_target_pairs={{0,16},{1,17},{2,18},{3,19},{4,20},{5,21},{6,22},{7,23},{8,24},{9,... | collective-permute-start | bytes 1572872 | tf_op jit(solution)/shard_map/ppermute | solution.py:54
  116.7 12.6 %collective-permute-start.21 = (f32[4,64,256]{2,1,0:T(8,128)S(1)}, f32[4,64,256]{2,1,0:T(8,128)S(1)}, u32[]{:S(2)}, u32[]{:S(2)}) collective-permute-start(f32[4,64,256]{2,1,0:T(8,128)S(1)} %fusion.3), channel_id=1, source_target_pairs={{0,16},{1,17},{2,18},{3,19},{4,20},{5,21},{6,22},{7,23},{8,24},{9,... | collective-permute-start | bytes 786440 | tf_op jit(solution)/shard_map/ppermute | solution.py:54
  123.2 7.6 %collective-permute-start.23 = (f32[4,64,256]{2,1,0:T(8,128)S(1)}, f32[4,64,256]{2,1,0:T(8,128)S(1)}, u32[]{:S(2)}, u32[]{:S(2)}) collective-permute-start(f32[4,64,256]{2,1,0:T(8,128)S(1)} %fusion), channel_id=1, source_target_pairs={{0,8},{1,9},{2,10},{3,11},{4,12},{5,13},{6,14},{7,15},{8,0},{9,1},... | collective-permute-start | bytes 786440 | tf_op jit(solution)/shard_map/ppermute | solution.py:54
  130.9 15.9 %collective-permute-start.24 = (f32[128,256]{1,0:T(8,128)S(1)}, f32[128,256]{1,0:T(8,128)S(1)}, u32[]{:S(2)}, u32[]{:S(2)}) collective-permute-start(f32[128,256]{1,0:T(8,128)S(1)} %pad_maximum_fusion.8), channel_id=1, source_target_pairs={{0,1},{1,2},{2,3},{3,0},{4,5},{5,6},{6,7},{7,4},{8,9},{9,10},{10,1... | collective-permute-start | bytes 393224 | tf_op jit(solution)/shard_map/ppermute | solution.py:54
  143.0 8.1 %collective-permute-start.25 = (f32[128,256]{1,0:T(8,128)S(1)}, f32[128,256]{1,0:T(8,128)S(1)}, u32[]{:S(2)}, u32[]{:S(2)}) collective-permute-start(f32[128,256]{1,0:T(8,128)S(1)} %pad_maximum_fusion.9), channel_id=1, source_target_pairs={{0,2},{1,3},{2,0},{3,1},{4,6},{5,7},{6,4},{7,5},{8,10},{9,11},{10,... | collective-permute-start | bytes 393224 | tf_op jit(solution)/shard_map/ppermute | solution.py:54
  143.1 8.0 %collective-permute-start.26 = (f32[128,256]{1,0:T(8,128)S(1)}, f32[128,256]{1,0:T(8,128)S(1)}, u32[]{:S(2)}, u32[]{:S(2)}) collective-permute-start(f32[128,256]{1,0:T(8,128)S(1)} %pad_maximum_fusion.10), channel_id=1, source_target_pairs={{0,3},{1,0},{2,1},{3,2},{4,7},{5,4},{6,5},{7,6},{8,11},{9,8},{10,9... | collective-permute-start | bytes 393224 | tf_op jit(solution)/shard_map/ppermute | solution.py:54
  (20 other events, 345.1 us)

commit v8 on v4

--- a/solution.py
+++ b/solution.py
@@ -72,8 +72,8 @@
 
 
 def slots_kernel(dims, local_blocks, piece_count, *refs):
-    coords_ref, count_ref, owner_ref, blocks_ref = refs[:4]
-    pieces = refs[4 : 4 + piece_count]
+    coords_ref, count_ref, owner_ref, peer_ref, blocks_ref, extra_ref = refs[:6]
+    pieces = refs[6 : 6 + piece_count]
     (
         mine_ref,
         other_ref,
@@ -86,17 +86,31 @@
         block_sems,
         piece_sems,
         out_sems,
-    ) = refs[4 + piece_count :]
+    ) = refs[6 + piece_count :]
     edge, rank = grad_ref.shape[1], grad_ref.shape[2]
     width = TILE_J * edge
     tiles = edge // TILE_J
-    count = count_ref[0]
+    slot_count = blocks_ref.shape[0]
+    live = count_ref[0]
+    peer_live = peer_ref[3 * slot_count]
+    give = lax.div(jnp.maximum(live - peer_live, 0), 2)
+    take = lax.div(jnp.maximum(peer_live - live, 0), 2)
+    mine = live - give
+    count = mine + take
     cut = 3 * local_blocks // 2
     here = split_index(lax.axis_index("blk") * dims["line"] + lax.axis_index("grp"), dims)
     columns = dims["core"] * dims["outer"] * dims["inner"] * dims["line"]
 
-    def row_place(mode, slot):
-        pos = owner_ref[mode, coords_ref[mode, slot]]
+    def position(mode, item):
+        own = jnp.minimum(item, slot_count - 1)
+        other = jnp.clip(item - mine + peer_live - take, 0, slot_count - 1)
+        coord = jnp.where(
+            item < mine, coords_ref[mode, own], peer_ref[mode * slot_count + other]
+        )
+        return owner_ref[mode, coord]
+
+    def row_place(mode, item):
+        pos = position(mode, item)
         there = split_index(lax.div(pos, local_blocks), dims)
         away = {
             name: lax.rem(here[name] - there[name] + dims[name], dims[name]) for name in dims
@@ -113,8 +127,8 @@
         base = jnp.where(late, columns * cut, 0)
         return base + spot * blocks_of + jnp.where(late, block - cut, block)
 
-    def grad_place(slot):
-        pos = owner_ref[0, coords_ref[0, slot]]
+    def grad_place(item):
+        pos = position(0, item)
         there = split_index(lax.div(pos, local_blocks), dims)
         away = {
             name: lax.rem(there[name] - here[name] + dims[name], dims[name]) for name in dims
@@ -131,22 +145,28 @@
         spot = spot * dims["line"] + away["line"]
         return spot * half_blocks + jnp.where(late, local - half_blocks, local)
 
-    def block_copies(slot):
-        at = lax.rem(slot, BUFFERS)
+    def block_copies(source, slot, item):
+        at = lax.rem(item, BUFFERS)
         span = edge // COPY_PARTS
         return [
             pltpu.make_async_copy(
-                blocks_ref.at[slot, pl.ds(part * span, span)],
+                source.at[slot, pl.ds(part * span, span)],
                 blocks_buf.at[at, pl.ds(part * span, span)],
                 block_sems.at[at, part],
             )
             for part in range(COPY_PARTS)
         ]
 
-    def start(slot):
-        @pl.when(slot < count)
+    def start(item):
+        @pl.when(item < mine)
         def _():
-            for copy in block_copies(slot):
+            for copy in block_copies(blocks_ref, item, item):
+                copy.start()
+
+        @pl.when((item >= mine) & (item < count))
+        def _():
+            slot = item - mine + peer_live - take
+            for copy in block_copies(extra_ref, slot, item):
                 copy.start()
 
     fills = []
@@ -178,7 +198,7 @@
 
     def step(slot, carry):
         start(slot + AHEAD)
-        for copy in block_copies(slot):
+        for copy in block_copies(blocks_ref, 0, slot):
             copy.wait()
         at = lax.rem(slot, BUFFERS)
         before = jnp.maximum(slot - 1, 0)
@@ -232,6 +252,8 @@
     row_blocks = row_owner.shape[1]
     dims = mesh_dims(lax.axis_size("blk"), lax.axis_size("grp"))
     shard = factors.astype(jnp.bfloat16).reshape(3 * local_blocks, edge, rank)
+    peer = shift(jnp.concatenate([block_coords.reshape(-1), block_count]), dims, "core", 1)
+    extra = shift(tensor_blocks, dims, "core", 1)
     halves = gather_rows(shard, dims)
     pieces = halves[0] + halves[1]
     smem = pl.BlockSpec(memory_space=pltpu.SMEM)
@@ -241,7 +263,7 @@
     mine, other = pl.pallas_call(
         functools.partial(slots_kernel, dims, local_blocks, len(pieces)),
         out_shape=(outgoing, outgoing),
-        in_specs=[smem, smem, smem, hbm] + [hbm] * len(pieces),
+        in_specs=[smem, smem, smem, smem, hbm, hbm] + [hbm] * len(pieces),
         out_specs=(hbm, hbm),
         scratch_shapes=[
             pltpu.VMEM((3 * row_blocks, edge, rank), jnp.bfloat16),
@@ -260,7 +282,7 @@
             bytes_accessed=2 * slot_count * edge * width,
             transcendentals=slot_count * edge * width,
         ),
-    )(block_coords, block_count, row_owner, tensor_blocks, *pieces)
+    )(block_coords, block_count, row_owner, peer, tensor_blocks, extra, *pieces)
 
     def by_half(values):
         values = values.reshape(2, row_blocks // 4, edge, rank)

time: 144 us -> 144 us (level)
  waiting for transfers between devices: 68.3 us -> 61.4 us
  starting transfers between devices: 41.4 us -> 44.6 us
  Pallas kernels: 29.1 us -> 31.6 us
    ppermute x19 -> x21, waiting for transfers between devices: 68.3 us -> 61.4 us  [shift(): return lax.ppermute(values, AXES, perm)]
    ppermute x19 -> x21, starting transfers between devices: 41.4 us -> 44.6 us  [shift(): return lax.ppermute(values, AXES, perm)]
    pallas_call x1, Pallas kernels: 29.1 us -> 31.6 us  [per_device(): pl.pallas_call(functools.partial(slots_kernel, dims, local_blocks, len(pi...]
  transfers between devices with their start and end apart: 19 -> 21, of which waited for: 13 -> 14; matrix products, arithmetic and copies ran while one was open for 0% -> 1% of each run, Pallas kernels for 0% -> 0%
where the time goes in v8:
time: 144 us; the launch traced here: 145 us
  waiting for transfers between devices  61.4 us (43%)
  starting transfers between devices  44.6 us (31%)
  Pallas kernels  31.6 us (22%)
  other arithmetic  5 us (3%)
  between operations  1.58 us (1%)
    ppermute x21, waiting for transfers between devices, shift(): return lax.ppermute(values, AXES, perm)  61.4 us
    ppermute x21, starting transfers between devices, shift(): return lax.ppermute(values, AXES, perm)  44.6 us
    pallas_call x1, Pallas kernels, per_device(): pl.pallas_call(functools.partial(slots_kernel, dims, local_blocks, len(pi...  31.6 us
  transfers between devices with their start and end apart: 21, of which 14 were waited for; matrix products, arithmetic and copies ran while one was open for 1% of the time, Pallas kernels for 0%

profile of v8, /device:TPU:0, one launch (start us, length us, event | category | flops | bytes accessed | tf_op | source)
XLA Modules:
  0.0 145.4 jit_solution(9261910932137670)
XLA Ops:
  2.2 4.7 %collective-permute-start.4 = (bf16[6,64,256]{2,1,0:T(8,128)(2,1)S(1)}, bf16[6,64,256]{2,1,0:T(8,128)(2,1)S(1)}, u32[]{:S(2)}, u32[]{:S(2)}) collective-permute-start(bf16[6,64,256]{2,1,0:T(8,128)(2,1)S(1)} %bitcast.49), channel_id=1, source_target_pairs={{0,3},{1,0},{2,1},{3,2},{4,7},{5,4},{6,5},{7,6},{8,11},{9,8},{10,9... | collective-permute-start | bytes 589832 | tf_op jit(solution)/shard_map/ppermute | solution.py:54
  7.9 13.2 %collective-permute-done.2 = bf16[6,64,256]{2,1,0:T(8,128)(2,1)S(1)} collective-permute-done((bf16[6,64,256]{2,1,0:T(8,128)(2,1)S(1)}, bf16[6,64,256]{2,1,0:T(8,128)(2,1)S(1)}, u32[]{:S(2)}, u32[]{:S(2)}) %collective-permute-start.2) | collective-permute-done | bytes 196640 | tf_op jit(solution)/shard_map/ppermute | solution.py:54
  21.1 3.1 %collective-permute-done.3 = bf16[6,64,256]{2,1,0:T(8,128)(2,1)S(1)} collective-permute-done((bf16[6,64,256]{2,1,0:T(8,128)(2,1)S(1)}, bf16[6,64,256]{2,1,0:T(8,128)(2,1)S(1)}, u32[]{:S(2)}, u32[]{:S(2)}) %collective-permute-start.3) | collective-permute-done | bytes 196640 | tf_op jit(solution)/shard_map/ppermute | solution.py:54
  24.3 1.6 %collective-permute-start.9 = (bf16[12,64,256]{2,1,0:T(8,128)(2,1)S(1)}, bf16[12,64,256]{2,1,0:T(8,128)(2,1)S(1)}, u32[]{:S(2)}, u32[]{:S(2)}) collective-permute-start(bf16[12,64,256]{2,1,0:T(8,128)(2,1)S(1)} %pad_maximum_fusion.1), channel_id=1, source_target_pairs={{0,8},{1,9},{2,10},{3,11},{4,12},{5,13},{6,14},{7,15},{8,0},{9,1},... | collective-permute-start | bytes 1179656 | tf_op jit(solution)/shard_map/ppermute | solution.py:54
  25.9 1.6 %collective-permute-start.5 = (bf16[12,64,256]{2,1,0:T(8,128)(2,1)S(1)}, bf16[12,64,256]{2,1,0:T(8,128)(2,1)S(1)}, u32[]{:S(2)}, u32[]{:S(2)}) collective-permute-start(bf16[12,64,256]{2,1,0:T(8,128)(2,1)S(1)} %pad_maximum_fusion), channel_id=1, source_target_pairs={{0,16},{1,17},{2,18},{3,19},{4,20},{5,21},{6,22},{7,23},{8,24},{9,... | collective-permute-start | bytes 1179656 | tf_op jit(solution)/shard_map/ppermute | solution.py:54
  27.5 7.6 %collective-permute-done.9 = bf16[12,64,256]{2,1,0:T(8,128)(2,1)S(1)} collective-permute-done((bf16[12,64,256]{2,1,0:T(8,128)(2,1)S(1)}, bf16[12,64,256]{2,1,0:T(8,128)(2,1)S(1)}, u32[]{:S(2)}, u32[]{:S(2)}) %collective-permute-start.9) | collective-permute-done | bytes 393248 | tf_op jit(solution)/shard_map/ppermute | solution.py:54
  35.2 1.6 %collective-permute-start.10 = (bf16[24,64,256]{2,1,0:T(8,128)(2,1)S(1)}, bf16[24,64,256]{2,1,0:T(8,128)(2,1)S(1)}, u32[]{:S(2)}, u32[]{:S(2)}) collective-permute-start(bf16[24,64,256]{2,1,0:T(8,128)(2,1)S(1)} %constant_dynamic-update-slice_fusion.5.refs_10_), channel_id=1, source_target_pairs={{0,16},{1,17},{2,18},{3,19},{4,20},{5,21},{6,22},{7,23},{8,24},{9,... | collective-permute-start | bytes 2359304 | tf_op jit(solution)/shard_map/ppermute | solution.py:54
  36.8 1.6 %collective-permute-start.6 = (bf16[24,64,256]{2,1,0:T(8,128)(2,1)S(1)}, bf16[24,64,256]{2,1,0:T(8,128)(2,1)S(1)}, u32[]{:S(2)}, u32[]{:S(2)}) collective-permute-start(bf16[24,64,256]{2,1,0:T(8,128)(2,1)S(1)} %constant_dynamic-update-slice_fusion.refs_6_), channel_id=1, source_target_pairs={{0,8},{1,9},{2,10},{3,11},{4,12},{5,13},{6,14},{7,15},{8,0},{9,1},... | collective-permute-start | bytes 2359304 | tf_op jit(solution)/shard_map/ppermute | solution.py:54
  40.5 13.0 %collective-permute-done.10.refs_11_ = bf16[24,64,256]{2,1,0:T(8,128)(2,1)S(1)} collective-permute-done((bf16[24,64,256]{2,1,0:T(8,128)(2,1)S(1)}, bf16[24,64,256]{2,1,0:T(8,128)(2,1)S(1)}, u32[]{:S(2)}, u32[]{:S(2)}) %collective-permute-start.10) | collective-permute-done | bytes 786464 | tf_op jit(solution)/shard_map/ppermute | solution.py:54
  53.5 1.3 collective-permute-done.6.refs_7_
  55.8 1.3 collective-permute-done.8.refs_9_
  58.0 31.6 %shard_map.94 = (f32[32,64,256]{2,1,0:T(8,128)}, f32[32,64,256]{2,1,0:T(8,128)}) custom-call(s32[3,36]{1,0:T(4,128)} %refs_0_.1, s32[1]{0:T(128)S(6)} %copy.18.refs_1_, s32[3,64]{1,0:T(4,128)} %refs_2_.1, s32[109]{0:T(128)} %copy-done.11, bf16[36,64,4096]{2,1,0:T(8,128)(2,1)} %refs_4_.1, bf16[36,64,4096]{2,1,0:T(8,128)(2,1)} %collective-permute-done.1.refs_5_, ...), custom_call_target="tpu_custom_call" | custom-call | flops 9663676416 | bytes 18874368 | tf_op jit(solution)/shard_map/pallas_call | solution.py:263
  89.8 4.4 %collective-permute-done.13 = f32[32,64,256]{2,1,0:T(8,128)S(1)} collective-permute-done((f32[32,64,256]{2,1,0:T(8,128)}, f32[32,64,256]{2,1,0:T(8,128)S(1)}, u32[]{:S(2)}, u32[]{:S(2)}) %collective-permute-start.13) | collective-permute-done | bytes 2097184 | tf_op jit(solution)/shard_map/ppermute | solution.py:54
  94.1 1.9 %slice_add_fusion.3 = (f32[8,64,256]{2,1,0:T(8,128)S(1)}, f32[8,64,256]{2,1,0:T(8,128)S(1)}, f32[8,64,256]{2,1,0:T(8,128)S(1)}, f32[8,64,256]{2,1,0:T(8,128)S(1)}) fusion(f32[32,64,256]{2,1,0:T(8,128)S(1)} %collective-permute-done.13, f32[32,64,256]{2,1,0:T(8,128)} %get-tuple-element.5), kind=kLoop, calls=%fused_computation.3 | loop fusion | flops 524288 | bytes 6291456 | tf_op jit(solution)/shard_map/add | solution.py:305
  96.0 4.8 %collective-permute-start.14 = (f32[2,4,64,256]{3,2,1,0:T(8,128)S(1)}, f32[2,4,64,256]{3,2,1,0:T(8,128)S(1)}, u32[]{:S(2)}, u32[]{:S(2)}) collective-permute-start(f32[2,4,64,256]{3,2,1,0:T(8,128)S(1)} %bitcast.54), channel_id=1, source_target_pairs={{0,8},{1,9},{2,10},{3,11},{4,12},{5,13},{6,14},{7,15},{8,0},{9,1},... | collective-permute-start | bytes 1572872 | tf_op jit(solution)/shard_map/ppermute | solution.py:54
  100.7 10.4 %collective-permute-start.16 = (f32[2,4,64,256]{3,2,1,0:T(8,128)S(1)}, f32[2,4,64,256]{3,2,1,0:T(8,128)S(1)}, u32[]{:S(2)}, u32[]{:S(2)}) collective-permute-start(f32[2,4,64,256]{3,2,1,0:T(8,128)S(1)} %bitcast.53), channel_id=1, source_target_pairs={{0,16},{1,17},{2,18},{3,19},{4,20},{5,21},{6,22},{7,23},{8,24},{9,... | collective-permute-start | bytes 1572872 | tf_op jit(solution)/shard_map/ppermute | solution.py:54
  111.1 2.1 %collective-permute-done.14 = f32[2,4,64,256]{3,2,1,0:T(8,128)S(1)} collective-permute-done((f32[2,4,64,256]{3,2,1,0:T(8,128)S(1)}, f32[2,4,64,256]{3,2,1,0:T(8,128)S(1)}, u32[]{:S(2)}, u32[]{:S(2)}) %collective-permute-start.14) | collective-permute-done | bytes 524320 | tf_op jit(solution)/shard_map/ppermute | solution.py:54
  113.2 11.9 %collective-permute-start.15 = (f32[4,64,256]{2,1,0:T(8,128)S(1)}, f32[4,64,256]{2,1,0:T(8,128)S(1)}, u32[]{:S(2)}, u32[]{:S(2)}) collective-permute-start(f32[4,64,256]{2,1,0:T(8,128)S(1)} %fusion.3), channel_id=1, source_target_pairs={{0,16},{1,17},{2,18},{3,19},{4,20},{5,21},{6,22},{7,23},{8,24},{9,... | collective-permute-start | bytes 786440 | tf_op jit(solution)/shard_map/ppermute | solution.py:54
  125.5 5.4 %collective-permute-done.15 = f32[4,64,256]{2,1,0:T(8,128)S(1)} collective-permute-done((f32[4,64,256]{2,1,0:T(8,128)S(1)}, f32[4,64,256]{2,1,0:T(8,128)S(1)}, u32[]{:S(2)}, u32[]{:S(2)}) %collective-permute-start.15) | collective-permute-done | bytes 262176 | tf_op jit(solution)/shard_map/ppermute | solution.py:54
  131.0 1.5 %collective-permute-done.17 = f32[4,64,256]{2,1,0:T(8,128)S(1)} collective-permute-done((f32[4,64,256]{2,1,0:T(8,128)S(1)}, f32[4,64,256]{2,1,0:T(8,128)S(1)}, u32[]{:S(2)}, u32[]{:S(2)}) %collective-permute-start.17) | collective-permute-done | bytes 262176 | tf_op jit(solution)/shard_map/ppermute | solution.py:54
  133.4 3.2 %collective-permute-start.20 = (f32[128,256]{1,0:T(8,128)S(1)}, f32[128,256]{1,0:T(8,128)S(1)}, u32[]{:S(2)}, u32[]{:S(2)}) collective-permute-start(f32[128,256]{1,0:T(8,128)S(1)} %pad_maximum_fusion.4), channel_id=1, source_target_pairs={{0,3},{1,0},{2,1},{3,2},{4,7},{5,4},{6,5},{7,6},{8,11},{9,8},{10,9... | collective-permute-start | bytes 393224 | tf_op jit(solution)/shard_map/ppermute | solution.py:54
  136.6 4.2 %collective-permute-done.18 = f32[128,256]{1,0:T(8,128)S(1)} collective-permute-done((f32[128,256]{1,0:T(8,128)S(1)}, f32[128,256]{1,0:T(8,128)S(1)}, u32[]{:S(2)}, u32[]{:S(2)}) %collective-permute-start.18) | collective-permute-done | bytes 131104 | tf_op jit(solution)/shard_map/ppermute | solution.py:54
  140.8 2.8 %collective-permute-done.19 = f32[128,256]{1,0:T(8,128)S(1)} collective-permute-done((f32[128,256]{1,0:T(8,128)S(1)}, f32[128,256]{1,0:T(8,128)S(1)}, u32[]{:S(2)}, u32[]{:S(2)}) %collective-permute-start.19) | collective-permute-done | bytes 131104 | tf_op jit(solution)/shard_map/ppermute | solution.py:54
  143.7 1.7 %bitcast_subtract_fusion = (f32[128,256]{1,0:T(8,128)}, f32[128,256]{1,0:T(8,128)}, f32[128,256]{1,0:T(8,128)}) fusion(f32[3,128,256]{2,1,0:T(8,128)} %param.11, f32[128,256]{1,0:T(8,128)S(1)} %copy-done.8, f32[128,256]{1,0:T(8,128)S(1)} %copy-done.9, f32[128,256]{1,0:T(8,128)S(1)} %collective-permute-done.20, f32[128,256]{1,0:T(8,128)S(1)} %collective-permute-done.19, ...), kind=kLoop, calls=%fused_computation.28 | loop fusion | flops 524288 | bytes 1310720 | tf_op jit(solution)/shard_map/sub | solution.py:316
  (65 shorter events, 7.6 us)
Async XLA Ops:
  0.6 56.5 %collective-permute-start.1 = (bf16[36,64,4096]{2,1,0:T(8,128)(2,1)}, bf16[36,64,4096]{2,1,0:T(8,128)(2,1)}, u32[]{:S(2)}, u32[]{:S(2)}) collective-permute-start(bf16[36,64,4096]{2,1,0:T(8,128)(2,1)} %refs_4_.1), channel_id=1, source_target_pairs={{0,4},{1,5},{2,6},{3,7},{4,0},{5,1},{6,2},{7,3},{8,12},{9,13},{10,... | collective-permute-start | bytes 56623112 | tf_op jit(solution)/shard_map/ppermute | solution.py:54
  2.2 22.1 %collective-permute-start.4 = (bf16[6,64,256]{2,1,0:T(8,128)(2,1)S(1)}, bf16[6,64,256]{2,1,0:T(8,128)(2,1)S(1)}, u32[]{:S(2)}, u32[]{:S(2)}) collective-permute-start(bf16[6,64,256]{2,1,0:T(8,128)(2,1)S(1)} %bitcast.49), channel_id=1, source_target_pairs={{0,3},{1,0},{2,1},{3,2},{4,7},{5,4},{6,5},{7,6},{8,11},{9,8},{10,9... | collective-permute-start | bytes 589832 | tf_op jit(solution)/shard_map/ppermute | solution.py:54
  6.8 17.3 %collective-permute-start.3 = (bf16[6,64,256]{2,1,0:T(8,128)(2,1)S(1)}, bf16[6,64,256]{2,1,0:T(8,128)(2,1)S(1)}, u32[]{:S(2)}, u32[]{:S(2)}) collective-permute-start(bf16[6,64,256]{2,1,0:T(8,128)(2,1)S(1)} %bitcast.50), channel_id=1, source_target_pairs={{0,2},{1,3},{2,0},{3,1},{4,6},{5,7},{6,4},{7,5},{8,10},{9,11},{10,... | collective-permute-start | bytes 589832 | tf_op jit(solution)/shard_map/ppermute | solution.py:54
  6.8 14.2 %collective-permute-start.2 = (bf16[6,64,256]{2,1,0:T(8,128)(2,1)S(1)}, bf16[6,64,256]{2,1,0:T(8,128)(2,1)S(1)}, u32[]{:S(2)}, u32[]{:S(2)}) collective-permute-start(bf16[6,64,256]{2,1,0:T(8,128)(2,1)S(1)} %bitcast.51), channel_id=1, source_target_pairs={{0,1},{1,2},{2,3},{3,0},{4,5},{5,6},{6,7},{7,4},{8,9},{9,10},{10,1... | collective-permute-start | bytes 589832 | tf_op jit(solution)/shard_map/ppermute | solution.py:54
  24.3 10.8 %collective-permute-start.9 = (bf16[12,64,256]{2,1,0:T(8,128)(2,1)S(1)}, bf16[12,64,256]{2,1,0:T(8,128)(2,1)S(1)}, u32[]{:S(2)}, u32[]{:S(2)}) collective-permute-start(bf16[12,64,256]{2,1,0:T(8,128)(2,1)S(1)} %pad_maximum_fusion.1), channel_id=1, source_target_pairs={{0,8},{1,9},{2,10},{3,11},{4,12},{5,13},{6,14},{7,15},{8,0},{9,1},... | collective-permute-start | bytes 1179656 | tf_op jit(solution)/shard_map/ppermute | solution.py:54
  25.9 10.8 %collective-permute-start.5 = (bf16[12,64,256]{2,1,0:T(8,128)(2,1)S(1)}, bf16[12,64,256]{2,1,0:T(8,128)(2,1)S(1)}, u32[]{:S(2)}, u32[]{:S(2)}) collective-permute-start(bf16[12,64,256]{2,1,0:T(8,128)(2,1)S(1)} %pad_maximum_fusion), channel_id=1, source_target_pairs={{0,16},{1,17},{2,18},{3,19},{4,20},{5,21},{6,22},{7,23},{8,24},{9,... | collective-permute-start | bytes 1179656 | tf_op jit(solution)/shard_map/ppermute | solution.py:54
  35.2 22.0 %copy-start.1 = (bf16[24,64,256]{2,1,0:T(8,128)(2,1)}, bf16[24,64,256]{2,1,0:T(8,128)(2,1)S(1)}, u32[]{:S(2)}) copy-start(bf16[24,64,256]{2,1,0:T(8,128)(2,1)S(1)} %constant_dynamic-update-slice_fusion.5.refs_10_) | copy-start | bytes 2359300
  35.2 18.3 %collective-permute-start.10 = (bf16[24,64,256]{2,1,0:T(8,128)(2,1)S(1)}, bf16[24,64,256]{2,1,0:T(8,128)(2,1)S(1)}, u32[]{:S(2)}, u32[]{:S(2)}) collective-permute-start(bf16[24,64,256]{2,1,0:T(8,128)(2,1)S(1)} %constant_dynamic-update-slice_fusion.5.refs_10_), channel_id=1, source_target_pairs={{0,16},{1,17},{2,18},{3,19},{4,20},{5,21},{6,22},{7,23},{8,24},{9,... | collective-permute-start | bytes 2359304 | tf_op jit(solution)/shard_map/ppermute | solution.py:54
  36.8 20.4 %copy-start = (bf16[24,64,256]{2,1,0:T(8,128)(2,1)}, bf16[24,64,256]{2,1,0:T(8,128)(2,1)S(1)}, u32[]{:S(2)}) copy-start(bf16[24,64,256]{2,1,0:T(8,128)(2,1)S(1)} %constant_dynamic-update-slice_fusion.refs_6_) | copy-start | bytes 2359300
  36.8 18.1 %collective-permute-start.6 = (bf16[24,64,256]{2,1,0:T(8,128)(2,1)S(1)}, bf16[24,64,256]{2,1,0:T(8,128)(2,1)S(1)}, u32[]{:S(2)}, u32[]{:S(2)}) collective-permute-start(bf16[24,64,256]{2,1,0:T(8,128)(2,1)S(1)} %constant_dynamic-update-slice_fusion.refs_6_), channel_id=1, source_target_pairs={{0,8},{1,9},{2,10},{3,11},{4,12},{5,13},{6,14},{7,15},{8,0},{9,1},... | collective-permute-start | bytes 2359304 | tf_op jit(solution)/shard_map/ppermute | solution.py:54
  39.2 1.1 collective-permute-start
  39.2 15.7 %collective-permute-start.11 = (bf16[24,64,256]{2,1,0:T(8,128)(2,1)S(1)}, bf16[24,64,256]{2,1,0:T(8,128)(2,1)S(1)}, u32[]{:S(2)}, u32[]{:S(2)}) collective-permute-start(bf16[24,64,256]{2,1,0:T(8,128)(2,1)S(1)} %constant_dynamic-update-slice_fusion.5.refs_10_), channel_id=1, source_target_pairs={{0,4},{1,5},{2,6},{3,7},{4,0},{5,1},{6,2},{7,3},{8,12},{9,13},{10,... | collective-permute-start | bytes 2359304 | tf_op jit(solution)/shard_map/ppermute | solution.py:54
  40.3 14.6 %collective-permute-start.7 = (bf16[24,64,256]{2,1,0:T(8,128)(2,1)S(1)}, bf16[24,64,256]{2,1,0:T(8,128)(2,1)S(1)}, u32[]{:S(2)}, u32[]{:S(2)}) collective-permute-start(bf16[24,64,256]{2,1,0:T(8,128)(2,1)S(1)} %constant_dynamic-update-slice_fusion.refs_6_), channel_id=1, source_target_pairs={{0,4},{1,5},{2,6},{3,7},{4,0},{5,1},{6,2},{7,3},{8,12},{9,13},{10,... | collective-permute-start | bytes 2359304 | tf_op jit(solution)/shard_map/ppermute | solution.py:54
  53.5 2.3 %collective-permute-start.12 = (bf16[24,64,256]{2,1,0:T(8,128)(2,1)S(1)}, bf16[24,64,256]{2,1,0:T(8,128)(2,1)S(1)}, u32[]{:S(2)}, u32[]{:S(2)}) collective-permute-start(bf16[24,64,256]{2,1,0:T(8,128)(2,1)S(1)} %collective-permute-done.10.refs_11_), channel_id=1, source_target_pairs={{0,4},{1,5},{2,6},{3,7},{4,0},{5,1},{6,2},{7,3},{8,12},{9,13},{10,... | collective-permute-start | bytes 2359304 | tf_op jit(solution)/shard_map/ppermute | solution.py:54
  54.9 2.3 %collective-permute-start.8 = (bf16[24,64,256]{2,1,0:T(8,128)(2,1)S(1)}, bf16[24,64,256]{2,1,0:T(8,128)(2,1)S(1)}, u32[]{:S(2)}, u32[]{:S(2)}) collective-permute-start(bf16[24,64,256]{2,1,0:T(8,128)(2,1)S(1)} %collective-permute-done.6.refs_7_), channel_id=1, source_target_pairs={{0,4},{1,5},{2,6},{3,7},{4,0},{5,1},{6,2},{7,3},{8,12},{9,13},{10,... | collective-permute-start | bytes 2359304 | tf_op jit(solution)/shard_map/ppermute | solution.py:54
  89.7 4.4 %collective-permute-start.13 = (f32[32,64,256]{2,1,0:T(8,128)}, f32[32,64,256]{2,1,0:T(8,128)S(1)}, u32[]{:S(2)}, u32[]{:S(2)}) collective-permute-start(f32[32,64,256]{2,1,0:T(8,128)} %get-tuple-element.6), channel_id=1, source_target_pairs={{0,4},{1,5},{2,6},{3,7},{4,0},{5,1},{6,2},{7,3},{8,12},{9,13},{10,... | collective-permute-start | bytes 6291464 | tf_op jit(solution)/shard_map/ppermute | solution.py:54
  96.0 17.2 %collective-permute-start.14 = (f32[2,4,64,256]{3,2,1,0:T(8,128)S(1)}, f32[2,4,64,256]{3,2,1,0:T(8,128)S(1)}, u32[]{:S(2)}, u32[]{:S(2)}) collective-permute-start(f32[2,4,64,256]{3,2,1,0:T(8,128)S(1)} %bitcast.54), channel_id=1, source_target_pairs={{0,8},{1,9},{2,10},{3,11},{4,12},{5,13},{6,14},{7,15},{8,0},{9,1},... | collective-permute-start | bytes 1572872 | tf_op jit(solution)/shard_map/ppermute | solution.py:54
  100.7 24.4 %collective-permute-start.16 = (f32[2,4,64,256]{3,2,1,0:T(8,128)S(1)}, f32[2,4,64,256]{3,2,1,0:T(8,128)S(1)}, u32[]{:S(2)}, u32[]{:S(2)}) collective-permute-start(f32[2,4,64,256]{3,2,1,0:T(8,128)S(1)} %bitcast.53), channel_id=1, source_target_pairs={{0,16},{1,17},{2,18},{3,19},{4,20},{5,21},{6,22},{7,23},{8,24},{9,... | collective-permute-start | bytes 1572872 | tf_op jit(solution)/shard_map/ppermute | solution.py:54
  113.2 17.6 %collective-permute-start.15 = (f32[4,64,256]{2,1,0:T(8,128)S(1)}, f32[4,64,256]{2,1,0:T(8,128)S(1)}, u32[]{:S(2)}, u32[]{:S(2)}) collective-permute-start(f32[4,64,256]{2,1,0:T(8,128)S(1)} %fusion.3), channel_id=1, source_target_pairs={{0,16},{1,17},{2,18},{3,19},{4,20},{5,21},{6,22},{7,23},{8,24},{9,... | collective-permute-start | bytes 786440 | tf_op jit(solution)/shard_map/ppermute | solution.py:54
  125.1 18.6 %copy-start.8 = (f32[128,256]{1,0:T(8,128)S(1)}, f32[128,256]{1,0:T(8,128)}, u32[]{:S(2)}) copy-start(f32[128,256]{1,0:T(8,128)} %param.12) | copy-start | bytes 393220
  125.2 7.3 %collective-permute-start.17 = (f32[4,64,256]{2,1,0:T(8,128)S(1)}, f32[4,64,256]{2,1,0:T(8,128)S(1)}, u32[]{:S(2)}, u32[]{:S(2)}) collective-permute-start(f32[4,64,256]{2,1,0:T(8,128)S(1)} %fusion), channel_id=1, source_target_pairs={{0,8},{1,9},{2,10},{3,11},{4,12},{5,13},{6,14},{7,15},{8,0},{9,1},... | collective-permute-start | bytes 786440 | tf_op jit(solution)/shard_map/ppermute | solution.py:54
  132.6 8.3 %collective-permute-start.18 = (f32[128,256]{1,0:T(8,128)S(1)}, f32[128,256]{1,0:T(8,128)S(1)}, u32[]{:S(2)}, u32[]{:S(2)}) collective-permute-start(f32[128,256]{1,0:T(8,128)S(1)} %pad_maximum_fusion.2), channel_id=1, source_target_pairs={{0,1},{1,2},{2,3},{3,0},{4,5},{5,6},{6,7},{7,4},{8,9},{9,10},{10,1... | collective-permute-start | bytes 393224 | tf_op jit(solution)/shard_map/ppermute | solution.py:54
  133.3 10.4 %collective-permute-start.19 = (f32[128,256]{1,0:T(8,128)S(1)}, f32[128,256]{1,0:T(8,128)S(1)}, u32[]{:S(2)}, u32[]{:S(2)}) collective-permute-start(f32[128,256]{1,0:T(8,128)S(1)} %pad_maximum_fusion.3), channel_id=1, source_target_pairs={{0,2},{1,3},{2,0},{3,1},{4,6},{5,7},{6,4},{7,5},{8,10},{9,11},{10,... | collective-permute-start | bytes 393224 | tf_op jit(solution)/shard_map/ppermute | solution.py:54
  133.4 10.3 %collective-permute-start.20 = (f32[128,256]{1,0:T(8,128)S(1)}, f32[128,256]{1,0:T(8,128)S(1)}, u32[]{:S(2)}, u32[]{:S(2)}) collective-permute-start(f32[128,256]{1,0:T(8,128)S(1)} %pad_maximum_fusion.4), channel_id=1, source_target_pairs={{0,3},{1,0},{2,1},{3,2},{4,7},{5,4},{6,5},{7,6},{8,11},{9,8},{10,9... | collective-permute-start | bytes 393224 | tf_op jit(solution)/shard_map/ppermute | solution.py:54
  (9 other events, 63.2 us)
